TPU v7x, 256 devices: a whole 4x4x8 slice. The times are simulated.
256 devices in a mesh: island: 8 (over z_hi, core), fsdp: 32 (over z_lo, y, x).
Axes of the slice: x: 4, y: 4, z: 8 (z_hi: 4, z_lo: 2; z = z_hi * 2 + z_lo), core: 2. Of those that a mesh axis runs over, the one named last changes fastest.
Arguments:
- base_in: float32 [2, 2048, 2048], P(None, 'fsdp')
- base_out: float32 [2, 1024, 2048], P(None, 'fsdp')
- local_in: bfloat16 [8, 2, 2048, 2048], P('island', None, 'fsdp')
- local_out: bfloat16 [8, 2, 1024, 2048], P('island', None, 'fsdp')
- mom_in: float32 [2, 2048, 2048], P(None, 'fsdp'), may hold values from -0.12 to 0.12
- mom_out: float32 [2, 1024, 2048], P(None, 'fsdp'), may hold values from -0.12 to 0.12
- exp_in: int32 [2, 2048], P(None, 'fsdp'), may hold values from -12 to -8
- exp_out: int32 [2, 1024], P(None, 'fsdp'), may hold values from -12 to -8
- tokens: bfloat16 [131072, 2048], P(('island', 'fsdp')), may hold values from -6 to 6
- routes: int32 [131072, 1], P(('island', 'fsdp')), may hold values from 0 to 1; in each aligned block of 512 rows (0 to 511, 512 to 1023, ...) at most 320 rows name the same one
- gains: float32 [131072], P(('island', 'fsdp')), may hold values from 0.25 to 1
Outputs:
- new_base_in: float32 [2, 2048, 2048], P(None, 'fsdp', 'island')
- new_base_out: float32 [2, 1024, 2048], P(None, 'fsdp', 'island')
- new_mom_in: float32 [2, 2048, 2048], P(None, 'fsdp', 'island')
- new_mom_out: float32 [2, 1024, 2048], P(None, 'fsdp', 'island')
- mixed: bfloat16 [131072, 2048], P(('island', 'fsdp'))
Inputs may be any that keep to these rules, and one draw needn't show every extreme that they name: `routes`: in the rows of one device at most 320 tokens go to one expert.
All inputs are finite; a program needn't handle non-finite values.
Results may differ from a plain program's by a relative error of at most 0.03.
Values may be sent and summed in bfloat16 or wider, within the bound.
No kernel may reach another device: no remote copies, remote signals or barrier semaphores. Data moves between devices by JAX's collectives and lax.ppermute only.
A program may use at most 128 MiB of HBM per device.

v0:
```python
import jax
import jax.numpy as jnp
from jax import lax
from jax.sharding import PartitionSpec as P

FF = 1024
CAP = 320


def quantize(base, local, expo):
    scale_down = jnp.exp2(-expo.astype(jnp.float32))[:, :, None]
    return jnp.clip((base - local[0].astype(jnp.float32)) * scale_down, -127.0, 127.0).astype(
        jnp.bfloat16
    )


def nesterov(base, moment, total, expo, groups):
    grad = total * jnp.exp2(expo.astype(jnp.float32))[:, :, None] / groups
    new_mom = 0.9 * moment + grad
    new_base = base - 0.7 * (grad + 0.9 * new_mom)
    return (new_base, new_mom)


def own_columns(whole, position, groups):
    width = whole.shape[2] // groups
    return lax.dynamic_slice_in_dim(whole, position * width, width, 2)


def body(
    base_in, base_out, local_in, local_out, mom_in, mom_out, exp_in, exp_out, tokens, routes, gains
):
    groups = lax.axis_size("island")
    position = lax.axis_index("island")
    quant_in = quantize(base_in, local_in, exp_in)
    quant_out = quantize(base_out, local_out, exp_out)
    total_in, total_out = (
        lax.psum(quant_in, "island").astype(jnp.float32),
        lax.psum(quant_out, "island").astype(jnp.float32),
    )
    full_in, full_mom_in = nesterov(base_in, mom_in, total_in, exp_in, groups)
    full_out, full_mom_out = nesterov(base_out, mom_out, total_out, exp_out, groups)
    weights_in = full_in.astype(jnp.bfloat16)
    weights_out = full_out.astype(jnp.bfloat16)
    new_base_in = own_columns(full_in, position, groups)
    new_mom_in = own_columns(full_mom_in, position, groups)
    new_base_out = own_columns(full_out, position, groups)
    new_mom_out = own_columns(full_mom_out, position, groups)
    tok_rows = tokens.shape[0]
    width = tokens.shape[1]
    experts = weights_in.shape[0]
    route = routes[:, 0]
    positions = jnp.arange(tok_rows, dtype=jnp.int32)
    slot_list = []
    valid_list = []
    for expert in range(experts):
        chosen = route == expert
        keys = jnp.where(chosen, positions, positions + tok_rows)
        slot_list.append(jnp.argsort(keys)[:CAP])
        count = jnp.sum(chosen.astype(jnp.int32))
        valid_list.append((jnp.arange(CAP, dtype=jnp.int32) < count).astype(jnp.float32))
    slot_rows = jnp.stack(slot_list)
    valid = jnp.stack(valid_list)
    picked = tokens[slot_rows]
    columns = picked
    proj = jnp.einsum(
        "ecr,erf->ecf",
        columns,
        lax.all_gather(weights_in, "fsdp", axis=1, tiled=True),
        preferred_element_type=jnp.float32,
    )
    hidden = (jax.nn.silu(proj[:, :, :FF]) * proj[:, :, FF:]).astype(jnp.bfloat16)
    columns = hidden
    outcome = jnp.einsum(
        "ecr,erd->ecd",
        columns,
        lax.all_gather(weights_out, "fsdp", axis=1, tiled=True),
        preferred_element_type=jnp.float32,
    )
    outcome = outcome * (gains[slot_rows] * valid)[:, :, None]
    mixed = (
        jnp.zeros((tok_rows, width), jnp.float32)
        .at[slot_rows.reshape(-1)]
        .add(outcome.reshape(-1, width))
    )
    return (new_base_in, new_base_out, new_mom_in, new_mom_out, mixed.astype(jnp.bfloat16))


def solution(mesh):
    in_specs = (
        P(None, "fsdp", None),
        P(None, "fsdp", None),
        P("island", None, "fsdp", None),
        P("island", None, "fsdp", None),
        P(None, "fsdp", None),
        P(None, "fsdp", None),
        P(None, "fsdp"),
        P(None, "fsdp"),
        P(("island", "fsdp"), None),
        P(("island", "fsdp"), None),
        P(("island", "fsdp")),
    )
    out_specs = (
        P(None, "fsdp", "island"),
        P(None, "fsdp", "island"),
        P(None, "fsdp", "island"),
        P(None, "fsdp", "island"),
        P(("island", "fsdp"), None),
    )
    return jax.shard_map(body, mesh=mesh, in_specs=in_specs, out_specs=out_specs, check_vma=False)
```

profile of v0, /device:TPU:32, one launch (start us, length us, event | category | flops | bytes accessed | tf_op | source)
XLA Modules:
  0.0 496.5 jit_solution(5699725866218064942)
XLA Ops:
  7.2 0.0 copy-start
  7.2 0.0 copy-start.2
  7.2 0.0 all-reduce.3.cloned.1.call-start
  7.2 0.9 multiply_exponential_fusion.3
  8.1 0.7 multiply_exponential_fusion
  8.8 2.3 fusion.7
  11.2 1.9 fusion.10
  13.1 0.0 all-reduce.3.cloned.1.call-update
  13.1 0.0 all-gather.3.cloned.1.call-start
  13.1 77.1 %all-reduce.3.cloned.1.call-done = (bf16[2,64,2048]{2,1,0:T(8,128)(2,1)}, bf16[2,32,2048]{2,1,0:T(8,128)(2,1)}) async-done(((bf16[2,64,2048]{2,1,0:T(8,128)(2,1)}, bf16[2,32,2048]{2,1,0:T(8,128)(2,1)}), (bf16[2,64,2048]{2,1,0:T(8,128)(2,1)}, bf16[2,32,2048]{2,1,0:T(8,128)(2,1)})) %all-reduce.3.cloned.1.call-update) | async-done | bytes 786448 | tf_op jit(solution)/shard_map/psum | solution.py:37
  90.2 0.0 copy-start.3
  90.2 0.0 copy-done.2
  90.2 0.0 copy-start.4
  90.2 0.0 copy-start.1
  90.2 3.3 fusion.15
  93.5 0.0 all-gather.3.cloned.1.call-update
  93.5 0.0 all-gather.5.cloned.1.call-start
  93.6 0.0 copy-done.3
  93.6 2.1 fusion.16
  95.7 0.0 all-gather.5.cloned.1.call-update
  95.8 0.0 copy-done.4
  95.8 0.6 convert_reduce_fusion
  96.4 3.8 sort.31
  100.2 3.8 sort.32
  104.0 0.1 reshape.182
  104.1 0.0 copy-done.1
  104.1 4.3 gather_fusion.1
  108.4 0.1 reshape.189
  108.5 0.0 copy-done
  108.5 4.1 gather_fusion
  112.6 0.1 reshape.176
  112.7 0.7 iota_compare_fusion
  113.3 0.7 iota_compare_fusion.1
  114.0 0.7 constant_dynamic-slice_fusion
  114.7 1.7 constant_dynamic-slice_fusion.1
  116.4 170.5 %all-gather.3.cloned.1.call-done = bf16[2,2048,2048]{2,1,0:T(8,128)(2,1)} async-done(((bf16[2,64,2048]{2,1,0:T(8,128)(2,1)}), bf16[2,2048,2048]{2,1,0:T(8,128)(2,1)}) %all-gather.3.cloned.1.call-update) | async-done | bytes 16777232 | tf_op jit(solution)/shard_map/all_gather | solution.py:68
  286.9 13.5 %fusion.17 = f32[2,320,2048]{2,1,0:T(8,128)} fusion(bf16[2,320,2048]{2,1,0:T(8,128)(2,1)} %bitcast.13, bf16[2,2048,2048]{2,1,0:T(8,128)(2,1)} %all-gather.3.cloned.1.call-done), kind=kOutput, calls=%fused_computation.52 | convolution fusion | flops 5368709120 | bytes 24641536 | tf_op jit(solution)/shard_map/ecr,erf->ecf/dot_general | solution.py:65
  300.4 158.3 %all-gather.5.cloned.1.call-done = bf16[2,1024,2048]{2,1,0:T(8,128)(2,1)} async-done(((bf16[2,32,2048]{2,1,0:T(8,128)(2,1)}), bf16[2,1024,2048]{2,1,0:T(8,128)(2,1)}) %all-gather.5.cloned.1.call-update) | async-done | bytes 8388624 | tf_op jit(solution)/shard_map/all_gather | solution.py:76
  458.8 10.2 %convolution_multiply_fusion = f32[2,320,2048]{2,1,0:T(8,128)} fusion(bf16[2,1024,2048]{2,1,0:T(8,128)(2,1)} %all-gather.5.cloned.1.call-done, f32[2,320]{1,0:T(2,128)S(1)} %add_select_fusion, f32[2,320,2048]{2,1,0:T(8,128)} %fusion.17), kind=kOutput, calls=%fused_computation.3 | convolution fusion | flops 2689597440 | bytes 18876928 | tf_op jit(solution)/shard_map/ecr,erd->ecd/dot_general | solution.py:73
  469.0 17.1 %scatter_custom_fusion = f32[512,2048]{1,0:T(8,128)} fusion(s32[640]{0:T(1024)S(1)} %fusion.12, f32[640,2048]{1,0:T(8,128)} %bitcast.18, f32[]{:T(128)} %constant.8.clone.1), kind=kCustom, calls=%fused_computation.6 | custom fusion | flops 1310720 | bytes 4194816 | tf_op jit(solution)/shard_map/scatter-add | solution.py:83
  486.1 3.8 convert_element_type.85
  (12 shorter events, 0.1 us)
Async XLA Ops:
  7.2 101.4 %copy-start = (bf16[512,2048]{1,0:T(8,128)(2,1)S(1)}, bf16[512,2048]{1,0:T(8,128)(2,1)}, u32[]{:S(2)}) copy-start(bf16[512,2048]{1,0:T(8,128)(2,1)} %param.19) | copy-start | bytes 6291460
  7.2 83.0 %copy-start.2 = (f32[2,64,2048]{2,1,0:T(8,128)S(1)}, f32[2,64,2048]{2,1,0:T(8,128)}, u32[]{:S(2)}) copy-start(f32[2,64,2048]{2,1,0:T(8,128)} %param.11) | copy-start | bytes 3145732
  7.2 83.0 %all-reduce.3.cloned.1.call-start = ((), (), s32[]{:S(2)}) async-start(), calls=%async_computation.2 | async-start | bytes 1572864 | tf_op jit(solution)/shard_map/psum | solution.py:37
  13.1 273.8 %all-gather.3.cloned.1.call-start = ((), (), s32[]{:S(2)}) async-start(), calls=%async_computation | async-start | bytes 17301504 | tf_op jit(solution)/shard_map/all_gather | solution.py:68
  90.2 3.4 copy-start.3
  90.2 5.6 %copy-start.4 = (s32[512,1]{0,1:T(1,128)S(1)}, s32[512,1]{0,1:T(1,128)}, u32[]{:S(2)}) copy-start(s32[512,1]{0,1:T(1,128)} %param.20) | copy-start | bytes 6148
  90.2 13.9 %copy-start.1 = (f32[512]{0:T(512)S(1)}, f32[512]{0:T(512)}, u32[]{:S(2)}) copy-start(f32[512]{0:T(512)} %param.21) | copy-start | bytes 6148
  93.5 365.3 %all-gather.5.cloned.1.call-start = ((), (), s32[]{:S(2)}) async-start(), calls=%async_computation.1 | async-start | bytes 8650752 | tf_op jit(solution)/shard_map/all_gather | solution.py:76
Sparse Core Ops, SparseCore 0:
  13.2 76.9 all-reduce.2
  93.7 193.2 all-gather.2
  288.9 169.8 all-gather.4
where the time goes:
time: 498 us; the launch traced here: 496 us
  waiting for transfers between devices  406 us (82%)
  other arithmetic  41.8 us (8%)
  matrix products  23.8 us (5%)
  between operations  13.8 us (3%)
  local copies, waits for them, and re-layouts  11 us (2%)
    all_gather x1, waiting for transfers between devices, body(): lax.all_gather(weights_in, 'fsdp', axis=1, tiled=True)  171 us
    all_gather x1, waiting for transfers between devices, body(): lax.all_gather(weights_out, 'fsdp', axis=1, tiled=True)  158 us
    psum x1, waiting for transfers between devices, body(): lax.psum(quant_in, 'island').astype(jnp.float32)  77.1 us
    scatter-add x1, other arithmetic, body(): mixed = jnp.zeros((tok_rows, width), jnp.float32).at[slot_rows.reshape(-1...  17.1 us
    dot_general x1, matrix products, body(): jnp.einsum('ecr,erf->ecf', columns, lax.all_gather(weights_in, 'fsdp', ax...  13.5 us
    dot_general x1, matrix products, body(): jnp.einsum('ecr,erd->ecd', columns, lax.all_gather(weights_out, 'fsdp', a...  10.2 us
  transfers between devices with their start and end apart: 3, of which 3 were waited for; matrix products, arithmetic and copies ran while one was open for 7% of the time, Pallas kernels for 0%

commit v1 on v0

v1 whole, which is shorter than its diff:
```python
import jax
import jax.numpy as jnp
import numpy as np
from jax import lax
from jax.experimental import pallas as pl
from jax.experimental.pallas import tpu as pltpu
from jax.sharding import Mesh
from jax.sharding import PartitionSpec as P

D = 2048
FF = 1024
CAP = 320
ZH, CORE, ZL, Y, X = 4, 2, 2, 4, 4
AXES = ("zh", "core", "zl", "y", "x")
ISLAND = ("zh", "core")
FSDP = ("zl", "y", "x")
COLUMN = ("zh", "core", "zl")
GROUPS = ZH * CORE
COLS = 256
ROWS_IN, ROWS_OUT = 64, 32
ROWS = ROWS_IN + ROWS_OUT
PIECES = Y * X
HALF = PIECES // 2
SETS = 2
BF16, F32 = jnp.bfloat16, jnp.float32

MASKS = ((1, 3), (3, 1))
REACH = tuple((0, a, b, a ^ b) for a, b in MASKS)


def piece_table():
    table = np.zeros((CORE, Y, X, 2, PIECES), np.int32)
    for core in range(CORE):
        for y in range(Y):
            for x in range(X):
                for p in range(PIECES):
                    first, second = REACH[core][p % 4], REACH[core][p // 4]
                    table[core, y, x, 0, p] = (y ^ second) * X + (x ^ first)
                    table[core, y, x, 1, p] = (y ^ first) * X + (x ^ second)
    return table


def shift(size, step):
    return [(i, (i + step) % size) for i in range(size)]


def flip_pairs(turn):
    return [
        (core * 4 + i, core * 4 + (i ^ MASKS[core][turn])) for core in range(CORE) for i in range(4)
    ]


def column_pairs(sign, swap):
    pairs = []
    for zh in range(ZH):
        for core in range(CORE):
            for zl in range(ZL):
                z = (zh * ZL + zl + sign * (1 - 2 * core)) % (ZH * ZL)
                sender = core ^ swap
                pairs.append(
                    ((zh * CORE + sender) * ZL + zl, ((z // ZL) * CORE + core) * ZL + z % ZL)
                )
    return pairs


def dot(a, b):
    return jnp.dot(a, b, preferred_element_type=F32)


def params(mib=48):
    return pltpu.CompilerParams(vmem_limit_bytes=mib * 2**20)


def row_exponents(expo, rows):
    eye = lax.broadcasted_iota(jnp.int32, (rows, rows), 0) == lax.broadcasted_iota(
        jnp.int32, (rows, rows), 1
    )
    lines = [jnp.where(eye, expo[e : e + 1, :].astype(F32), 0.0) for e in range(2)]
    return jnp.stack([jnp.sum(line, axis=1, keepdims=True) for line in lines])


def give_kernel(
    place, b_in, l_in, e_in, b_out, l_out, e_out, m_in, m_out,
    given, kept, ob_in, ob_out, om_in, om_out, sems,
):
    zh, core = place[0], place[1]
    mine = pl.ds(pl.multiple_of((zh * CORE + core) * COLS, COLS), COLS)
    copies = [
        pltpu.make_async_copy(whole.at[:, :, mine], out, sems.at[i])
        for i, (whole, out) in enumerate(((m_in, om_in), (m_out, om_out)))
    ]
    for copy in copies:
        copy.start()
    ob_in[...] = b_in[:, :, mine]
    ob_out[...] = b_out[:, :, mine]
    for base, local, expo, rows, first in (
        (b_in, l_in, e_in, ROWS_IN, 0),
        (b_out, l_out, e_out, ROWS_OUT, ROWS_IN),
    ):
        scale = jnp.exp2(-row_exponents(expo, rows))
        for step in range(ZH):
            for out, side in ((given, 1 - core), (kept, core)):
                column = (((zh + step) % ZH) * CORE + side) * COLS
                at = pl.ds(pl.multiple_of(column, COLS), COLS)
                quant = (base[:, :, at] - local[0, :, :, at].astype(F32)) * scale
                out[step, :, first : first + rows] = jnp.clip(quant, -127.0, 127.0).astype(BF16)
    for copy in copies:
        copy.wait()


def give_call(place, arrays, moments):
    vmem, anywhere = pl.BlockSpec(memory_space=pltpu.VMEM), pl.BlockSpec(memory_space=pl.ANY)
    own = [jax.ShapeDtypeStruct((2, r, COLS), F32) for r in (ROWS_IN, ROWS_OUT) * 2]
    return pl.pallas_call(
        give_kernel,
        in_specs=[pl.BlockSpec(memory_space=pltpu.SMEM)] + [vmem] * 6 + [anywhere] * 2,
        out_specs=[vmem] * 6,
        out_shape=[jax.ShapeDtypeStruct((ZH, 2, ROWS, COLS), BF16)] * 2 + own,
        scratch_shapes=[pltpu.SemaphoreType.DMA((2,))],
        compiler_params=params(60),
        cost_estimate=pl.CostEstimate(flops=10**6, bytes_accessed=4 * 2**20, transcendentals=0),
        name="give",
    )(place, *arrays, *moments)


def pair_kernel(kept, taken, own, *sent):
    for step, out in enumerate((own,) + sent):
        out[...] = (kept[step].astype(F32) + taken[step].astype(F32)).astype(out.dtype)


def pair_call(kept, taken):
    vmem = pl.BlockSpec(memory_space=pltpu.VMEM)
    return pl.pallas_call(
        pair_kernel,
        in_specs=[vmem] * 2,
        out_specs=[vmem] * ZH,
        out_shape=[jax.ShapeDtypeStruct((2, ROWS, COLS), F32)]
        + [jax.ShapeDtypeStruct((2, ROWS, COLS), BF16)] * (ZH - 1),
        compiler_params=params(16),
        cost_estimate=pl.CostEstimate(flops=10**6, bytes_accessed=2 * 2**20, transcendentals=0),
        name="pair",
    )(kept, taken)


def step_kernel(
    place, own, r1, r2, r3, b_in, m_in, e_in, b_out, m_out, e_out,
    nb_in, nb_out, nm_in, nm_out, kept, given, weights,
):
    total = own[...] + r1[...].astype(F32) + r2[...].astype(F32) + r3[...].astype(F32)

    def nesterov(base, moment, part, expo):
        grad = part * jnp.exp2(expo) / GROUPS
        new_mom = 0.9 * moment + grad
        return base - 0.7 * (grad + 0.9 * new_mom), new_mom

    nb_in[...], nm_in[...] = nesterov(
        b_in[...], m_in[...], total[:, :ROWS_IN], row_exponents(e_in, ROWS_IN)
    )
    nb_out[...], nm_out[...] = nesterov(
        b_out[...], m_out[...], total[:, ROWS_IN:], row_exponents(e_out, ROWS_OUT)
    )
    weights[:, :ROWS_IN] = nb_in[...].astype(BF16)
    weights[:, ROWS_IN:] = nb_out[...].astype(BF16)
    kept[...] = weights[place[2]]
    given[...] = weights[1 - place[2]]


def step_call(place, own, received, base_in, mom_in, exp_in, base_out, mom_out, exp_out):
    vmem = pl.BlockSpec(memory_space=pltpu.VMEM)
    new = [(2, r, COLS) for r in (ROWS_IN, ROWS_OUT, ROWS_IN, ROWS_OUT)]
    return pl.pallas_call(
        step_kernel,
        in_specs=[pl.BlockSpec(memory_space=pltpu.SMEM)] + [vmem] * 10,
        out_specs=[vmem] * 6,
        out_shape=[jax.ShapeDtypeStruct(shape, F32) for shape in new]
        + [jax.ShapeDtypeStruct((ROWS, COLS), BF16)] * 2,
        scratch_shapes=[pltpu.VMEM((2, ROWS, COLS), BF16)],
        compiler_params=params(16),
        cost_estimate=pl.CostEstimate(flops=10**6, bytes_accessed=2 * 2**20, transcendentals=0),
        name="step",
    )(place, own, *received, base_in, mom_in, exp_in, base_out, mom_out, exp_out)


def load_pieces(table, pieces, held, sems, colour, rows):
    copies = []
    for p in range(PIECES):
        copies.append(
            pltpu.make_async_copy(
                pieces[colour * 4 + p // 4].at[p % 4, :, :, rows],
                held.at[colour, :, :, table[4 + colour * PIECES + p]],
                sems.at[colour, p],
            )
        )
    for copy in copies:
        copy.start()
    return copies


def hidden_kernel(table, *refs):
    sets, pieces, (out, x, held, x_sems, sems) = refs[:SETS], refs[SETS : SETS + 8], refs[SETS + 8 :]
    zh, zl = table[0], table[2]
    rows = pl.ds(0, ROWS_IN)
    loads = [pltpu.make_async_copy(sets[i], x.at[i], x_sems.at[i]) for i in range(SETS)]
    loads[0].start()
    copies = [load_pieces(table, pieces, held, sems, 0, rows)]
    loads[1].start()
    copies.append(load_pieces(table, pieces, held, sems, 1, rows))
    gates = (zh // 2, jnp.where((zh == 0) | (zh == 3), 1, 0))
    for colour in range(2):
        for copy in copies[colour]:
            copy.wait()
        for i in range(SETS):
            if colour == 0:
                loads[i].wait()

            def product(k):
                return sum(
                    dot(
                        x[i, :, part * 1024 : (part + 1) * 1024],
                        held[colour, k, part ^ zl].reshape(PIECES * ROWS_IN, COLS),
                    )
                    for part in range(ZL)
                )

            gate, up = product(gates[colour]), product(1 - gates[colour])
            out[i * CAP : (i + 1) * CAP, colour * COLS : (colour + 1) * COLS] = (
                jax.nn.silu(gate) * up
            ).astype(BF16)


SMALL = pl.CostEstimate(flops=10**6, bytes_accessed=10**5, transcendentals=0)


def hidden_call(table, sets, pieces):
    vmem, anywhere = pl.BlockSpec(memory_space=pltpu.VMEM), pl.BlockSpec(memory_space=pl.ANY)
    return pl.pallas_call(
        hidden_kernel,
        in_specs=[pl.BlockSpec(memory_space=pltpu.SMEM)] + [anywhere] * (SETS + 8),
        out_specs=vmem,
        out_shape=jax.ShapeDtypeStruct((SETS * CAP, FF // 2), BF16),
        scratch_shapes=[
            pltpu.VMEM((SETS, CAP, D), BF16),
            pltpu.VMEM((2, 2, ZL, PIECES, ROWS_IN, COLS), BF16),
            pltpu.SemaphoreType.DMA((SETS,)),
            pltpu.SemaphoreType.DMA((2, PIECES)),
        ],
        compiler_params=params(24),
        cost_estimate=pl.CostEstimate(flops=10**6, bytes_accessed=8 * 2**20, transcendentals=0),
        name="hidden",
    )(table, *sets, *pieces)


def outcome_kernel(table, made, got, *refs):
    pieces, outs, (held, sems) = refs[:8], refs[8 : 8 + SETS], refs[8 + SETS :]
    zh, core = table[0], table[1]
    rows = pl.ds(ROWS_IN, ROWS_OUT)
    copies = [load_pieces(table, pieces, held, sems, colour, rows) for colour in range(2)]
    for colour in range(2):
        for copy in copies[colour]:
            copy.wait()
    for i, out in enumerate(outs):
        halves = ((made, i, core), (got, i ^ 1, 1 - core))
        for column in range(ZH):
            k = (zh - column + ZH) % ZH
            total = 0.0
            for colour in range(2):
                part = ((zh + colour) % 2) ^ table[2]
                for hidden, at, side in halves:
                    w = held[k % 2, k // 2, part, pl.ds(side * HALF, HALF)]
                    total = total + dot(
                        hidden[at * CAP : (at + 1) * CAP, colour * COLS : (colour + 1) * COLS],
                        w.reshape(HALF * ROWS_OUT, COLS),
                    )
            out[:, column * COLS : (column + 1) * COLS] = total.astype(BF16)


def outcome_call(table, made, got, pieces):
    vmem, anywhere = pl.BlockSpec(memory_space=pltpu.VMEM), pl.BlockSpec(memory_space=pl.ANY)
    return pl.pallas_call(
        outcome_kernel,
        in_specs=[pl.BlockSpec(memory_space=pltpu.SMEM)] + [vmem] * 2 + [anywhere] * 8,
        out_specs=[vmem] * SETS,
        out_shape=[jax.ShapeDtypeStruct((CAP, D // 2), BF16)] * SETS,
        scratch_shapes=[
            pltpu.VMEM((2, 2, ZL, PIECES, ROWS_OUT, COLS), BF16),
            pltpu.SemaphoreType.DMA((2, PIECES)),
        ],
        compiler_params=params(16),
        cost_estimate=pl.CostEstimate(flops=10**6, bytes_accessed=4 * 2**20, transcendentals=0),
        name="outcome",
    )(table, made, got, *pieces)


def put_kernel(first, table, put, same, cross, gains, *refs):
    out = refs[-1]
    core = table[1]
    for values, side in ((same, core), (cross, 1 - core)):
        at = pl.ds(pl.multiple_of(side * COLS, COLS), COLS)
        rows = (dot(put[...], values[...]) * gains[...]).astype(BF16)
        out[:, at] = rows if first else rows + refs[0][:, at]


def put_call(table, put, same, cross, gains, before=None):
    rows = put.shape[0]
    values = pl.BlockSpec((CAP, COLS), lambda i, s: (0, i))
    block = pl.BlockSpec((rows, 2 * COLS), lambda i, s: (0, i))
    more = [] if before is None else [before]

    def kernel(*refs):
        put_kernel(before is None, *refs)

    return pl.pallas_call(
        kernel,
        grid_spec=pltpu.PrefetchScalarGridSpec(
            num_scalar_prefetch=1,
            grid=(ZH,),
            in_specs=[
                pl.BlockSpec((rows, CAP), lambda i, s: (0, 0)),
                values,
                values,
                pl.BlockSpec((rows, 1), lambda i, s: (0, 0)),
            ]
            + [block] * len(more),
            out_specs=block,
        ),
        out_shape=jax.ShapeDtypeStruct((rows, D), BF16),
        compiler_params=params(16),
        cost_estimate=SMALL,
        name="put",
    )(table, put, same, cross, gains, *more)


def body(
    base_in, base_out, local_in, local_out, mom_in, mom_out, exp_in, exp_out, tokens, routes, gains
):
    zh, core, zl = lax.axis_index("zh"), lax.axis_index("core"), lax.axis_index("zl")
    y, x = lax.axis_index("y"), lax.axis_index("x")
    place = jnp.stack([zh, core, zl, zl]).astype(jnp.int32)
    spots = jnp.asarray(piece_table().reshape(CORE * Y * X, 2 * PIECES))
    spots = lax.dynamic_index_in_dim(spots, (core * Y + y) * X + x, 0, keepdims=False)
    table = jnp.concatenate([place, spots])

    given, kept, b_in, b_out, m_in, m_out = give_call(
        place, (base_in, local_in, exp_in, base_out, local_out, exp_out), (mom_in, mom_out)
    )
    own, *sent = pair_call(kept, lax.ppermute(given, "core", shift(CORE, 1)))
    received = [lax.ppermute(sent[s - 1], "zh", shift(ZH, s)) for s in range(1, ZH)]
    new_base_in, new_base_out, new_mom_in, new_mom_out, kept, given = step_call(
        place, own, received, b_in, m_in, exp_in, b_out, m_out, exp_out
    )

    routes, _ = lax.optimization_barrier((routes, own))
    route = routes[:, 0]
    rank_of = []
    for named in (zl, 1 - zl):
        chosen = route == named
        rank = jnp.cumsum(chosen.astype(jnp.int32)) - 1
        rank_of.append(jnp.where(chosen, rank, -1))
    slots = jnp.arange(CAP, dtype=jnp.int32)
    pick_own, pick_got = [(slots[:, None] == r[None, :]).astype(BF16) for r in rank_of]
    put_own, put_got = [(r[:, None] == slots[None, :]).astype(BF16) for r in rank_of]
    tokens_own = dot(pick_own, tokens).astype(BF16)
    tokens_sent = dot(pick_got, tokens).astype(BF16)
    other_own = lax.ppermute(tokens_own, "core", shift(CORE, 1))

    taken = lax.ppermute(given, "zl", shift(ZL, 1))
    kept, taken, tokens_sent, other_own = lax.optimization_barrier(
        (kept, taken, tokens_sent, other_own)
    )
    both = jnp.stack([kept, taken])
    column = [both] + [lax.ppermute(both, "zh", shift(ZH, s)) for s in range(1, ZH)]
    *column, tokens_sent = lax.optimization_barrier((*column, tokens_sent))

    tokens_got = lax.ppermute(tokens_sent, COLUMN, column_pairs(1, 0))
    held = [jnp.stack([column[c], column[c + 2]])[None] for c in (0, 1)]

    def exchange(arrays, axes, turn):
        return [
            lax.ppermute(a, ("core", axis), flip_pairs(turn)) for a, axis in zip(arrays, axes)
        ]

    for turn in range(2):
        held = [jnp.concatenate(pair) for pair in zip(held, exchange(held, ("x", "y"), turn))]
    first = exchange(held, ("y", "x"), 0)
    second = exchange(held, ("y", "x"), 1)
    third = exchange(first, ("y", "x"), 1)
    pieces = [part[c] for c in range(2) for part in (held, first, second, third)]
    other_got = lax.ppermute(tokens_got, "core", shift(CORE, 1))

    made = hidden_call(table, (other_got, tokens_got), pieces)
    got = lax.ppermute(made, "core", shift(CORE, 1))
    other_own, tokens_own, _ = lax.optimization_barrier((other_own, tokens_own, made))
    near = hidden_call(table, (other_own, tokens_own), pieces)
    far_other, far_mine = outcome_call(table, made, got, pieces)
    near, far_other, far_mine = lax.optimization_barrier((near, far_other, far_mine))
    back_same = lax.ppermute(far_mine, COLUMN, column_pairs(-1, 0))
    back_cross = lax.ppermute(far_other, COLUMN, column_pairs(-1, 1))
    near_got = lax.ppermute(near, "core", shift(CORE, 1))
    near_other, near_mine = outcome_call(table, near, near_got, pieces)
    near_cross = lax.ppermute(near_other, "core", shift(CORE, 1))
    scale = gains[:, None]
    mixed = put_call(table, put_own, near_mine, near_cross, scale)
    mixed = put_call(table, put_got, back_same, back_cross, scale, mixed)
    return (new_base_in, new_base_out, new_mom_in, new_mom_out, mixed)


def solution(mesh):
    split = Mesh(mesh.devices.reshape(ZH, CORE, ZL, Y, X), AXES)
    in_specs = (
        P(None, FSDP, None),
        P(None, FSDP, None),
        P(ISLAND, None, FSDP, None),
        P(ISLAND, None, FSDP, None),
        P(None, FSDP, None),
        P(None, FSDP, None),
        P(None, FSDP),
        P(None, FSDP),
        P(ISLAND + FSDP, None),
        P(ISLAND + FSDP, None),
        P(ISLAND + FSDP),
    )
    out_specs = (
        P(None, FSDP, ISLAND),
        P(None, FSDP, ISLAND),
        P(None, FSDP, ISLAND),
        P(None, FSDP, ISLAND),
        P(ISLAND + FSDP, None),
    )
    return jax.shard_map(body, mesh=split, in_specs=in_specs, out_specs=out_specs, check_vma=False)
```

time: 498 us -> 147 us (0.30)
  waiting for transfers between devices: 406 us -> 58.2 us
  starting transfers between devices: 0.12 us -> 45.2 us
  other arithmetic: 41.8 us -> 2.84 us
  Pallas kernels: 0 us -> 32.4 us
  matrix products: 23.8 us -> 1.69 us
  between operations: 13.8 us -> 0.97 us
  local copies, waits for them, and re-layouts: 11 us -> 5.44 us
    all_gather x2 -> x0, waiting for transfers between devices: 329 us -> none  [the longest x1 171 us: body(): lax.all_gather(weights_in, 'fsdp', axis=1, tiled=True)]
    psum x1 -> x0, waiting for transfers between devices: 77.1 us -> none  [body(): lax.psum(quant_in, 'island').astype(jnp.float32)]
    ppermute x0 -> x26, waiting for transfers between devices: none -> 58.2 us  [the longest x10 36.7 us: exchange(): lax.ppermute(a, ('core', axis), flip_pairs(turn))]
    ppermute x0 -> x26, starting transfers between devices: none -> 45.2 us  [the longest x10 17 us: exchange(): lax.ppermute(a, ('core', axis), flip_pairs(turn))]
    pallas_call x0 -> x9, Pallas kernels: none -> 32.4 us  [the longest x2 12 us: hidden_call(): pl.pallas_call(hidden_kernel, in_specs=[pl.BlockSpec(memory_space=pltpu.S...]
    dot_general x2, matrix products: 23.8 us -> 1.69 us  [dot(): return jnp.dot(a, b, preferred_element_type=F32)]
    scatter-add x1 -> x0, other arithmetic: 17.1 us -> none  [body(): mixed = jnp.zeros((tok_rows, width), jnp.float32).at[slot_rows.reshape(-1...]
    convert_element_type x5 -> x2, other arithmetic: 13.5 us -> 0.27 us  [body(): (r[:, None] == slots[None, :]).astype(BF16)]
  transfers between devices with their start and end apart: 3 -> 26, of which waited for: 3 -> 16; matrix products, arithmetic and copies ran while one was open for 7% -> 3% of each run, Pallas kernels for 0% -> 10%
where the time goes in v1:
time: 147 us
  waiting for transfers between devices  58.2 us (40%)
  starting transfers between devices  45.2 us (31%)
  Pallas kernels  32.4 us (22%)
  local copies, waits for them, and re-layouts  5.44 us (4%)
  other arithmetic  2.84 us (2%)
  matrix products  1.69 us (1%)
    ppermute x10, waiting for transfers between devices, exchange(): lax.ppermute(a, ('core', axis), flip_pairs(turn))  36.7 us
    ppermute x10, starting transfers between devices, exchange(): lax.ppermute(a, ('core', axis), flip_pairs(turn))  17 us
    pallas_call x2, Pallas kernels, hidden_call(): pl.pallas_call(hidden_kernel, in_specs=[pl.BlockSpec(memory_space=pltpu.S...  12 us
    ppermute x3, starting transfers between devices, body(): lax.ppermute(sent[s - 1], 'zh', shift(ZH, s))  10.4 us
    ppermute x3, starting transfers between devices, body(): lax.ppermute(both, 'zh', shift(ZH, s))  8.56 us
    pallas_call x2, Pallas kernels, outcome_call(): pl.pallas_call(outcome_kernel, in_specs=[pl.BlockSpec(memory_space=pltpu....  8.3 us
    ppermute x1, waiting for transfers between devices, body(): back_same = lax.ppermute(far_mine, COLUMN, column_pairs(-1, 0))  7.35 us
    pallas_call x2, Pallas kernels, put_call(): pl.pallas_call(kernel, grid_spec=pltpu.PrefetchScalarGridSpec(num_scalar_...  6.65 us
  transfers between devices with their start and end apart: 26, of which 16 were waited for; matrix products, arithmetic and copies ran while one was open for 3% of the time, Pallas kernels for 10%

profile of v1, /device:TPU:32, one launch (start us, length us, event | category | flops | bytes accessed | tf_op | source)
XLA Modules:
  0.0 146.7 jit_solution(7332909725466542399)
XLA Ops:
  0.7 0.6 pad_add_fusion.place
  1.3 3.8 %give.1 = (bf16[4,2,96,256]{3,2,1,0:T(8,128)(2,1)}, bf16[4,2,96,256]{3,2,1,0:T(8,128)(2,1)}, f32[2,64,256]{2,1,0:T(8,128)}, f32[2,32,256]{2,1,0:T(8,128)}, f32[2,64,256]{2,1,0:T(8,128)}, /*index=5*/f32[2,32,256]{2,1,0:T(8,128)}) custom-call(s32[4]{0:T(128)} %pad_add_fusion.place, f32[2,64,2048]{2,1,0:T(8,128)} %b_in.1, bf16[1,2,64,2048]{3,2,1,0:T(8,128)(2,1)} %l_in.1, ...), custom_call_target="tpu_custom_call" | custom-call | flops 1000000 | bytes 4194304 | tf_op jit(solution)/shard_map/give/pallas_call | solution.py:114
  5.2 1.9 %collective-permute-done.taken = bf16[4,2,96,256]{3,2,1,0:T(8,128)(2,1)S(1)} collective-permute-done((bf16[4,2,96,256]{3,2,1,0:T(8,128)(2,1)}, bf16[4,2,96,256]{3,2,1,0:T(8,128)(2,1)S(1)}, u32[]{:S(2)}, u32[]{:S(2)}) %collective-permute-start) | collective-permute-done | bytes 393248 | tf_op jit(solution)/shard_map/ppermute | solution.py:346
  7.1 1.0 copy-done.6
  9.5 0.8 convolution_convert_fusion.refs_1_
  10.6 3.3 %collective-permute-start.1 = (bf16[2,96,256]{2,1,0:T(8,128)(2,1)S(1)}, bf16[2,96,256]{2,1,0:T(8,128)(2,1)S(1)}, u32[]{:S(2)}, u32[]{:S(2)}) collective-permute-start(bf16[2,96,256]{2,1,0:T(8,128)(2,1)S(1)} %get-tuple-element.43), channel_id=1, source_target_pairs={{0,64},{64,128},{128,192},{192,0},{1,65},{65,129},{129,193},{193,1... | collective-permute-start | bytes 294920 | tf_op jit(solution)/shard_map/ppermute | solution.py:347
  13.9 4.5 %collective-permute-start.2 = (bf16[2,96,256]{2,1,0:T(8,128)(2,1)S(1)}, bf16[2,96,256]{2,1,0:T(8,128)(2,1)S(1)}, u32[]{:S(2)}, u32[]{:S(2)}) collective-permute-start(bf16[2,96,256]{2,1,0:T(8,128)(2,1)S(1)} %get-tuple-element.44), channel_id=1, source_target_pairs={{0,128},{64,192},{128,0},{192,64},{1,129},{65,193},{129,1},{193,65... | collective-permute-start | bytes 294920 | tf_op jit(solution)/shard_map/ppermute | solution.py:347
  18.3 2.7 %collective-permute-start.3 = (bf16[2,96,256]{2,1,0:T(8,128)(2,1)S(1)}, bf16[2,96,256]{2,1,0:T(8,128)(2,1)S(1)}, u32[]{:S(2)}, u32[]{:S(2)}) collective-permute-start(bf16[2,96,256]{2,1,0:T(8,128)(2,1)S(1)} %get-tuple-element.45), channel_id=1, source_target_pairs={{0,192},{64,0},{128,64},{192,128},{1,193},{65,1},{129,65},{193,129... | collective-permute-start | bytes 294920 | tf_op jit(solution)/shard_map/ppermute | solution.py:347
  21.0 0.5 collective-permute-done.1.r1
  21.5 1.2 collective-permute-done.2.r2
  22.7 3.4 %collective-permute-done.3.r3 = bf16[2,96,256]{2,1,0:T(8,128)(2,1)S(1)} collective-permute-done((bf16[2,96,256]{2,1,0:T(8,128)(2,1)S(1)}, bf16[2,96,256]{2,1,0:T(8,128)(2,1)S(1)}, u32[]{:S(2)}, u32[]{:S(2)}) %collective-permute-start.3) | collective-permute-done | bytes 98336 | tf_op jit(solution)/shard_map/ppermute | solution.py:347
  26.2 1.5 %step.1 = (f32[2,64,256]{2,1,0:T(8,128)}, f32[2,32,256]{2,1,0:T(8,128)}, f32[2,64,256]{2,1,0:T(8,128)}, f32[2,32,256]{2,1,0:T(8,128)}, bf16[96,256]{1,0:T(8,128)(2,1)S(1)}, /*index=5*/bf16[96,256]{1,0:T(8,128)(2,1)S(1)}) custom-call(s32[4]{0:T(128)S(1)} %copy-done.11, f32[2,96,256]{2,1,0:T(8,128)S(1)} %get-tuple-element.42.own, ...), custom_call_target="tpu_custom_call" | custom-call | flops 1000000 | bytes 2097152 | tf_op jit(solution)/shard_map/step/pallas_call | solution.py:171
  27.8 3.0 %collective-permute-start.4 = (bf16[96,256]{1,0:T(8,128)(2,1)S(1)}, bf16[96,256]{1,0:T(8,128)(2,1)S(1)}, u32[]{:S(2)}, u32[]{:S(2)}) collective-permute-start(bf16[96,256]{1,0:T(8,128)(2,1)S(1)} %get-tuple-element.56), channel_id=1, source_target_pairs={{0,16},{16,0},{1,17},{17,1},{2,18},{18,2},{3,19},{19,3},{4,20},{20... | collective-permute-start | bytes 147464 | tf_op jit(solution)/shard_map/ppermute | solution.py:366
  30.7 0.8 convolution_convert_fusion.1
  31.6 1.2 collective-permute-done.4
  32.8 2.7 %collective-permute-start.6 = (bf16[2,96,256]{2,1,0:T(8,128)(2,1)S(1)}, bf16[2,96,256]{2,1,0:T(8,128)(2,1)S(1)}, u32[]{:S(2)}, u32[]{:S(2)}) collective-permute-start(bf16[2,96,256]{2,1,0:T(8,128)(2,1)S(1)} %pad_maximum_fusion.4), channel_id=1, source_target_pairs={{0,64},{64,128},{128,192},{192,0},{1,65},{65,129},{129,193},{193,1... | collective-permute-start | bytes 294920 | tf_op jit(solution)/shard_map/ppermute | solution.py:371
  35.5 3.3 %collective-permute-start.7 = (bf16[2,96,256]{2,1,0:T(8,128)(2,1)S(1)}, bf16[2,96,256]{2,1,0:T(8,128)(2,1)S(1)}, u32[]{:S(2)}, u32[]{:S(2)}) collective-permute-start(bf16[2,96,256]{2,1,0:T(8,128)(2,1)S(1)} %pad_maximum_fusion.4), channel_id=1, source_target_pairs={{0,128},{64,192},{128,0},{192,64},{1,129},{65,193},{129,1},{193,65... | collective-permute-start | bytes 294920 | tf_op jit(solution)/shard_map/ppermute | solution.py:371
  38.9 2.5 %collective-permute-start.8 = (bf16[2,96,256]{2,1,0:T(8,128)(2,1)S(1)}, bf16[2,96,256]{2,1,0:T(8,128)(2,1)S(1)}, u32[]{:S(2)}, u32[]{:S(2)}) collective-permute-start(bf16[2,96,256]{2,1,0:T(8,128)(2,1)S(1)} %pad_maximum_fusion.4), channel_id=1, source_target_pairs={{0,192},{64,0},{128,64},{192,128},{1,193},{65,1},{129,65},{193,129... | collective-permute-start | bytes 294920 | tf_op jit(solution)/shard_map/ppermute | solution.py:371
  41.4 4.1 %collective-permute-done.7 = bf16[2,96,256]{2,1,0:T(8,128)(2,1)S(1)} collective-permute-done((bf16[2,96,256]{2,1,0:T(8,128)(2,1)S(1)}, bf16[2,96,256]{2,1,0:T(8,128)(2,1)S(1)}, u32[]{:S(2)}, u32[]{:S(2)}) %collective-permute-start.7) | collective-permute-done | bytes 98336 | tf_op jit(solution)/shard_map/ppermute | solution.py:371
  45.6 4.5 %collective-permute-start.9 = (bf16[320,2048]{1,0:T(8,128)(2,1)S(1)}, bf16[320,2048]{1,0:T(8,128)(2,1)}, u32[]{:S(2)}, u32[]{:S(2)}) collective-permute-start(bf16[320,2048]{1,0:T(8,128)(2,1)S(1)} %convolution_convert_fusion.1), channel_id=1, source_target_pairs={{0,16},{16,64},{32,240},{48,32},{64,80},{80,128},{96,48},{112,96},... | collective-permute-start | bytes 3932168 | tf_op jit(solution)/shard_map/ppermute | solution.py:374
  50.1 1.7 %collective-permute-start.16 = (bf16[1,2,2,96,256]{4,3,2,1,0:T(8,128)(2,1)S(1)}, bf16[1,2,2,96,256]{4,3,2,1,0:T(8,128)(2,1)S(1)}, u32[]{:S(2)}, u32[]{:S(2)}) collective-permute-start(bf16[1,2,2,96,256]{4,3,2,1,0:T(8,128)(2,1)S(1)} %maximum_bitcast_fusion.1), channel_id=1, source_target_pairs={{0,4},{4,0},{8,12},{12,8},{32,44},{36,40},{40,36},{44,32},{1,5},{5... | collective-permute-start | bytes 589832 | tf_op jit(solution)/shard_map/ppermute | solution.py:379
  51.8 1.6 %collective-permute-start.11 = (bf16[1,2,2,96,256]{4,3,2,1,0:T(8,128)(2,1)S(1)}, bf16[1,2,2,96,256]{4,3,2,1,0:T(8,128)(2,1)S(1)}, u32[]{:S(2)}, u32[]{:S(2)}) collective-permute-start(bf16[1,2,2,96,256]{4,3,2,1,0:T(8,128)(2,1)S(1)} %maximum_bitcast_fusion), channel_id=1, source_target_pairs={{0,1},{1,0},{2,3},{3,2},{32,35},{33,34},{34,33},{35,32},{4,5},{5,4... | collective-permute-start | bytes 589832 | tf_op jit(solution)/shard_map/ppermute | solution.py:379
  53.4 2.5 %collective-permute-done.16 = bf16[1,2,2,96,256]{4,3,2,1,0:T(8,128)(2,1)S(1)} collective-permute-done((bf16[1,2,2,96,256]{4,3,2,1,0:T(8,128)(2,1)S(1)}, bf16[1,2,2,96,256]{4,3,2,1,0:T(8,128)(2,1)S(1)}, u32[]{:S(2)}, u32[]{:S(2)}) %collective-permute-start.16) | collective-permute-done | bytes 196640 | tf_op jit(solution)/shard_map/ppermute | solution.py:379
  55.9 3.1 %collective-permute-start.17 = (bf16[2,2,2,96,256]{4,3,2,1,0:T(8,128)(2,1)S(1)}, bf16[2,2,2,96,256]{4,3,2,1,0:T(8,128)(2,1)S(1)}, u32[]{:S(2)}, u32[]{:S(2)}) collective-permute-start(bf16[2,2,2,96,256]{4,3,2,1,0:T(8,128)(2,1)S(1)} %pad_maximum_fusion.3), channel_id=1, source_target_pairs={{0,12},{4,8},{8,4},{12,0},{32,36},{36,32},{40,44},{44,40},{1,13},{... | collective-permute-start | bytes 1179656 | tf_op jit(solution)/shard_map/ppermute | solution.py:379
  59.0 2.8 %collective-permute-start.12 = (bf16[2,2,2,96,256]{4,3,2,1,0:T(8,128)(2,1)S(1)}, bf16[2,2,2,96,256]{4,3,2,1,0:T(8,128)(2,1)S(1)}, u32[]{:S(2)}, u32[]{:S(2)}) collective-permute-start(bf16[2,2,2,96,256]{4,3,2,1,0:T(8,128)(2,1)S(1)} %pad_maximum_fusion.2), channel_id=1, source_target_pairs={{0,3},{1,2},{2,1},{3,0},{32,33},{33,32},{34,35},{35,34},{4,7},{5,6... | collective-permute-start | bytes 1179656 | tf_op jit(solution)/shard_map/ppermute | solution.py:379
  61.9 3.1 %collective-permute-done.17 = bf16[2,2,2,96,256]{4,3,2,1,0:T(8,128)(2,1)S(1)} collective-permute-done((bf16[2,2,2,96,256]{4,3,2,1,0:T(8,128)(2,1)S(1)}, bf16[2,2,2,96,256]{4,3,2,1,0:T(8,128)(2,1)S(1)}, u32[]{:S(2)}, u32[]{:S(2)}) %collective-permute-start.17) | collective-permute-done | bytes 393248 | tf_op jit(solution)/shard_map/ppermute | solution.py:379
  65.1 1.8 %collective-permute-start.18 = (bf16[4,2,2,96,256]{4,3,2,1,0:T(8,128)(2,1)S(1)}, bf16[4,2,2,96,256]{4,3,2,1,0:T(8,128)(2,1)}, u32[]{:S(2)}, u32[]{:S(2)}) collective-permute-start(bf16[4,2,2,96,256]{4,3,2,1,0:T(8,128)(2,1)S(1)} %pad_maximum_fusion.1.refs_6_.refs_4_), channel_id=1, source_target_pairs={{0,1},{1,0},{2,3},{3,2},{32,35},{33,34},{34,33},{35,32},{4,5},{5,4... | collective-permute-start | bytes 2359304 | tf_op jit(solution)/shard_map/ppermute | solution.py:379
  66.8 3.9 %collective-permute-done.12 = bf16[2,2,2,96,256]{4,3,2,1,0:T(8,128)(2,1)S(1)} collective-permute-done((bf16[2,2,2,96,256]{4,3,2,1,0:T(8,128)(2,1)S(1)}, bf16[2,2,2,96,256]{4,3,2,1,0:T(8,128)(2,1)S(1)}, u32[]{:S(2)}, u32[]{:S(2)}) %collective-permute-start.12) | collective-permute-done | bytes 393248 | tf_op jit(solution)/shard_map/ppermute | solution.py:379
  70.7 1.0 pad_maximum_fusion.refs_2_.refs_0_
  71.7 2.8 %collective-permute-start.19 = (bf16[4,2,2,96,256]{4,3,2,1,0:T(8,128)(2,1)S(1)}, bf16[4,2,2,96,256]{4,3,2,1,0:T(8,128)(2,1)}, u32[]{:S(2)}, u32[]{:S(2)}) collective-permute-start(bf16[4,2,2,96,256]{4,3,2,1,0:T(8,128)(2,1)S(1)} %pad_maximum_fusion.1.refs_6_.refs_4_), channel_id=1, source_target_pairs={{0,3},{1,2},{2,1},{3,0},{32,33},{33,32},{34,35},{35,34},{4,7},{5,6... | collective-permute-start | bytes 2359304 | tf_op jit(solution)/shard_map/ppermute | solution.py:379
  74.6 0.6 collective-permute-start.14
  75.2 4.8 %collective-permute-done.18.refs_7_.refs_5_ = bf16[4,2,2,96,256]{4,3,2,1,0:T(8,128)(2,1)} collective-permute-done((bf16[4,2,2,96,256]{4,3,2,1,0:T(8,128)(2,1)S(1)}, bf16[4,2,2,96,256]{4,3,2,1,0:T(8,128)(2,1)}, u32[]{:S(2)}, u32[]{:S(2)}) %collective-permute-start.18) | collective-permute-done | bytes 786464 | tf_op jit(solution)/shard_map/ppermute | solution.py:379
  79.9 2.6 %collective-permute-start.20 = (bf16[4,2,2,96,256]{4,3,2,1,0:T(8,128)(2,1)}, bf16[4,2,2,96,256]{4,3,2,1,0:T(8,128)(2,1)}, u32[]{:S(2)}, u32[]{:S(2)}) collective-permute-start(bf16[4,2,2,96,256]{4,3,2,1,0:T(8,128)(2,1)} %collective-permute-done.18.refs_7_.refs_5_), channel_id=1, source_target_pairs={{0,3},{1,2},{2,1},{3,0},{32,33},{33,32},{34,35},{35,34},{4,7},{5,6... | collective-permute-start | bytes 2359304 | tf_op jit(solution)/shard_map/ppermute | solution.py:379
  82.6 9.8 %collective-permute-done.13.refs_3_.refs_1_ = bf16[4,2,2,96,256]{4,3,2,1,0:T(8,128)(2,1)} collective-permute-done((bf16[4,2,2,96,256]{4,3,2,1,0:T(8,128)(2,1)}, bf16[4,2,2,96,256]{4,3,2,1,0:T(8,128)(2,1)}, u32[]{:S(2)}, u32[]{:S(2)}) %collective-permute-start.13) | collective-permute-done | bytes 786464 | tf_op jit(solution)/shard_map/ppermute | solution.py:379
  92.4 0.7 dynamic-slice_bitcast_fusion
  93.6 12.3 %collective-permute-done.15.refs_5_.refs_3_ = bf16[4,2,2,96,256]{4,3,2,1,0:T(8,128)(2,1)} collective-permute-done((bf16[4,2,2,96,256]{4,3,2,1,0:T(8,128)(2,1)}, bf16[4,2,2,96,256]{4,3,2,1,0:T(8,128)(2,1)}, u32[]{:S(2)}, u32[]{:S(2)}) %collective-permute-start.15) | collective-permute-done | bytes 786464 | tf_op jit(solution)/shard_map/ppermute | solution.py:379
  105.9 6.2 %hidden.2.made = bf16[640,512]{1,0:T(8,128)(2,1)S(1)} custom-call(s32[36]{0:T(128)S(1)} %concatenate.18.table.refs_0_, bf16[320,2048]{1,0:T(8,128)(2,1)} %collective-permute-done.10.refs_0_, bf16[320,2048]{1,0:T(8,128)(2,1)} %collective-permute-done.9.refs_1_, bf16[4,2,2,96,256]{4,3,2,1,0:T(8,128)(2,1)} %pad_maximum_fusion.refs_2_.refs_0_, ...), custom_call_target="tpu_custom_call" | custom-call | flops 1000000 | bytes 8388608 | tf_op jit(solution)/shard_map/hidden/pallas_call | solution.py:236
  112.2 5.9 %hidden.3.made = bf16[640,512]{1,0:T(8,128)(2,1)S(1)} custom-call(s32[36]{0:T(128)S(1)} %concatenate.18.table.refs_0_, bf16[320,2048]{1,0:T(8,128)(2,1)S(1)} %copy-done.5, bf16[320,2048]{1,0:T(8,128)(2,1)S(1)} %copy-done.3, bf16[4,2,2,96,256]{4,3,2,1,0:T(8,128)(2,1)} %pad_maximum_fusion.refs_2_.refs_0_, ...), custom_call_target="tpu_custom_call" | custom-call | flops 1000000 | bytes 8388608 | tf_op jit(solution)/shard_map/hidden/pallas_call | solution.py:236
  118.1 3.9 %outcome.2 = (bf16[320,1024]{1,0:T(8,128)(2,1)S(1)}, bf16[320,1024]{1,0:T(8,128)(2,1)S(1)}) custom-call(s32[36]{0:T(128)S(1)} %concatenate.18.table.refs_0_, bf16[640,512]{1,0:T(8,128)(2,1)S(1)} %hidden.2.made, bf16[640,512]{1,0:T(8,128)(2,1)S(1)} %collective-permute-done.21.got, bf16[4,2,2,96,256]{4,3,2,1,0:T(8,128)(2,1)} %pad_maximum_fusion.refs_2_.refs_0_, ...), custom_call_target="tpu_custom_call" | custom-call | flops 1000000 | bytes 4194304 | tf_op jit(solution)/shard_map/outcome/pallas_call | solution.py:279
  121.9 0.8 copy-done.14
  122.8 0.8 copy-done.15
  124.1 1.5 %copy.18.refs_4_ = f32[512,1]{1,0:T(8,128)} copy(f32[512,1]{0,1:T(1,128)} %bitcast.40) | data formatting | bytes 4096 | tf_op jit(solution)/shard_map/broadcast_in_dim | solution.py:401
  125.6 0.5 collective-permute-start.23
  126.1 4.4 %outcome.3 = (bf16[320,1024]{1,0:T(8,128)(2,1)S(1)}, bf16[320,1024]{1,0:T(8,128)(2,1)S(1)}) custom-call(s32[36]{0:T(128)S(1)} %concatenate.18.table.refs_0_, bf16[640,512]{1,0:T(8,128)(2,1)S(1)} %hidden.3.made, bf16[640,512]{1,0:T(8,128)(2,1)} %collective-permute-done.24.got, bf16[4,2,2,96,256]{4,3,2,1,0:T(8,128)(2,1)} %pad_maximum_fusion.refs_2_.refs_0_, ...), custom_call_target="tpu_custom_call" | custom-call | flops 1000000 | bytes 4194304 | tf_op jit(solution)/shard_map/outcome/pallas_call | solution.py:279
  131.1 1.6 %collective-permute-done.25.refs_3_ = bf16[320,1024]{1,0:T(8,128)(2,1)S(1)} collective-permute-done((bf16[320,1024]{1,0:T(8,128)(2,1)S(1)}, bf16[320,1024]{1,0:T(8,128)(2,1)S(1)}, u32[]{:S(2)}, u32[]{:S(2)}) %collective-permute-start.25) | collective-permute-done | bytes 655392 | tf_op jit(solution)/shard_map/ppermute | solution.py:400
  132.7 2.8 %put.2.refs_5_ = bf16[512,2048]{1,0:T(8,128)(2,1)S(1)} custom-call(s32[36]{0:T(128)S(1)} %concatenate.18.table.refs_0_, bf16[512,320]{1,0:T(8,128)(2,1)S(1)} %fusion.1.refs_1_, bf16[320,1024]{1,0:T(8,128)(2,1)S(1)} %get-tuple-element.73.refs_2_, bf16[320,1024]{1,0:T(8,128)(2,1)S(1)} %collective-permute-done.25.refs_3_, f32[512,1]{1,0:T(8,128)S(1)} %copy-done.1), custom_call_target="tpu_custom_call" | custom-call | flops 1000000 | bytes 100000 | tf_op jit(solution)/shard_map/put/pallas_call | solution.py:312
  135.6 7.3 %collective-permute-done.22.refs_2_ = bf16[320,1024]{1,0:T(8,128)(2,1)S(1)} collective-permute-done((bf16[320,1024]{1,0:T(8,128)(2,1)}, bf16[320,1024]{1,0:T(8,128)(2,1)S(1)}, u32[]{:S(2)}, u32[]{:S(2)}) %collective-permute-start.22) | collective-permute-done | bytes 655392 | tf_op jit(solution)/shard_map/ppermute | solution.py:396
  142.9 3.8 %put.3 = bf16[512,2048]{1,0:T(8,128)(2,1)} custom-call(s32[36]{0:T(128)S(1)} %concatenate.18.table.refs_0_, bf16[512,320]{1,0:T(8,128)(2,1)S(1)} %fusion.refs_1_, bf16[320,1024]{1,0:T(8,128)(2,1)S(1)} %collective-permute-done.22.refs_2_, bf16[320,1024]{1,0:T(8,128)(2,1)S(1)} %collective-permute-done.23.refs_3_, f32[512,1]{1,0:T(8,128)S(1)} %copy-done.1, ...), custom_call_target="tpu_custom_call" | custom-call | flops 1000000 | bytes 100000 | tf_op jit(solution)/shard_map/put/pallas_call | solution.py:312
  (73 shorter events, 3.7 us)
Async XLA Ops:
  0.6 8.8 %copy-start = (bf16[512,2048]{1,0:T(8,128)(2,1)S(1)}, bf16[512,2048]{1,0:T(8,128)(2,1)}, u32[]{:S(2)}) copy-start(bf16[512,2048]{1,0:T(8,128)(2,1)} %param.20) | copy-start | bytes 6291460
  1.3 7.0 %copy-start.16 = (s32[512,1]{0,1:T(1,128)S(1)}, s32[512,1]{0,1:T(1,128)}, u32[]{:S(2)}) copy-start(s32[512,1]{0,1:T(1,128)} %param.21) | copy-start | bytes 6148
  5.1 2.0 %collective-permute-start = (bf16[4,2,96,256]{3,2,1,0:T(8,128)(2,1)}, bf16[4,2,96,256]{3,2,1,0:T(8,128)(2,1)S(1)}, u32[]{:S(2)}, u32[]{:S(2)}) collective-permute-start(bf16[4,2,96,256]{3,2,1,0:T(8,128)(2,1)} %get-tuple-element.41), channel_id=1, source_target_pairs={{0,32},{32,0},{1,33},{33,1},{2,34},{34,2},{3,35},{35,3},{4,36},{36... | collective-permute-start | bytes 1179656 | tf_op jit(solution)/shard_map/ppermute | solution.py:346
  7.1 1.0 copy-start.6
  9.4 16.8 %copy-start.7 = (f32[2,64,256]{2,1,0:T(8,128)S(1)}, f32[2,64,256]{2,1,0:T(8,128)}, u32[]{:S(2)}) copy-start(f32[2,64,256]{2,1,0:T(8,128)} %get-tuple-element.46.b_in) | copy-start | bytes 393220
  9.4 16.8 %copy-start.8 = (f32[2,64,256]{2,1,0:T(8,128)S(1)}, f32[2,64,256]{2,1,0:T(8,128)}, u32[]{:S(2)}) copy-start(f32[2,64,256]{2,1,0:T(8,128)} %get-tuple-element.47.m_in) | copy-start | bytes 393220
  9.4 16.8 %copy-start.9 = (f32[2,32,256]{2,1,0:T(8,128)S(1)}, f32[2,32,256]{2,1,0:T(8,128)}, u32[]{:S(2)}) copy-start(f32[2,32,256]{2,1,0:T(8,128)} %get-tuple-element.48.b_out) | copy-start | bytes 196612
  9.4 16.7 %copy-start.10 = (f32[2,32,256]{2,1,0:T(8,128)S(1)}, f32[2,32,256]{2,1,0:T(8,128)}, u32[]{:S(2)}) copy-start(f32[2,32,256]{2,1,0:T(8,128)} %get-tuple-element.49.m_out) | copy-start | bytes 196612
  9.5 16.7 %copy-start.11 = (s32[4]{0:T(128)S(1)}, s32[4]{0:T(128)}, u32[]{:S(2)}) copy-start(s32[4]{0:T(128)} %pad_add_fusion.place) | copy-start | bytes 52
  9.5 16.7 %copy-start.12 = (s32[2,64]{1,0:T(2,128)S(1)}, s32[2,64]{1,0:T(2,128)}, u32[]{:S(2)}) copy-start(s32[2,64]{1,0:T(2,128)} %e_in.3) | copy-start | bytes 1540
  9.5 16.7 %copy-start.13 = (s32[2,32]{1,0:T(2,128)S(1)}, s32[2,32]{1,0:T(2,128)}, u32[]{:S(2)}) copy-start(s32[2,32]{1,0:T(2,128)} %e_out.3) | copy-start | bytes 772
  10.3 21.3 %copy-start.2 = (bf16[320,2048]{1,0:T(8,128)(2,1)}, bf16[320,2048]{1,0:T(8,128)(2,1)S(1)}, u32[]{:S(2)}) copy-start(bf16[320,2048]{1,0:T(8,128)(2,1)S(1)} %convolution_convert_fusion.refs_1_) | copy-start | bytes 3932164
  10.4 22.5 %collective-permute-start.5 = (bf16[320,2048]{1,0:T(8,128)(2,1)S(1)}, bf16[320,2048]{1,0:T(8,128)(2,1)S(1)}, u32[]{:S(2)}, u32[]{:S(2)}) collective-permute-start(bf16[320,2048]{1,0:T(8,128)(2,1)S(1)} %convolution_convert_fusion.refs_1_), channel_id=1, source_target_pairs={{0,32},{32,0},{1,33},{33,1},{2,34},{34,2},{3,35},{35,3},{4,36},{36... | collective-permute-start | bytes 3932168 | tf_op jit(solution)/shard_map/ppermute | solution.py:364
  10.6 10.9 %collective-permute-start.1 = (bf16[2,96,256]{2,1,0:T(8,128)(2,1)S(1)}, bf16[2,96,256]{2,1,0:T(8,128)(2,1)S(1)}, u32[]{:S(2)}, u32[]{:S(2)}) collective-permute-start(bf16[2,96,256]{2,1,0:T(8,128)(2,1)S(1)} %get-tuple-element.43), channel_id=1, source_target_pairs={{0,64},{64,128},{128,192},{192,0},{1,65},{65,129},{129,193},{193,1... | collective-permute-start | bytes 294920 | tf_op jit(solution)/shard_map/ppermute | solution.py:347
  13.9 8.9 %collective-permute-start.2 = (bf16[2,96,256]{2,1,0:T(8,128)(2,1)S(1)}, bf16[2,96,256]{2,1,0:T(8,128)(2,1)S(1)}, u32[]{:S(2)}, u32[]{:S(2)}) collective-permute-start(bf16[2,96,256]{2,1,0:T(8,128)(2,1)S(1)} %get-tuple-element.44), channel_id=1, source_target_pairs={{0,128},{64,192},{128,0},{192,64},{1,129},{65,193},{129,1},{193,65... | collective-permute-start | bytes 294920 | tf_op jit(solution)/shard_map/ppermute | solution.py:347
  18.3 7.8 %collective-permute-start.3 = (bf16[2,96,256]{2,1,0:T(8,128)(2,1)S(1)}, bf16[2,96,256]{2,1,0:T(8,128)(2,1)S(1)}, u32[]{:S(2)}, u32[]{:S(2)}) collective-permute-start(bf16[2,96,256]{2,1,0:T(8,128)(2,1)S(1)} %get-tuple-element.45), channel_id=1, source_target_pairs={{0,192},{64,0},{128,64},{192,128},{1,193},{65,1},{129,65},{193,129... | collective-permute-start | bytes 294920 | tf_op jit(solution)/shard_map/ppermute | solution.py:347
  27.8 5.1 %collective-permute-start.4 = (bf16[96,256]{1,0:T(8,128)(2,1)S(1)}, bf16[96,256]{1,0:T(8,128)(2,1)S(1)}, u32[]{:S(2)}, u32[]{:S(2)}) collective-permute-start(bf16[96,256]{1,0:T(8,128)(2,1)S(1)} %get-tuple-element.56), channel_id=1, source_target_pairs={{0,16},{16,0},{1,17},{17,1},{2,18},{18,2},{3,19},{19,3},{4,20},{20... | collective-permute-start | bytes 147464 | tf_op jit(solution)/shard_map/ppermute | solution.py:366
  32.8 38.8 %copy-start.4 = (bf16[320,2048]{1,0:T(8,128)(2,1)}, bf16[320,2048]{1,0:T(8,128)(2,1)S(1)}, u32[]{:S(2)}) copy-start(bf16[320,2048]{1,0:T(8,128)(2,1)S(1)} %collective-permute-done.5.refs_0_) | copy-start | bytes 3932164
  32.8 8.6 %collective-permute-start.6 = (bf16[2,96,256]{2,1,0:T(8,128)(2,1)S(1)}, bf16[2,96,256]{2,1,0:T(8,128)(2,1)S(1)}, u32[]{:S(2)}, u32[]{:S(2)}) collective-permute-start(bf16[2,96,256]{2,1,0:T(8,128)(2,1)S(1)} %pad_maximum_fusion.4), channel_id=1, source_target_pairs={{0,64},{64,128},{128,192},{192,0},{1,65},{65,129},{129,193},{193,1... | collective-permute-start | bytes 294920 | tf_op jit(solution)/shard_map/ppermute | solution.py:371
  35.5 10.0 %collective-permute-start.7 = (bf16[2,96,256]{2,1,0:T(8,128)(2,1)S(1)}, bf16[2,96,256]{2,1,0:T(8,128)(2,1)S(1)}, u32[]{:S(2)}, u32[]{:S(2)}) collective-permute-start(bf16[2,96,256]{2,1,0:T(8,128)(2,1)S(1)} %pad_maximum_fusion.4), channel_id=1, source_target_pairs={{0,128},{64,192},{128,0},{192,64},{1,129},{65,193},{129,1},{193,65... | collective-permute-start | bytes 294920 | tf_op jit(solution)/shard_map/ppermute | solution.py:371
  38.9 6.7 %collective-permute-start.8 = (bf16[2,96,256]{2,1,0:T(8,128)(2,1)S(1)}, bf16[2,96,256]{2,1,0:T(8,128)(2,1)S(1)}, u32[]{:S(2)}, u32[]{:S(2)}) collective-permute-start(bf16[2,96,256]{2,1,0:T(8,128)(2,1)S(1)} %pad_maximum_fusion.4), channel_id=1, source_target_pairs={{0,192},{64,0},{128,64},{192,128},{1,193},{65,1},{129,65},{193,129... | collective-permute-start | bytes 294920 | tf_op jit(solution)/shard_map/ppermute | solution.py:371
  45.6 26.0 %collective-permute-start.9 = (bf16[320,2048]{1,0:T(8,128)(2,1)S(1)}, bf16[320,2048]{1,0:T(8,128)(2,1)}, u32[]{:S(2)}, u32[]{:S(2)}) collective-permute-start(bf16[320,2048]{1,0:T(8,128)(2,1)S(1)} %convolution_convert_fusion.1), channel_id=1, source_target_pairs={{0,16},{16,64},{32,240},{48,32},{64,80},{80,128},{96,48},{112,96},... | collective-permute-start | bytes 3932168 | tf_op jit(solution)/shard_map/ppermute | solution.py:374
  50.1 5.8 %collective-permute-start.16 = (bf16[1,2,2,96,256]{4,3,2,1,0:T(8,128)(2,1)S(1)}, bf16[1,2,2,96,256]{4,3,2,1,0:T(8,128)(2,1)S(1)}, u32[]{:S(2)}, u32[]{:S(2)}) collective-permute-start(bf16[1,2,2,96,256]{4,3,2,1,0:T(8,128)(2,1)S(1)} %maximum_bitcast_fusion.1), channel_id=1, source_target_pairs={{0,4},{4,0},{8,12},{12,8},{32,44},{36,40},{40,36},{44,32},{1,5},{5... | collective-permute-start | bytes 589832 | tf_op jit(solution)/shard_map/ppermute | solution.py:379
  51.8 7.2 %collective-permute-start.11 = (bf16[1,2,2,96,256]{4,3,2,1,0:T(8,128)(2,1)S(1)}, bf16[1,2,2,96,256]{4,3,2,1,0:T(8,128)(2,1)S(1)}, u32[]{:S(2)}, u32[]{:S(2)}) collective-permute-start(bf16[1,2,2,96,256]{4,3,2,1,0:T(8,128)(2,1)S(1)} %maximum_bitcast_fusion), channel_id=1, source_target_pairs={{0,1},{1,0},{2,3},{3,2},{32,35},{33,34},{34,33},{35,32},{4,5},{5,4... | collective-permute-start | bytes 589832 | tf_op jit(solution)/shard_map/ppermute | solution.py:379
  55.9 9.1 %collective-permute-start.17 = (bf16[2,2,2,96,256]{4,3,2,1,0:T(8,128)(2,1)S(1)}, bf16[2,2,2,96,256]{4,3,2,1,0:T(8,128)(2,1)S(1)}, u32[]{:S(2)}, u32[]{:S(2)}) collective-permute-start(bf16[2,2,2,96,256]{4,3,2,1,0:T(8,128)(2,1)S(1)} %pad_maximum_fusion.3), channel_id=1, source_target_pairs={{0,12},{4,8},{8,4},{12,0},{32,36},{36,32},{40,44},{44,40},{1,13},{... | collective-permute-start | bytes 1179656 | tf_op jit(solution)/shard_map/ppermute | solution.py:379
  59.0 11.6 %collective-permute-start.12 = (bf16[2,2,2,96,256]{4,3,2,1,0:T(8,128)(2,1)S(1)}, bf16[2,2,2,96,256]{4,3,2,1,0:T(8,128)(2,1)S(1)}, u32[]{:S(2)}, u32[]{:S(2)}) collective-permute-start(bf16[2,2,2,96,256]{4,3,2,1,0:T(8,128)(2,1)S(1)} %pad_maximum_fusion.2), channel_id=1, source_target_pairs={{0,3},{1,2},{2,1},{3,0},{32,33},{33,32},{34,35},{35,34},{4,7},{5,6... | collective-permute-start | bytes 1179656 | tf_op jit(solution)/shard_map/ppermute | solution.py:379
  65.1 14.9 %collective-permute-start.18 = (bf16[4,2,2,96,256]{4,3,2,1,0:T(8,128)(2,1)S(1)}, bf16[4,2,2,96,256]{4,3,2,1,0:T(8,128)(2,1)}, u32[]{:S(2)}, u32[]{:S(2)}) collective-permute-start(bf16[4,2,2,96,256]{4,3,2,1,0:T(8,128)(2,1)S(1)} %pad_maximum_fusion.1.refs_6_.refs_4_), channel_id=1, source_target_pairs={{0,1},{1,0},{2,3},{3,2},{32,35},{33,34},{34,33},{35,32},{4,5},{5,4... | collective-permute-start | bytes 2359304 | tf_op jit(solution)/shard_map/ppermute | solution.py:379
  71.6 20.7 %collective-permute-start.13 = (bf16[4,2,2,96,256]{4,3,2,1,0:T(8,128)(2,1)}, bf16[4,2,2,96,256]{4,3,2,1,0:T(8,128)(2,1)}, u32[]{:S(2)}, u32[]{:S(2)}) collective-permute-start(bf16[4,2,2,96,256]{4,3,2,1,0:T(8,128)(2,1)} %pad_maximum_fusion.refs_2_.refs_0_), channel_id=1, source_target_pairs={{0,4},{4,0},{8,12},{12,8},{32,44},{36,40},{40,36},{44,32},{1,5},{5... | collective-permute-start | bytes 2359304 | tf_op jit(solution)/shard_map/ppermute | solution.py:379
  71.6 34.2 %collective-permute-start.10 = (bf16[320,2048]{1,0:T(8,128)(2,1)}, bf16[320,2048]{1,0:T(8,128)(2,1)}, u32[]{:S(2)}, u32[]{:S(2)}) collective-permute-start(bf16[320,2048]{1,0:T(8,128)(2,1)} %collective-permute-done.9.refs_1_), channel_id=1, source_target_pairs={{0,32},{32,0},{1,33},{33,1},{2,34},{34,2},{3,35},{35,3},{4,36},{36... | collective-permute-start | bytes 3932168 | tf_op jit(solution)/shard_map/ppermute | solution.py:388
  71.7 21.4 %collective-permute-start.19 = (bf16[4,2,2,96,256]{4,3,2,1,0:T(8,128)(2,1)S(1)}, bf16[4,2,2,96,256]{4,3,2,1,0:T(8,128)(2,1)}, u32[]{:S(2)}, u32[]{:S(2)}) collective-permute-start(bf16[4,2,2,96,256]{4,3,2,1,0:T(8,128)(2,1)S(1)} %pad_maximum_fusion.1.refs_6_.refs_4_), channel_id=1, source_target_pairs={{0,3},{1,2},{2,1},{3,0},{32,33},{33,32},{34,35},{35,34},{4,7},{5,6... | collective-permute-start | bytes 2359304 | tf_op jit(solution)/shard_map/ppermute | solution.py:379
  74.6 18.6 %collective-permute-start.14 = (bf16[4,2,2,96,256]{4,3,2,1,0:T(8,128)(2,1)}, bf16[4,2,2,96,256]{4,3,2,1,0:T(8,128)(2,1)}, u32[]{:S(2)}, u32[]{:S(2)}) collective-permute-start(bf16[4,2,2,96,256]{4,3,2,1,0:T(8,128)(2,1)} %pad_maximum_fusion.refs_2_.refs_0_), channel_id=1, source_target_pairs={{0,12},{4,8},{8,4},{12,0},{32,36},{36,32},{40,44},{44,40},{1,13},{... | collective-permute-start | bytes 2359304 | tf_op jit(solution)/shard_map/ppermute | solution.py:379
  79.9 13.6 %collective-permute-start.20 = (bf16[4,2,2,96,256]{4,3,2,1,0:T(8,128)(2,1)}, bf16[4,2,2,96,256]{4,3,2,1,0:T(8,128)(2,1)}, u32[]{:S(2)}, u32[]{:S(2)}) collective-permute-start(bf16[4,2,2,96,256]{4,3,2,1,0:T(8,128)(2,1)} %collective-permute-done.18.refs_7_.refs_5_), channel_id=1, source_target_pairs={{0,3},{1,2},{2,1},{3,0},{32,33},{33,32},{34,35},{35,34},{4,7},{5,6... | collective-permute-start | bytes 2359304 | tf_op jit(solution)/shard_map/ppermute | solution.py:379
  92.4 13.5 %collective-permute-start.15 = (bf16[4,2,2,96,256]{4,3,2,1,0:T(8,128)(2,1)}, bf16[4,2,2,96,256]{4,3,2,1,0:T(8,128)(2,1)}, u32[]{:S(2)}, u32[]{:S(2)}) collective-permute-start(bf16[4,2,2,96,256]{4,3,2,1,0:T(8,128)(2,1)} %collective-permute-done.13.refs_3_.refs_1_), channel_id=1, source_target_pairs={{0,12},{4,8},{8,4},{12,0},{32,36},{36,32},{40,44},{44,40},{1,13},{... | collective-permute-start | bytes 2359304 | tf_op jit(solution)/shard_map/ppermute | solution.py:379
  93.1 19.0 %copy-start.3 = (bf16[320,2048]{1,0:T(8,128)(2,1)S(1)}, bf16[320,2048]{1,0:T(8,128)(2,1)}, u32[]{:S(2)}) copy-start(bf16[320,2048]{1,0:T(8,128)(2,1)} %copy-done.2) | copy-start | bytes 3932164
  93.1 19.0 %copy-start.5 = (bf16[320,2048]{1,0:T(8,128)(2,1)S(1)}, bf16[320,2048]{1,0:T(8,128)(2,1)}, u32[]{:S(2)}) copy-start(bf16[320,2048]{1,0:T(8,128)(2,1)} %copy-done.4) | copy-start | bytes 3932164
  112.1 6.0 %collective-permute-start.21 = (bf16[640,512]{1,0:T(8,128)(2,1)S(1)}, bf16[640,512]{1,0:T(8,128)(2,1)S(1)}, u32[]{:S(2)}, u32[]{:S(2)}) collective-permute-start(bf16[640,512]{1,0:T(8,128)(2,1)S(1)} %hidden.2.made), channel_id=1, source_target_pairs={{0,32},{32,0},{1,33},{33,1},{2,34},{34,2},{3,35},{35,3},{4,36},{36... | collective-permute-start | bytes 1966088 | tf_op jit(solution)/shard_map/ppermute | solution.py:391
  121.9 0.8 copy-start.14
  122.8 0.8 copy-start.15
  123.6 2.5 %collective-permute-start.24 = (bf16[640,512]{1,0:T(8,128)(2,1)S(1)}, bf16[640,512]{1,0:T(8,128)(2,1)}, u32[]{:S(2)}, u32[]{:S(2)}) collective-permute-start(bf16[640,512]{1,0:T(8,128)(2,1)S(1)} %hidden.3.made), channel_id=1, source_target_pairs={{0,32},{32,0},{1,33},{33,1},{2,34},{34,2},{3,35},{35,3},{4,36},{36... | collective-permute-start | bytes 1966088 | tf_op jit(solution)/shard_map/ppermute | solution.py:398
  125.6 7.1 %copy-start.1 = (f32[512,1]{1,0:T(8,128)S(1)}, f32[512,1]{1,0:T(8,128)}, u32[]{:S(2)}) copy-start(f32[512,1]{1,0:T(8,128)} %copy.18.refs_4_) | copy-start | bytes 6148
  125.6 17.3 %collective-permute-start.22 = (bf16[320,1024]{1,0:T(8,128)(2,1)}, bf16[320,1024]{1,0:T(8,128)(2,1)S(1)}, u32[]{:S(2)}, u32[]{:S(2)}) collective-permute-start(bf16[320,1024]{1,0:T(8,128)(2,1)} %copy-done.15), channel_id=1, source_target_pairs={{0,208},{16,0},{32,48},{48,96},{64,16},{80,64},{96,112},{112,160},... | collective-permute-start | bytes 1966088 | tf_op jit(solution)/shard_map/ppermute | solution.py:396
  125.6 17.3 %collective-permute-start.23 = (bf16[320,1024]{1,0:T(8,128)(2,1)}, bf16[320,1024]{1,0:T(8,128)(2,1)S(1)}, u32[]{:S(2)}, u32[]{:S(2)}) collective-permute-start(bf16[320,1024]{1,0:T(8,128)(2,1)} %copy-done.14), channel_id=1, source_target_pairs={{32,208},{48,0},{0,48},{16,96},{96,16},{112,64},{64,112},{80,160},... | collective-permute-start | bytes 1966088 | tf_op jit(solution)/shard_map/ppermute | solution.py:397
  130.6 2.2 %collective-permute-start.25 = (bf16[320,1024]{1,0:T(8,128)(2,1)S(1)}, bf16[320,1024]{1,0:T(8,128)(2,1)S(1)}, u32[]{:S(2)}, u32[]{:S(2)}) collective-permute-start(bf16[320,1024]{1,0:T(8,128)(2,1)S(1)} %get-tuple-element.74), channel_id=1, source_target_pairs={{0,32},{32,0},{1,33},{33,1},{2,34},{34,2},{3,35},{35,3},{4,36},{36... | collective-permute-start | bytes 1966088 | tf_op jit(solution)/shard_map/ppermute | solution.py:400

commit v2 on v1

--- a/solution.py
+++ b/solution.py
@@ -1,3 +1,5 @@
+import functools
+
 import jax
 import jax.numpy as jnp
 import numpy as np
@@ -71,12 +73,16 @@
     return pltpu.CompilerParams(vmem_limit_bytes=mib * 2**20)
 
 
-def row_exponents(expo, rows):
-    eye = lax.broadcasted_iota(jnp.int32, (rows, rows), 0) == lax.broadcasted_iota(
-        jnp.int32, (rows, rows), 1
-    )
-    lines = [jnp.where(eye, expo[e : e + 1, :].astype(F32), 0.0) for e in range(2)]
-    return jnp.stack([jnp.sum(line, axis=1, keepdims=True) for line in lines])
+def column_of(line):
+    size = line.shape[1]
+    eye = lax.broadcasted_iota(jnp.int32, (size, size), 0) == lax.broadcasted_iota(
+        jnp.int32, (size, size), 1
+    )
+    return jnp.sum(jnp.where(eye, line, 0.0), axis=1, keepdims=True)
+
+
+def row_exponents(expo):
+    return jnp.stack([column_of(expo[e : e + 1, :].astype(F32)) for e in range(2)])
 
 
 def give_kernel(
@@ -97,7 +103,7 @@
         (b_in, l_in, e_in, ROWS_IN, 0),
         (b_out, l_out, e_out, ROWS_OUT, ROWS_IN),
     ):
-        scale = jnp.exp2(-row_exponents(expo, rows))
+        scale = jnp.exp2(-row_exponents(expo))
         for step in range(ZH):
             for out, side in ((given, 1 - core), (kept, core)):
                 column = (((zh + step) % ZH) * CORE + side) * COLS
@@ -154,10 +160,10 @@
         return base - 0.7 * (grad + 0.9 * new_mom), new_mom
 
     nb_in[...], nm_in[...] = nesterov(
-        b_in[...], m_in[...], total[:, :ROWS_IN], row_exponents(e_in, ROWS_IN)
+        b_in[...], m_in[...], total[:, :ROWS_IN], row_exponents(e_in)
     )
     nb_out[...], nm_out[...] = nesterov(
-        b_out[...], m_out[...], total[:, ROWS_IN:], row_exponents(e_out, ROWS_OUT)
+        b_out[...], m_out[...], total[:, ROWS_IN:], row_exponents(e_out)
     )
     weights[:, :ROWS_IN] = nb_in[...].astype(BF16)
     weights[:, ROWS_IN:] = nb_out[...].astype(BF16)
@@ -196,8 +202,13 @@
     return copies
 
 
-def hidden_kernel(table, *refs):
-    sets, pieces, (out, x, held, x_sems, sems) = refs[:SETS], refs[SETS : SETS + 8], refs[SETS + 8 :]
+def hidden_kernel(parts, table, *refs):
+    sets, pieces, outs, (x, held, x_sems, sems) = (
+        refs[:SETS],
+        refs[SETS : SETS + 8],
+        refs[SETS + 8 : -4],
+        refs[-4:],
+    )
     zh, zl = table[0], table[2]
     rows = pl.ds(0, ROWS_IN)
     loads = [pltpu.make_async_copy(sets[i], x.at[i], x_sems.at[i]) for i in range(SETS)]
@@ -223,21 +234,26 @@
                 )
 
             gate, up = product(gates[colour]), product(1 - gates[colour])
-            out[i * CAP : (i + 1) * CAP, colour * COLS : (colour + 1) * COLS] = (
-                jax.nn.silu(gate) * up
-            ).astype(BF16)
-
-
-SMALL = pl.CostEstimate(flops=10**6, bytes_accessed=10**5, transcendentals=0)
-
-
-def hidden_call(table, sets, pieces):
+            value = (jax.nn.silu(gate) * up).astype(BF16)
+            at = slice(colour * COLS, (colour + 1) * COLS)
+            outs[0][i * CAP : (i + 1) * CAP, at] = value
+            for part in range(parts):
+                step = CAP // parts
+                outs[1 + i * parts + part][:, at] = value[part * step : (part + 1) * step]
+
+
+SMALL = pl.CostEstimate(flops=10**3, bytes_accessed=10**3, transcendentals=0)
+LARGE = pl.CostEstimate(flops=10**9, bytes_accessed=6 * 2**20, transcendentals=0)
+
+
+def hidden_call(table, sets, pieces, parts):
     vmem, anywhere = pl.BlockSpec(memory_space=pltpu.VMEM), pl.BlockSpec(memory_space=pl.ANY)
     return pl.pallas_call(
-        hidden_kernel,
+        functools.partial(hidden_kernel, parts),
         in_specs=[pl.BlockSpec(memory_space=pltpu.SMEM)] + [anywhere] * (SETS + 8),
-        out_specs=vmem,
-        out_shape=jax.ShapeDtypeStruct((SETS * CAP, FF // 2), BF16),
+        out_specs=[vmem] * (1 + SETS * parts),
+        out_shape=[jax.ShapeDtypeStruct((SETS * CAP, FF // 2), BF16)]
+        + [jax.ShapeDtypeStruct((CAP // parts, FF // 2), BF16)] * (SETS * parts),
         scratch_shapes=[
             pltpu.VMEM((SETS, CAP, D), BF16),
             pltpu.VMEM((2, 2, ZL, PIECES, ROWS_IN, COLS), BF16),
@@ -245,89 +261,101 @@
             pltpu.SemaphoreType.DMA((2, PIECES)),
         ],
         compiler_params=params(24),
-        cost_estimate=pl.CostEstimate(flops=10**6, bytes_accessed=8 * 2**20, transcendentals=0),
+        cost_estimate=SMALL,
         name="hidden",
     )(table, *sets, *pieces)
 
 
-def outcome_kernel(table, made, got, *refs):
-    pieces, outs, (held, sems) = refs[:8], refs[8 : 8 + SETS], refs[8 + SETS :]
+def outcome_kernel(table, made, got0, got1, *refs):
+    pieces, outs, (held, sems) = refs[:8], refs[8:-2], refs[-2:]
     zh, core = table[0], table[1]
     rows = pl.ds(ROWS_IN, ROWS_OUT)
     copies = [load_pieces(table, pieces, held, sems, colour, rows) for colour in range(2)]
     for colour in range(2):
         for copy in copies[colour]:
             copy.wait()
-    for i, out in enumerate(outs):
-        halves = ((made, i, core), (got, i ^ 1, 1 - core))
+    step = CAP // (len(outs) - 1)
+    for i, got in enumerate((got1, got0)):
+        halves = ((made[i * CAP : (i + 1) * CAP, :], core), (got[...], 1 - core))
         for column in range(ZH):
             k = (zh - column + ZH) % ZH
             total = 0.0
             for colour in range(2):
                 part = ((zh + colour) % 2) ^ table[2]
-                for hidden, at, side in halves:
+                for hidden, side in halves:
                     w = held[k % 2, k // 2, part, pl.ds(side * HALF, HALF)]
                     total = total + dot(
-                        hidden[at * CAP : (at + 1) * CAP, colour * COLS : (colour + 1) * COLS],
+                        hidden[:, colour * COLS : (colour + 1) * COLS],
                         w.reshape(HALF * ROWS_OUT, COLS),
                     )
-            out[:, column * COLS : (column + 1) * COLS] = total.astype(BF16)
-
-
-def outcome_call(table, made, got, pieces):
+            total = total.astype(BF16)
+            at = slice(column * COLS, (column + 1) * COLS)
+            if i == 1:
+                outs[-1][:, at] = total
+            else:
+                for part, out in enumerate(outs[:-1]):
+                    out[:, at] = total[part * step : (part + 1) * step]
+
+
+def outcome_call(table, made, got, pieces, parts):
     vmem, anywhere = pl.BlockSpec(memory_space=pltpu.VMEM), pl.BlockSpec(memory_space=pl.ANY)
     return pl.pallas_call(
         outcome_kernel,
-        in_specs=[pl.BlockSpec(memory_space=pltpu.SMEM)] + [vmem] * 2 + [anywhere] * 8,
-        out_specs=[vmem] * SETS,
-        out_shape=[jax.ShapeDtypeStruct((CAP, D // 2), BF16)] * SETS,
+        in_specs=[pl.BlockSpec(memory_space=pltpu.SMEM)] + [vmem] * 3 + [anywhere] * 8,
+        out_specs=[vmem] * (parts + 1),
+        out_shape=[jax.ShapeDtypeStruct((CAP // parts, D // 2), BF16)] * parts
+        + [jax.ShapeDtypeStruct((CAP, D // 2), BF16)],
         scratch_shapes=[
             pltpu.VMEM((2, 2, ZL, PIECES, ROWS_OUT, COLS), BF16),
             pltpu.SemaphoreType.DMA((2, PIECES)),
         ],
-        compiler_params=params(16),
-        cost_estimate=pl.CostEstimate(flops=10**6, bytes_accessed=4 * 2**20, transcendentals=0),
+        compiler_params=params(20),
+        cost_estimate=SMALL,
         name="outcome",
-    )(table, made, got, *pieces)
-
-
-def put_kernel(first, table, put, same, cross, gains, *refs):
-    out = refs[-1]
+    )(table, made, *got, *pieces)
+
+
+def put_kernel(before, table, put, gains, same, *refs):
+    cross, out, scale = [ref[...] for ref in refs[before:-2]], refs[-2], refs[-1]
     core = table[1]
-    for values, side in ((same, core), (cross, 1 - core)):
+
+    @pl.when(pl.program_id(0) == 0)
+    def _():
+        scale[...] = column_of(gains[...])
+
+    for values, side in (
+        (same[...], core),
+        (cross[0] if len(cross) == 1 else jnp.concatenate(cross), 1 - core),
+    ):
         at = pl.ds(pl.multiple_of(side * COLS, COLS), COLS)
-        rows = (dot(put[...], values[...]) * gains[...]).astype(BF16)
-        out[:, at] = rows if first else rows + refs[0][:, at]
-
-
-def put_call(table, put, same, cross, gains, before=None):
+        rows = (dot(put[...], values) * scale[...]).astype(BF16)
+        out[:, at] = rows + refs[0][:, at] if before else rows
+
+
+def put_call(table, put, gains, same, cross, *before):
     rows = put.shape[0]
-    values = pl.BlockSpec((CAP, COLS), lambda i, s: (0, i))
+    part = pl.BlockSpec((CAP // len(cross), COLS), lambda i, s: (0, i))
     block = pl.BlockSpec((rows, 2 * COLS), lambda i, s: (0, i))
-    more = [] if before is None else [before]
-
-    def kernel(*refs):
-        put_kernel(before is None, *refs)
-
-    return pl.pallas_call(
-        kernel,
+    return pl.pallas_call(
+        functools.partial(put_kernel, len(before)),
         grid_spec=pltpu.PrefetchScalarGridSpec(
             num_scalar_prefetch=1,
             grid=(ZH,),
             in_specs=[
                 pl.BlockSpec((rows, CAP), lambda i, s: (0, 0)),
-                values,
-                values,
-                pl.BlockSpec((rows, 1), lambda i, s: (0, 0)),
+                pl.BlockSpec((1, rows), lambda i, s: (0, 0)),
+                pl.BlockSpec((CAP, COLS), lambda i, s: (0, i)),
             ]
-            + [block] * len(more),
+            + [block] * len(before)
+            + [part] * len(cross),
             out_specs=block,
+            scratch_shapes=[pltpu.VMEM((rows, 1), F32)],
         ),
         out_shape=jax.ShapeDtypeStruct((rows, D), BF16),
         compiler_params=params(16),
-        cost_estimate=SMALL,
+        cost_estimate=LARGE if before else SMALL,
         name="put",
-    )(table, put, same, cross, gains, *more)
+    )(table, put, gains, same, *before, *cross)
 
 
 def body(
@@ -387,20 +415,25 @@
     pieces = [part[c] for c in range(2) for part in (held, first, second, third)]
     other_got = lax.ppermute(tokens_got, "core", shift(CORE, 1))
 
-    made = hidden_call(table, (other_got, tokens_got), pieces)
-    got = lax.ppermute(made, "core", shift(CORE, 1))
-    other_own, tokens_own, _ = lax.optimization_barrier((other_own, tokens_own, made))
-    near = hidden_call(table, (other_own, tokens_own), pieces)
-    far_other, far_mine = outcome_call(table, made, got, pieces)
-    near, far_other, far_mine = lax.optimization_barrier((near, far_other, far_mine))
+    def swap(arrays):
+        return [lax.ppermute(a, "core", shift(CORE, 1)) for a in arrays]
+
+    far = hidden_call(table, (other_got, tokens_got), pieces, 1)
+    far_got = swap(far[1:])
+    other_own, tokens_own, _ = lax.optimization_barrier((other_own, tokens_own, far[0]))
+    near = hidden_call(table, (other_own, tokens_own), pieces, 1)
+    near_got = swap(near[1:])
+    far_other, far_mine = outcome_call(table, far[0], far_got, pieces, 1)
+    far_other, far_mine, near, near_got = lax.optimization_barrier(
+        (far_other, far_mine, near[0], near_got)
+    )
     back_same = lax.ppermute(far_mine, COLUMN, column_pairs(-1, 0))
     back_cross = lax.ppermute(far_other, COLUMN, column_pairs(-1, 1))
-    near_got = lax.ppermute(near, "core", shift(CORE, 1))
-    near_other, near_mine = outcome_call(table, near, near_got, pieces)
-    near_cross = lax.ppermute(near_other, "core", shift(CORE, 1))
-    scale = gains[:, None]
-    mixed = put_call(table, put_own, near_mine, near_cross, scale)
-    mixed = put_call(table, put_got, back_same, back_cross, scale, mixed)
+    *near_other, near_mine = outcome_call(table, near, near_got, pieces, 4)
+    near_cross = swap(near_other)
+    line = gains[None, :]
+    mixed = put_call(table, put_own, line, near_mine, near_cross)
+    mixed = put_call(table, put_got, line, back_same, [back_cross], mixed)
     return (new_base_in, new_base_out, new_mom_in, new_mom_out, mixed)
 
 

time: 147 us -> 145 us (0.986)
  local copies, waits for them, and re-layouts: 5.44 us -> 2.23 us
  starting transfers between devices: 45.2 us -> 46.8 us
    unnamed x34 -> x30, local copies, waits for them, and re-layouts: 2.74 us -> 1.07 us
    broadcast_in_dim x1 -> x0, local copies, waits for them, and re-layouts: 1.53 us -> none  [body(): scale = gains[:, None]]
  transfers between devices with their start and end apart: 26 -> 31, of which waited for: 16 -> 19; matrix products, arithmetic and copies ran while one was open for 3% -> 2% of each run, Pallas kernels for 10% -> 13%
where the time goes in v2:
time: 145 us; the launch traced here: 144 us
  waiting for transfers between devices  57.7 us (40%)
  starting transfers between devices  46.8 us (32%)
  Pallas kernels  32.1 us (22%)
  other arithmetic  2.9 us (2%)
  local copies, waits for them, and re-layouts  2.23 us (2%)
  matrix products  1.69 us (1%)
    ppermute x10, waiting for transfers between devices, exchange(): lax.ppermute(a, ('core', axis), flip_pairs(turn))  36.7 us
    ppermute x10, starting transfers between devices, exchange(): lax.ppermute(a, ('core', axis), flip_pairs(turn))  17 us
    pallas_call x2, Pallas kernels, hidden_call(): pl.pallas_call(functools.partial(hidden_kernel, parts), in_specs=[pl.Bloc...  11.9 us
    ppermute x3, starting transfers between devices, body(): lax.ppermute(sent[s - 1], 'zh', shift(ZH, s))  10.4 us
    ppermute x3, starting transfers between devices, body(): lax.ppermute(both, 'zh', shift(ZH, s))  8.56 us
    pallas_call x2, Pallas kernels, outcome_call(): pl.pallas_call(outcome_kernel, in_specs=[pl.BlockSpec(memory_space=pltpu....  7.75 us
    pallas_call x2, Pallas kernels, put_call(): pl.pallas_call(functools.partial(put_kernel, len(before)), grid_spec=pltp...  7.01 us
    ppermute x1, waiting for transfers between devices, body(): back_same = lax.ppermute(far_mine, COLUMN, column_pairs(-1, 0))  6.8 us
  transfers between devices with their start and end apart: 31, of which 19 were waited for; matrix products, arithmetic and copies ran while one was open for 2% of the time, Pallas kernels for 13%

profile of v2, /device:TPU:32, one launch (start us, length us, event | category | flops | bytes accessed | tf_op | source)
XLA Modules:
  0.0 144.4 jit_solution(15751410056140841574)
XLA Ops:
  0.7 0.7 pad_add_fusion.place
  1.3 3.8 %give.1 = (bf16[4,2,96,256]{3,2,1,0:T(8,128)(2,1)}, bf16[4,2,96,256]{3,2,1,0:T(8,128)(2,1)}, f32[2,64,256]{2,1,0:T(8,128)}, f32[2,32,256]{2,1,0:T(8,128)}, f32[2,64,256]{2,1,0:T(8,128)}, /*index=5*/f32[2,32,256]{2,1,0:T(8,128)}) custom-call(s32[4]{0:T(128)} %pad_add_fusion.place, f32[2,64,2048]{2,1,0:T(8,128)} %b_in.1, bf16[1,2,64,2048]{3,2,1,0:T(8,128)(2,1)} %l_in.1, ...), custom_call_target="tpu_custom_call" | custom-call | flops 1000000 | bytes 4194304 | tf_op jit(solution)/shard_map/give/pallas_call | solution.py:120
  5.3 1.9 %collective-permute-done.taken = bf16[4,2,96,256]{3,2,1,0:T(8,128)(2,1)S(1)} collective-permute-done((bf16[4,2,96,256]{3,2,1,0:T(8,128)(2,1)}, bf16[4,2,96,256]{3,2,1,0:T(8,128)(2,1)S(1)}, u32[]{:S(2)}, u32[]{:S(2)}) %collective-permute-start) | collective-permute-done | bytes 393248 | tf_op jit(solution)/shard_map/ppermute | solution.py:374
  7.2 1.0 copy-done.5
  9.5 0.9 convolution_convert_fusion.refs_1_
  10.6 3.3 %collective-permute-start.1 = (bf16[2,96,256]{2,1,0:T(8,128)(2,1)S(1)}, bf16[2,96,256]{2,1,0:T(8,128)(2,1)S(1)}, u32[]{:S(2)}, u32[]{:S(2)}) collective-permute-start(bf16[2,96,256]{2,1,0:T(8,128)(2,1)S(1)} %get-tuple-element.54), channel_id=1, source_target_pairs={{0,64},{64,128},{128,192},{192,0},{1,65},{65,129},{129,193},{193,1... | collective-permute-start | bytes 294920 | tf_op jit(solution)/shard_map/ppermute | solution.py:375
  13.9 4.5 %collective-permute-start.2 = (bf16[2,96,256]{2,1,0:T(8,128)(2,1)S(1)}, bf16[2,96,256]{2,1,0:T(8,128)(2,1)S(1)}, u32[]{:S(2)}, u32[]{:S(2)}) collective-permute-start(bf16[2,96,256]{2,1,0:T(8,128)(2,1)S(1)} %get-tuple-element.55), channel_id=1, source_target_pairs={{0,128},{64,192},{128,0},{192,64},{1,129},{65,193},{129,1},{193,65... | collective-permute-start | bytes 294920 | tf_op jit(solution)/shard_map/ppermute | solution.py:375
  18.4 2.7 %collective-permute-start.3 = (bf16[2,96,256]{2,1,0:T(8,128)(2,1)S(1)}, bf16[2,96,256]{2,1,0:T(8,128)(2,1)S(1)}, u32[]{:S(2)}, u32[]{:S(2)}) collective-permute-start(bf16[2,96,256]{2,1,0:T(8,128)(2,1)S(1)} %get-tuple-element.56), channel_id=1, source_target_pairs={{0,192},{64,0},{128,64},{192,128},{1,193},{65,1},{129,65},{193,129... | collective-permute-start | bytes 294920 | tf_op jit(solution)/shard_map/ppermute | solution.py:375
  21.1 0.5 collective-permute-done.1.r1
  21.6 1.2 collective-permute-done.2.r2
  22.8 3.4 %collective-permute-done.3.r3 = bf16[2,96,256]{2,1,0:T(8,128)(2,1)S(1)} collective-permute-done((bf16[2,96,256]{2,1,0:T(8,128)(2,1)S(1)}, bf16[2,96,256]{2,1,0:T(8,128)(2,1)S(1)}, u32[]{:S(2)}, u32[]{:S(2)}) %collective-permute-start.3) | collective-permute-done | bytes 98336 | tf_op jit(solution)/shard_map/ppermute | solution.py:375
  26.3 1.5 %step.1 = (f32[2,64,256]{2,1,0:T(8,128)}, f32[2,32,256]{2,1,0:T(8,128)}, f32[2,64,256]{2,1,0:T(8,128)}, f32[2,32,256]{2,1,0:T(8,128)}, bf16[96,256]{1,0:T(8,128)(2,1)S(1)}, /*index=5*/bf16[96,256]{1,0:T(8,128)(2,1)S(1)}) custom-call(s32[4]{0:T(128)S(1)} %copy-done.11, f32[2,96,256]{2,1,0:T(8,128)S(1)} %get-tuple-element.53.own, ...), custom_call_target="tpu_custom_call" | custom-call | flops 1000000 | bytes 2097152 | tf_op jit(solution)/shard_map/step/pallas_call | solution.py:177
  27.8 3.0 %collective-permute-start.4 = (bf16[96,256]{1,0:T(8,128)(2,1)S(1)}, bf16[96,256]{1,0:T(8,128)(2,1)S(1)}, u32[]{:S(2)}, u32[]{:S(2)}) collective-permute-start(bf16[96,256]{1,0:T(8,128)(2,1)S(1)} %get-tuple-element.67), channel_id=1, source_target_pairs={{0,16},{16,0},{1,17},{17,1},{2,18},{18,2},{3,19},{19,3},{4,20},{20... | collective-permute-start | bytes 147464 | tf_op jit(solution)/shard_map/ppermute | solution.py:394
  30.8 0.8 convolution_convert_fusion.1
  31.7 1.2 collective-permute-done.4
  32.9 2.7 %collective-permute-start.6 = (bf16[2,96,256]{2,1,0:T(8,128)(2,1)S(1)}, bf16[2,96,256]{2,1,0:T(8,128)(2,1)S(1)}, u32[]{:S(2)}, u32[]{:S(2)}) collective-permute-start(bf16[2,96,256]{2,1,0:T(8,128)(2,1)S(1)} %pad_maximum_fusion.4), channel_id=1, source_target_pairs={{0,64},{64,128},{128,192},{192,0},{1,65},{65,129},{129,193},{193,1... | collective-permute-start | bytes 294920 | tf_op jit(solution)/shard_map/ppermute | solution.py:399
  35.6 3.3 %collective-permute-start.7 = (bf16[2,96,256]{2,1,0:T(8,128)(2,1)S(1)}, bf16[2,96,256]{2,1,0:T(8,128)(2,1)S(1)}, u32[]{:S(2)}, u32[]{:S(2)}) collective-permute-start(bf16[2,96,256]{2,1,0:T(8,128)(2,1)S(1)} %pad_maximum_fusion.4), channel_id=1, source_target_pairs={{0,128},{64,192},{128,0},{192,64},{1,129},{65,193},{129,1},{193,65... | collective-permute-start | bytes 294920 | tf_op jit(solution)/shard_map/ppermute | solution.py:399
  38.9 2.5 %collective-permute-start.8 = (bf16[2,96,256]{2,1,0:T(8,128)(2,1)S(1)}, bf16[2,96,256]{2,1,0:T(8,128)(2,1)S(1)}, u32[]{:S(2)}, u32[]{:S(2)}) collective-permute-start(bf16[2,96,256]{2,1,0:T(8,128)(2,1)S(1)} %pad_maximum_fusion.4), channel_id=1, source_target_pairs={{0,192},{64,0},{128,64},{192,128},{1,193},{65,1},{129,65},{193,129... | collective-permute-start | bytes 294920 | tf_op jit(solution)/shard_map/ppermute | solution.py:399
  41.4 4.1 %collective-permute-done.7 = bf16[2,96,256]{2,1,0:T(8,128)(2,1)S(1)} collective-permute-done((bf16[2,96,256]{2,1,0:T(8,128)(2,1)S(1)}, bf16[2,96,256]{2,1,0:T(8,128)(2,1)S(1)}, u32[]{:S(2)}, u32[]{:S(2)}) %collective-permute-start.7) | collective-permute-done | bytes 98336 | tf_op jit(solution)/shard_map/ppermute | solution.py:399
  45.6 4.5 %collective-permute-start.9 = (bf16[320,2048]{1,0:T(8,128)(2,1)S(1)}, bf16[320,2048]{1,0:T(8,128)(2,1)}, u32[]{:S(2)}, u32[]{:S(2)}) collective-permute-start(bf16[320,2048]{1,0:T(8,128)(2,1)S(1)} %convolution_convert_fusion.1), channel_id=1, source_target_pairs={{0,16},{16,64},{32,240},{48,32},{64,80},{80,128},{96,48},{112,96},... | collective-permute-start | bytes 3932168 | tf_op jit(solution)/shard_map/ppermute | solution.py:402
  50.1 1.7 %collective-permute-start.16 = (bf16[1,2,2,96,256]{4,3,2,1,0:T(8,128)(2,1)S(1)}, bf16[1,2,2,96,256]{4,3,2,1,0:T(8,128)(2,1)S(1)}, u32[]{:S(2)}, u32[]{:S(2)}) collective-permute-start(bf16[1,2,2,96,256]{4,3,2,1,0:T(8,128)(2,1)S(1)} %maximum_bitcast_fusion.1), channel_id=1, source_target_pairs={{0,4},{4,0},{8,12},{12,8},{32,44},{36,40},{40,36},{44,32},{1,5},{5... | collective-permute-start | bytes 589832 | tf_op jit(solution)/shard_map/ppermute | solution.py:407
  51.8 1.6 %collective-permute-start.11 = (bf16[1,2,2,96,256]{4,3,2,1,0:T(8,128)(2,1)S(1)}, bf16[1,2,2,96,256]{4,3,2,1,0:T(8,128)(2,1)S(1)}, u32[]{:S(2)}, u32[]{:S(2)}) collective-permute-start(bf16[1,2,2,96,256]{4,3,2,1,0:T(8,128)(2,1)S(1)} %maximum_bitcast_fusion), channel_id=1, source_target_pairs={{0,1},{1,0},{2,3},{3,2},{32,35},{33,34},{34,33},{35,32},{4,5},{5,4... | collective-permute-start | bytes 589832 | tf_op jit(solution)/shard_map/ppermute | solution.py:407
  53.4 2.5 %collective-permute-done.16 = bf16[1,2,2,96,256]{4,3,2,1,0:T(8,128)(2,1)S(1)} collective-permute-done((bf16[1,2,2,96,256]{4,3,2,1,0:T(8,128)(2,1)S(1)}, bf16[1,2,2,96,256]{4,3,2,1,0:T(8,128)(2,1)S(1)}, u32[]{:S(2)}, u32[]{:S(2)}) %collective-permute-start.16) | collective-permute-done | bytes 196640 | tf_op jit(solution)/shard_map/ppermute | solution.py:407
  55.9 3.1 %collective-permute-start.17 = (bf16[2,2,2,96,256]{4,3,2,1,0:T(8,128)(2,1)S(1)}, bf16[2,2,2,96,256]{4,3,2,1,0:T(8,128)(2,1)S(1)}, u32[]{:S(2)}, u32[]{:S(2)}) collective-permute-start(bf16[2,2,2,96,256]{4,3,2,1,0:T(8,128)(2,1)S(1)} %pad_maximum_fusion.3), channel_id=1, source_target_pairs={{0,12},{4,8},{8,4},{12,0},{32,36},{36,32},{40,44},{44,40},{1,13},{... | collective-permute-start | bytes 1179656 | tf_op jit(solution)/shard_map/ppermute | solution.py:407
  59.1 2.8 %collective-permute-start.12 = (bf16[2,2,2,96,256]{4,3,2,1,0:T(8,128)(2,1)S(1)}, bf16[2,2,2,96,256]{4,3,2,1,0:T(8,128)(2,1)S(1)}, u32[]{:S(2)}, u32[]{:S(2)}) collective-permute-start(bf16[2,2,2,96,256]{4,3,2,1,0:T(8,128)(2,1)S(1)} %pad_maximum_fusion.2), channel_id=1, source_target_pairs={{0,3},{1,2},{2,1},{3,0},{32,33},{33,32},{34,35},{35,34},{4,7},{5,6... | collective-permute-start | bytes 1179656 | tf_op jit(solution)/shard_map/ppermute | solution.py:407
  61.9 3.1 %collective-permute-done.17 = bf16[2,2,2,96,256]{4,3,2,1,0:T(8,128)(2,1)S(1)} collective-permute-done((bf16[2,2,2,96,256]{4,3,2,1,0:T(8,128)(2,1)S(1)}, bf16[2,2,2,96,256]{4,3,2,1,0:T(8,128)(2,1)S(1)}, u32[]{:S(2)}, u32[]{:S(2)}) %collective-permute-start.17) | collective-permute-done | bytes 393248 | tf_op jit(solution)/shard_map/ppermute | solution.py:407
  65.1 1.8 %collective-permute-start.18 = (bf16[4,2,2,96,256]{4,3,2,1,0:T(8,128)(2,1)S(1)}, bf16[4,2,2,96,256]{4,3,2,1,0:T(8,128)(2,1)}, u32[]{:S(2)}, u32[]{:S(2)}) collective-permute-start(bf16[4,2,2,96,256]{4,3,2,1,0:T(8,128)(2,1)S(1)} %pad_maximum_fusion.1.refs_6_.refs_4_), channel_id=1, source_target_pairs={{0,1},{1,0},{2,3},{3,2},{32,35},{33,34},{34,33},{35,32},{4,5},{5,4... | collective-permute-start | bytes 2359304 | tf_op jit(solution)/shard_map/ppermute | solution.py:407
  66.9 3.9 %collective-permute-done.12 = bf16[2,2,2,96,256]{4,3,2,1,0:T(8,128)(2,1)S(1)} collective-permute-done((bf16[2,2,2,96,256]{4,3,2,1,0:T(8,128)(2,1)S(1)}, bf16[2,2,2,96,256]{4,3,2,1,0:T(8,128)(2,1)S(1)}, u32[]{:S(2)}, u32[]{:S(2)}) %collective-permute-start.12) | collective-permute-done | bytes 393248 | tf_op jit(solution)/shard_map/ppermute | solution.py:407
  70.7 1.0 pad_maximum_fusion.refs_2_.refs_0_
  71.8 2.8 %collective-permute-start.19 = (bf16[4,2,2,96,256]{4,3,2,1,0:T(8,128)(2,1)S(1)}, bf16[4,2,2,96,256]{4,3,2,1,0:T(8,128)(2,1)}, u32[]{:S(2)}, u32[]{:S(2)}) collective-permute-start(bf16[4,2,2,96,256]{4,3,2,1,0:T(8,128)(2,1)S(1)} %pad_maximum_fusion.1.refs_6_.refs_4_), channel_id=1, source_target_pairs={{0,3},{1,2},{2,1},{3,0},{32,33},{33,32},{34,35},{35,34},{4,7},{5,6... | collective-permute-start | bytes 2359304 | tf_op jit(solution)/shard_map/ppermute | solution.py:407
  74.6 0.6 collective-permute-start.14
  75.2 4.7 %collective-permute-done.18.refs_7_.refs_5_ = bf16[4,2,2,96,256]{4,3,2,1,0:T(8,128)(2,1)} collective-permute-done((bf16[4,2,2,96,256]{4,3,2,1,0:T(8,128)(2,1)S(1)}, bf16[4,2,2,96,256]{4,3,2,1,0:T(8,128)(2,1)}, u32[]{:S(2)}, u32[]{:S(2)}) %collective-permute-start.18) | collective-permute-done | bytes 786464 | tf_op jit(solution)/shard_map/ppermute | solution.py:407
  80.0 2.7 %collective-permute-start.20 = (bf16[4,2,2,96,256]{4,3,2,1,0:T(8,128)(2,1)}, bf16[4,2,2,96,256]{4,3,2,1,0:T(8,128)(2,1)}, u32[]{:S(2)}, u32[]{:S(2)}) collective-permute-start(bf16[4,2,2,96,256]{4,3,2,1,0:T(8,128)(2,1)} %collective-permute-done.18.refs_7_.refs_5_), channel_id=1, source_target_pairs={{0,3},{1,2},{2,1},{3,0},{32,33},{33,32},{34,35},{35,34},{4,7},{5,6... | collective-permute-start | bytes 2359304 | tf_op jit(solution)/shard_map/ppermute | solution.py:407
  82.6 9.8 %collective-permute-done.13.refs_3_.refs_1_ = bf16[4,2,2,96,256]{4,3,2,1,0:T(8,128)(2,1)} collective-permute-done((bf16[4,2,2,96,256]{4,3,2,1,0:T(8,128)(2,1)}, bf16[4,2,2,96,256]{4,3,2,1,0:T(8,128)(2,1)}, u32[]{:S(2)}, u32[]{:S(2)}) %collective-permute-start.13) | collective-permute-done | bytes 786464 | tf_op jit(solution)/shard_map/ppermute | solution.py:407
  92.4 0.7 dynamic-slice_bitcast_fusion
  93.6 12.3 %collective-permute-done.15.refs_5_.refs_3_ = bf16[4,2,2,96,256]{4,3,2,1,0:T(8,128)(2,1)} collective-permute-done((bf16[4,2,2,96,256]{4,3,2,1,0:T(8,128)(2,1)}, bf16[4,2,2,96,256]{4,3,2,1,0:T(8,128)(2,1)}, u32[]{:S(2)}, u32[]{:S(2)}) %collective-permute-start.15) | collective-permute-done | bytes 786464 | tf_op jit(solution)/shard_map/ppermute | solution.py:407
  105.9 6.1 %hidden.2 = (bf16[640,512]{1,0:T(8,128)(2,1)S(1)}, bf16[320,512]{1,0:T(8,128)(2,1)S(1)}, bf16[320,512]{1,0:T(8,128)(2,1)S(1)}) custom-call(s32[36]{0:T(128)S(1)} %concatenate.18.table, bf16[320,2048]{1,0:T(8,128)(2,1)} %collective-permute-done.10.refs_0_, bf16[320,2048]{1,0:T(8,128)(2,1)} %collective-permute-done.9.refs_1_, ...), custom_call_target="tpu_custom_call" | custom-call | flops 1000 | bytes 1000 | tf_op jit(solution)/shard_map/hidden/pallas_call | solution.py:251
  112.2 0.5 collective-permute-start.22
  112.7 5.8 %hidden.3 = (bf16[640,512]{1,0:T(8,128)(2,1)S(1)}, bf16[320,512]{1,0:T(8,128)(2,1)S(1)}, bf16[320,512]{1,0:T(8,128)(2,1)S(1)}) custom-call(s32[36]{0:T(128)S(1)} %concatenate.18.table, bf16[320,2048]{1,0:T(8,128)(2,1)S(1)} %copy-done.4, bf16[320,2048]{1,0:T(8,128)(2,1)S(1)} %copy-done.2, bf16[4,2,2,96,256]{4,3,2,1,0:T(8,128)(2,1)} %pad_maximum_fusion.refs_2_.refs_0_, ...), custom_call_target="tpu_custom_call" | custom-call | flops 1000 | bytes 1000 | tf_op jit(solution)/shard_map/hidden/pallas_call | solution.py:251
  119.1 3.9 %outcome.2 = (bf16[320,1024]{1,0:T(8,128)(2,1)S(1)}, bf16[320,1024]{1,0:T(8,128)(2,1)S(1)}) custom-call(s32[36]{0:T(128)S(1)} %concatenate.18.table, bf16[640,512]{1,0:T(8,128)(2,1)S(1)} %get-tuple-element.76.made, bf16[320,512]{1,0:T(8,128)(2,1)S(1)} %collective-permute-done.21.got0, bf16[320,512]{1,0:T(8,128)(2,1)S(1)} %collective-permute-done.22.got1, ...), custom_call_target="tpu_custom_call" | custom-call | flops 1000 | bytes 1000 | tf_op jit(solution)/shard_map/outcome/pallas_call | solution.py:302
  123.3 0.5 collective-permute-start.30
  123.8 3.9 %outcome.3 = (bf16[80,1024]{1,0:T(8,128)(2,1)S(1)}, bf16[80,1024]{1,0:T(8,128)(2,1)S(1)}, bf16[80,1024]{1,0:T(8,128)(2,1)S(1)}, bf16[80,1024]{1,0:T(8,128)(2,1)S(1)}, bf16[320,1024]{1,0:T(8,128)(2,1)S(1)}) custom-call(s32[36]{0:T(128)S(1)} %concatenate.18.table, bf16[640,512]{1,0:T(8,128)(2,1)S(1)} %get-tuple-element.88.made, ...), custom_call_target="tpu_custom_call" | custom-call | flops 1000 | bytes 1000 | tf_op jit(solution)/shard_map/outcome/pallas_call | solution.py:302
  127.9 0.6 collective-permute-start.27
  128.6 0.6 collective-permute-done.26.refs_0_
  129.9 0.7 collective-permute-done.29.refs_3_
  130.6 3.0 %put.2.refs_0_ = bf16[512,2048]{1,0:T(8,128)(2,1)S(1)} custom-call(s32[36]{0:T(128)S(1)} %concatenate.18.table, bf16[512,320]{1,0:T(8,128)(2,1)S(1)} %fusion.1.put, f32[1,512]{1,0:T(1,128)S(1)} %bitcast.29, bf16[320,1024]{1,0:T(8,128)(2,1)S(1)} %get-tuple-element.91.same, bf16[80,1024]{1,0:T(8,128)(2,1)S(1)} %collective-permute-done.26.refs_0_, ...), custom_call_target="tpu_custom_call" | custom-call | flops 1000 | bytes 1000 | tf_op jit(solution)/shard_map/put/pallas_call | solution.py:339
  133.6 6.8 %collective-permute-done.25.same = bf16[320,1024]{1,0:T(8,128)(2,1)S(1)} collective-permute-done((bf16[320,1024]{1,0:T(8,128)(2,1)S(1)}, bf16[320,1024]{1,0:T(8,128)(2,1)S(1)}, u32[]{:S(2)}, u32[]{:S(2)}) %collective-permute-start.25) | collective-permute-done | bytes 655392 | tf_op jit(solution)/shard_map/ppermute | solution.py:430
  140.4 4.0 %put.3 = bf16[512,2048]{1,0:T(8,128)(2,1)} custom-call(s32[36]{0:T(128)S(1)} %concatenate.18.table, bf16[512,320]{1,0:T(8,128)(2,1)S(1)} %fusion.put, f32[1,512]{1,0:T(1,128)S(1)} %bitcast.30, bf16[320,1024]{1,0:T(8,128)(2,1)S(1)} %collective-permute-done.25.same, bf16[512,2048]{1,0:T(8,128)(2,1)S(1)} %put.2.refs_0_, ...), custom_call_target="tpu_custom_call" | custom-call | flops 1000000000 | bytes 6291456 | tf_op jit(solution)/shard_map/put/pallas_call | solution.py:339
  (78 shorter events, 4.6 us)
Async XLA Ops:
  0.6 8.8 %copy-start = (bf16[512,2048]{1,0:T(8,128)(2,1)S(1)}, bf16[512,2048]{1,0:T(8,128)(2,1)}, u32[]{:S(2)}) copy-start(bf16[512,2048]{1,0:T(8,128)(2,1)} %param.20) | copy-start | bytes 6291460
  1.3 7.0 %copy-start.14 = (s32[512,1]{0,1:T(1,128)S(1)}, s32[512,1]{0,1:T(1,128)}, u32[]{:S(2)}) copy-start(s32[512,1]{0,1:T(1,128)} %param.21) | copy-start | bytes 6148
  5.2 2.0 %collective-permute-start = (bf16[4,2,96,256]{3,2,1,0:T(8,128)(2,1)}, bf16[4,2,96,256]{3,2,1,0:T(8,128)(2,1)S(1)}, u32[]{:S(2)}, u32[]{:S(2)}) collective-permute-start(bf16[4,2,96,256]{3,2,1,0:T(8,128)(2,1)} %get-tuple-element.52), channel_id=1, source_target_pairs={{0,32},{32,0},{1,33},{33,1},{2,34},{34,2},{3,35},{35,3},{4,36},{36... | collective-permute-start | bytes 1179656 | tf_op jit(solution)/shard_map/ppermute | solution.py:374
  7.2 1.0 copy-start.5
  9.5 16.8 %copy-start.6 = (f32[2,64,256]{2,1,0:T(8,128)S(1)}, f32[2,64,256]{2,1,0:T(8,128)}, u32[]{:S(2)}) copy-start(f32[2,64,256]{2,1,0:T(8,128)} %get-tuple-element.57.b_in) | copy-start | bytes 393220
  9.5 16.8 %copy-start.7 = (f32[2,64,256]{2,1,0:T(8,128)S(1)}, f32[2,64,256]{2,1,0:T(8,128)}, u32[]{:S(2)}) copy-start(f32[2,64,256]{2,1,0:T(8,128)} %get-tuple-element.58.m_in) | copy-start | bytes 393220
  9.5 16.8 %copy-start.8 = (f32[2,32,256]{2,1,0:T(8,128)S(1)}, f32[2,32,256]{2,1,0:T(8,128)}, u32[]{:S(2)}) copy-start(f32[2,32,256]{2,1,0:T(8,128)} %get-tuple-element.59.b_out) | copy-start | bytes 196612
  9.5 16.7 %copy-start.9 = (f32[2,32,256]{2,1,0:T(8,128)S(1)}, f32[2,32,256]{2,1,0:T(8,128)}, u32[]{:S(2)}) copy-start(f32[2,32,256]{2,1,0:T(8,128)} %get-tuple-element.60.m_out) | copy-start | bytes 196612
  9.5 16.7 %copy-start.11 = (s32[4]{0:T(128)S(1)}, s32[4]{0:T(128)}, u32[]{:S(2)}) copy-start(s32[4]{0:T(128)} %pad_add_fusion.place) | copy-start | bytes 52
  9.5 16.7 %copy-start.12 = (s32[2,64]{1,0:T(2,128)S(1)}, s32[2,64]{1,0:T(2,128)}, u32[]{:S(2)}) copy-start(s32[2,64]{1,0:T(2,128)} %e_in.3) | copy-start | bytes 1540
  9.5 16.7 %copy-start.13 = (s32[2,32]{1,0:T(2,128)S(1)}, s32[2,32]{1,0:T(2,128)}, u32[]{:S(2)}) copy-start(s32[2,32]{1,0:T(2,128)} %e_out.3) | copy-start | bytes 772
  10.4 21.2 %copy-start.1 = (bf16[320,2048]{1,0:T(8,128)(2,1)}, bf16[320,2048]{1,0:T(8,128)(2,1)S(1)}, u32[]{:S(2)}) copy-start(bf16[320,2048]{1,0:T(8,128)(2,1)S(1)} %convolution_convert_fusion.refs_1_) | copy-start | bytes 3932164
  10.4 22.5 %collective-permute-start.5 = (bf16[320,2048]{1,0:T(8,128)(2,1)S(1)}, bf16[320,2048]{1,0:T(8,128)(2,1)S(1)}, u32[]{:S(2)}, u32[]{:S(2)}) collective-permute-start(bf16[320,2048]{1,0:T(8,128)(2,1)S(1)} %convolution_convert_fusion.refs_1_), channel_id=1, source_target_pairs={{0,32},{32,0},{1,33},{33,1},{2,34},{34,2},{3,35},{35,3},{4,36},{36... | collective-permute-start | bytes 3932168 | tf_op jit(solution)/shard_map/ppermute | solution.py:392
  10.6 10.9 %collective-permute-start.1 = (bf16[2,96,256]{2,1,0:T(8,128)(2,1)S(1)}, bf16[2,96,256]{2,1,0:T(8,128)(2,1)S(1)}, u32[]{:S(2)}, u32[]{:S(2)}) collective-permute-start(bf16[2,96,256]{2,1,0:T(8,128)(2,1)S(1)} %get-tuple-element.54), channel_id=1, source_target_pairs={{0,64},{64,128},{128,192},{192,0},{1,65},{65,129},{129,193},{193,1... | collective-permute-start | bytes 294920 | tf_op jit(solution)/shard_map/ppermute | solution.py:375
  13.9 8.9 %collective-permute-start.2 = (bf16[2,96,256]{2,1,0:T(8,128)(2,1)S(1)}, bf16[2,96,256]{2,1,0:T(8,128)(2,1)S(1)}, u32[]{:S(2)}, u32[]{:S(2)}) collective-permute-start(bf16[2,96,256]{2,1,0:T(8,128)(2,1)S(1)} %get-tuple-element.55), channel_id=1, source_target_pairs={{0,128},{64,192},{128,0},{192,64},{1,129},{65,193},{129,1},{193,65... | collective-permute-start | bytes 294920 | tf_op jit(solution)/shard_map/ppermute | solution.py:375
  18.4 7.8 %collective-permute-start.3 = (bf16[2,96,256]{2,1,0:T(8,128)(2,1)S(1)}, bf16[2,96,256]{2,1,0:T(8,128)(2,1)S(1)}, u32[]{:S(2)}, u32[]{:S(2)}) collective-permute-start(bf16[2,96,256]{2,1,0:T(8,128)(2,1)S(1)} %get-tuple-element.56), channel_id=1, source_target_pairs={{0,192},{64,0},{128,64},{192,128},{1,193},{65,1},{129,65},{193,129... | collective-permute-start | bytes 294920 | tf_op jit(solution)/shard_map/ppermute | solution.py:375
  27.8 5.1 %collective-permute-start.4 = (bf16[96,256]{1,0:T(8,128)(2,1)S(1)}, bf16[96,256]{1,0:T(8,128)(2,1)S(1)}, u32[]{:S(2)}, u32[]{:S(2)}) collective-permute-start(bf16[96,256]{1,0:T(8,128)(2,1)S(1)} %get-tuple-element.67), channel_id=1, source_target_pairs={{0,16},{16,0},{1,17},{17,1},{2,18},{18,2},{3,19},{19,3},{4,20},{20... | collective-permute-start | bytes 147464 | tf_op jit(solution)/shard_map/ppermute | solution.py:394
  32.9 38.8 %copy-start.3 = (bf16[320,2048]{1,0:T(8,128)(2,1)}, bf16[320,2048]{1,0:T(8,128)(2,1)S(1)}, u32[]{:S(2)}) copy-start(bf16[320,2048]{1,0:T(8,128)(2,1)S(1)} %collective-permute-done.5.refs_0_) | copy-start | bytes 3932164
  32.9 8.6 %collective-permute-start.6 = (bf16[2,96,256]{2,1,0:T(8,128)(2,1)S(1)}, bf16[2,96,256]{2,1,0:T(8,128)(2,1)S(1)}, u32[]{:S(2)}, u32[]{:S(2)}) collective-permute-start(bf16[2,96,256]{2,1,0:T(8,128)(2,1)S(1)} %pad_maximum_fusion.4), channel_id=1, source_target_pairs={{0,64},{64,128},{128,192},{192,0},{1,65},{65,129},{129,193},{193,1... | collective-permute-start | bytes 294920 | tf_op jit(solution)/shard_map/ppermute | solution.py:399
  35.6 10.0 %collective-permute-start.7 = (bf16[2,96,256]{2,1,0:T(8,128)(2,1)S(1)}, bf16[2,96,256]{2,1,0:T(8,128)(2,1)S(1)}, u32[]{:S(2)}, u32[]{:S(2)}) collective-permute-start(bf16[2,96,256]{2,1,0:T(8,128)(2,1)S(1)} %pad_maximum_fusion.4), channel_id=1, source_target_pairs={{0,128},{64,192},{128,0},{192,64},{1,129},{65,193},{129,1},{193,65... | collective-permute-start | bytes 294920 | tf_op jit(solution)/shard_map/ppermute | solution.py:399
  38.9 6.7 %collective-permute-start.8 = (bf16[2,96,256]{2,1,0:T(8,128)(2,1)S(1)}, bf16[2,96,256]{2,1,0:T(8,128)(2,1)S(1)}, u32[]{:S(2)}, u32[]{:S(2)}) collective-permute-start(bf16[2,96,256]{2,1,0:T(8,128)(2,1)S(1)} %pad_maximum_fusion.4), channel_id=1, source_target_pairs={{0,192},{64,0},{128,64},{192,128},{1,193},{65,1},{129,65},{193,129... | collective-permute-start | bytes 294920 | tf_op jit(solution)/shard_map/ppermute | solution.py:399
  45.6 26.1 %collective-permute-start.9 = (bf16[320,2048]{1,0:T(8,128)(2,1)S(1)}, bf16[320,2048]{1,0:T(8,128)(2,1)}, u32[]{:S(2)}, u32[]{:S(2)}) collective-permute-start(bf16[320,2048]{1,0:T(8,128)(2,1)S(1)} %convolution_convert_fusion.1), channel_id=1, source_target_pairs={{0,16},{16,64},{32,240},{48,32},{64,80},{80,128},{96,48},{112,96},... | collective-permute-start | bytes 3932168 | tf_op jit(solution)/shard_map/ppermute | solution.py:402
  50.1 5.8 %collective-permute-start.16 = (bf16[1,2,2,96,256]{4,3,2,1,0:T(8,128)(2,1)S(1)}, bf16[1,2,2,96,256]{4,3,2,1,0:T(8,128)(2,1)S(1)}, u32[]{:S(2)}, u32[]{:S(2)}) collective-permute-start(bf16[1,2,2,96,256]{4,3,2,1,0:T(8,128)(2,1)S(1)} %maximum_bitcast_fusion.1), channel_id=1, source_target_pairs={{0,4},{4,0},{8,12},{12,8},{32,44},{36,40},{40,36},{44,32},{1,5},{5... | collective-permute-start | bytes 589832 | tf_op jit(solution)/shard_map/ppermute | solution.py:407
  51.8 7.2 %collective-permute-start.11 = (bf16[1,2,2,96,256]{4,3,2,1,0:T(8,128)(2,1)S(1)}, bf16[1,2,2,96,256]{4,3,2,1,0:T(8,128)(2,1)S(1)}, u32[]{:S(2)}, u32[]{:S(2)}) collective-permute-start(bf16[1,2,2,96,256]{4,3,2,1,0:T(8,128)(2,1)S(1)} %maximum_bitcast_fusion), channel_id=1, source_target_pairs={{0,1},{1,0},{2,3},{3,2},{32,35},{33,34},{34,33},{35,32},{4,5},{5,4... | collective-permute-start | bytes 589832 | tf_op jit(solution)/shard_map/ppermute | solution.py:407
  55.9 9.1 %collective-permute-start.17 = (bf16[2,2,2,96,256]{4,3,2,1,0:T(8,128)(2,1)S(1)}, bf16[2,2,2,96,256]{4,3,2,1,0:T(8,128)(2,1)S(1)}, u32[]{:S(2)}, u32[]{:S(2)}) collective-permute-start(bf16[2,2,2,96,256]{4,3,2,1,0:T(8,128)(2,1)S(1)} %pad_maximum_fusion.3), channel_id=1, source_target_pairs={{0,12},{4,8},{8,4},{12,0},{32,36},{36,32},{40,44},{44,40},{1,13},{... | collective-permute-start | bytes 1179656 | tf_op jit(solution)/shard_map/ppermute | solution.py:407
  59.1 11.6 %collective-permute-start.12 = (bf16[2,2,2,96,256]{4,3,2,1,0:T(8,128)(2,1)S(1)}, bf16[2,2,2,96,256]{4,3,2,1,0:T(8,128)(2,1)S(1)}, u32[]{:S(2)}, u32[]{:S(2)}) collective-permute-start(bf16[2,2,2,96,256]{4,3,2,1,0:T(8,128)(2,1)S(1)} %pad_maximum_fusion.2), channel_id=1, source_target_pairs={{0,3},{1,2},{2,1},{3,0},{32,33},{33,32},{34,35},{35,34},{4,7},{5,6... | collective-permute-start | bytes 1179656 | tf_op jit(solution)/shard_map/ppermute | solution.py:407
  65.1 14.9 %collective-permute-start.18 = (bf16[4,2,2,96,256]{4,3,2,1,0:T(8,128)(2,1)S(1)}, bf16[4,2,2,96,256]{4,3,2,1,0:T(8,128)(2,1)}, u32[]{:S(2)}, u32[]{:S(2)}) collective-permute-start(bf16[4,2,2,96,256]{4,3,2,1,0:T(8,128)(2,1)S(1)} %pad_maximum_fusion.1.refs_6_.refs_4_), channel_id=1, source_target_pairs={{0,1},{1,0},{2,3},{3,2},{32,35},{33,34},{34,33},{35,32},{4,5},{5,4... | collective-permute-start | bytes 2359304 | tf_op jit(solution)/shard_map/ppermute | solution.py:407
  71.7 20.7 %collective-permute-start.13 = (bf16[4,2,2,96,256]{4,3,2,1,0:T(8,128)(2,1)}, bf16[4,2,2,96,256]{4,3,2,1,0:T(8,128)(2,1)}, u32[]{:S(2)}, u32[]{:S(2)}) collective-permute-start(bf16[4,2,2,96,256]{4,3,2,1,0:T(8,128)(2,1)} %pad_maximum_fusion.refs_2_.refs_0_), channel_id=1, source_target_pairs={{0,4},{4,0},{8,12},{12,8},{32,44},{36,40},{40,36},{44,32},{1,5},{5... | collective-permute-start | bytes 2359304 | tf_op jit(solution)/shard_map/ppermute | solution.py:407
  71.7 34.2 %collective-permute-start.10 = (bf16[320,2048]{1,0:T(8,128)(2,1)}, bf16[320,2048]{1,0:T(8,128)(2,1)}, u32[]{:S(2)}, u32[]{:S(2)}) collective-permute-start(bf16[320,2048]{1,0:T(8,128)(2,1)} %collective-permute-done.9.refs_1_), channel_id=1, source_target_pairs={{0,32},{32,0},{1,33},{33,1},{2,34},{34,2},{3,35},{35,3},{4,36},{36... | collective-permute-start | bytes 3932168 | tf_op jit(solution)/shard_map/ppermute | solution.py:416
  71.8 21.4 %collective-permute-start.19 = (bf16[4,2,2,96,256]{4,3,2,1,0:T(8,128)(2,1)S(1)}, bf16[4,2,2,96,256]{4,3,2,1,0:T(8,128)(2,1)}, u32[]{:S(2)}, u32[]{:S(2)}) collective-permute-start(bf16[4,2,2,96,256]{4,3,2,1,0:T(8,128)(2,1)S(1)} %pad_maximum_fusion.1.refs_6_.refs_4_), channel_id=1, source_target_pairs={{0,3},{1,2},{2,1},{3,0},{32,33},{33,32},{34,35},{35,34},{4,7},{5,6... | collective-permute-start | bytes 2359304 | tf_op jit(solution)/shard_map/ppermute | solution.py:407
  74.6 18.6 %collective-permute-start.14 = (bf16[4,2,2,96,256]{4,3,2,1,0:T(8,128)(2,1)}, bf16[4,2,2,96,256]{4,3,2,1,0:T(8,128)(2,1)}, u32[]{:S(2)}, u32[]{:S(2)}) collective-permute-start(bf16[4,2,2,96,256]{4,3,2,1,0:T(8,128)(2,1)} %pad_maximum_fusion.refs_2_.refs_0_), channel_id=1, source_target_pairs={{0,12},{4,8},{8,4},{12,0},{32,36},{36,32},{40,44},{44,40},{1,13},{... | collective-permute-start | bytes 2359304 | tf_op jit(solution)/shard_map/ppermute | solution.py:407
  80.0 13.7 %collective-permute-start.20 = (bf16[4,2,2,96,256]{4,3,2,1,0:T(8,128)(2,1)}, bf16[4,2,2,96,256]{4,3,2,1,0:T(8,128)(2,1)}, u32[]{:S(2)}, u32[]{:S(2)}) collective-permute-start(bf16[4,2,2,96,256]{4,3,2,1,0:T(8,128)(2,1)} %collective-permute-done.18.refs_7_.refs_5_), channel_id=1, source_target_pairs={{0,3},{1,2},{2,1},{3,0},{32,33},{33,32},{34,35},{35,34},{4,7},{5,6... | collective-permute-start | bytes 2359304 | tf_op jit(solution)/shard_map/ppermute | solution.py:407
  92.4 13.5 %collective-permute-start.15 = (bf16[4,2,2,96,256]{4,3,2,1,0:T(8,128)(2,1)}, bf16[4,2,2,96,256]{4,3,2,1,0:T(8,128)(2,1)}, u32[]{:S(2)}, u32[]{:S(2)}) collective-permute-start(bf16[4,2,2,96,256]{4,3,2,1,0:T(8,128)(2,1)} %collective-permute-done.13.refs_3_.refs_1_), channel_id=1, source_target_pairs={{0,12},{4,8},{8,4},{12,0},{32,36},{36,32},{40,44},{44,40},{1,13},{... | collective-permute-start | bytes 2359304 | tf_op jit(solution)/shard_map/ppermute | solution.py:407
  93.2 19.5 %copy-start.2 = (bf16[320,2048]{1,0:T(8,128)(2,1)S(1)}, bf16[320,2048]{1,0:T(8,128)(2,1)}, u32[]{:S(2)}) copy-start(bf16[320,2048]{1,0:T(8,128)(2,1)} %copy-done.1) | copy-start | bytes 3932164
  93.2 19.5 %copy-start.4 = (bf16[320,2048]{1,0:T(8,128)(2,1)S(1)}, bf16[320,2048]{1,0:T(8,128)(2,1)}, u32[]{:S(2)}) copy-start(bf16[320,2048]{1,0:T(8,128)(2,1)} %copy-done.3) | copy-start | bytes 3932164
  112.1 7.0 %collective-permute-start.21 = (bf16[320,512]{1,0:T(8,128)(2,1)S(1)}, bf16[320,512]{1,0:T(8,128)(2,1)S(1)}, u32[]{:S(2)}, u32[]{:S(2)}) collective-permute-start(bf16[320,512]{1,0:T(8,128)(2,1)S(1)} %get-tuple-element.77), channel_id=1, source_target_pairs={{0,32},{32,0},{1,33},{33,1},{2,34},{34,2},{3,35},{35,3},{4,36},{36... | collective-permute-start | bytes 983048 | tf_op jit(solution)/shard_map/ppermute | solution.py:419
  112.2 6.9 %collective-permute-start.22 = (bf16[320,512]{1,0:T(8,128)(2,1)S(1)}, bf16[320,512]{1,0:T(8,128)(2,1)S(1)}, u32[]{:S(2)}, u32[]{:S(2)}) collective-permute-start(bf16[320,512]{1,0:T(8,128)(2,1)S(1)} %get-tuple-element.78), channel_id=1, source_target_pairs={{0,32},{32,0},{1,33},{33,1},{2,34},{34,2},{3,35},{35,3},{4,36},{36... | collective-permute-start | bytes 983048 | tf_op jit(solution)/shard_map/ppermute | solution.py:419
  118.5 4.5 %collective-permute-start.23 = (bf16[320,512]{1,0:T(8,128)(2,1)S(1)}, bf16[320,512]{1,0:T(8,128)(2,1)S(1)}, u32[]{:S(2)}, u32[]{:S(2)}) collective-permute-start(bf16[320,512]{1,0:T(8,128)(2,1)S(1)} %get-tuple-element.85), channel_id=1, source_target_pairs={{0,32},{32,0},{1,33},{33,1},{2,34},{34,2},{3,35},{35,3},{4,36},{36... | collective-permute-start | bytes 983048 | tf_op jit(solution)/shard_map/ppermute | solution.py:419
  118.7 4.3 %collective-permute-start.24 = (bf16[320,512]{1,0:T(8,128)(2,1)S(1)}, bf16[320,512]{1,0:T(8,128)(2,1)S(1)}, u32[]{:S(2)}, u32[]{:S(2)}) collective-permute-start(bf16[320,512]{1,0:T(8,128)(2,1)S(1)} %get-tuple-element.86), channel_id=1, source_target_pairs={{0,32},{32,0},{1,33},{33,1},{2,34},{34,2},{3,35},{35,3},{4,36},{36... | collective-permute-start | bytes 983048 | tf_op jit(solution)/shard_map/ppermute | solution.py:419
  123.0 17.4 %collective-permute-start.25 = (bf16[320,1024]{1,0:T(8,128)(2,1)S(1)}, bf16[320,1024]{1,0:T(8,128)(2,1)S(1)}, u32[]{:S(2)}, u32[]{:S(2)}) collective-permute-start(bf16[320,1024]{1,0:T(8,128)(2,1)S(1)} %get-tuple-element.87), channel_id=1, source_target_pairs={{0,208},{16,0},{32,48},{48,96},{64,16},{80,64},{96,112},{112,160},... | collective-permute-start | bytes 1966088 | tf_op jit(solution)/shard_map/ppermute | solution.py:430
  123.3 17.1 %collective-permute-start.30 = (bf16[320,1024]{1,0:T(8,128)(2,1)S(1)}, bf16[320,1024]{1,0:T(8,128)(2,1)S(1)}, u32[]{:S(2)}, u32[]{:S(2)}) collective-permute-start(bf16[320,1024]{1,0:T(8,128)(2,1)S(1)} %get-tuple-element.96), channel_id=1, source_target_pairs={{32,208},{48,0},{0,48},{16,96},{96,16},{112,64},{64,112},{80,160},... | collective-permute-start | bytes 1966088 | tf_op jit(solution)/shard_map/ppermute | solution.py:431
  123.8 6.8 %copy-start.10 = (f32[512]{0:T(512)S(1)}, f32[512]{0:T(512)}, u32[]{:S(2)}) copy-start(f32[512]{0:T(512)} %param.22) | copy-start | bytes 6148
  127.7 1.5 %collective-permute-start.26 = (bf16[80,1024]{1,0:T(8,128)(2,1)S(1)}, bf16[80,1024]{1,0:T(8,128)(2,1)S(1)}, u32[]{:S(2)}, u32[]{:S(2)}) collective-permute-start(bf16[80,1024]{1,0:T(8,128)(2,1)S(1)} %get-tuple-element.92), channel_id=1, source_target_pairs={{0,32},{32,0},{1,33},{33,1},{2,34},{34,2},{3,35},{35,3},{4,36},{36... | collective-permute-start | bytes 491528 | tf_op jit(solution)/shard_map/ppermute | solution.py:419
  127.9 1.6 %collective-permute-start.27 = (bf16[80,1024]{1,0:T(8,128)(2,1)S(1)}, bf16[80,1024]{1,0:T(8,128)(2,1)S(1)}, u32[]{:S(2)}, u32[]{:S(2)}) collective-permute-start(bf16[80,1024]{1,0:T(8,128)(2,1)S(1)} %get-tuple-element.93), channel_id=1, source_target_pairs={{0,32},{32,0},{1,33},{33,1},{2,34},{34,2},{3,35},{35,3},{4,36},{36... | collective-permute-start | bytes 491528 | tf_op jit(solution)/shard_map/ppermute | solution.py:419
  128.5 1.4 collective-permute-start.28
  129.2 1.4 collective-permute-start.29

commit v3 on v2

--- a/solution.py
+++ b/solution.py
@@ -327,24 +327,26 @@
         (same[...], core),
         (cross[0] if len(cross) == 1 else jnp.concatenate(cross), 1 - core),
     ):
-        at = pl.ds(pl.multiple_of(side * COLS, COLS), COLS)
         rows = (dot(put[...], values) * scale[...]).astype(BF16)
-        out[:, at] = rows + refs[0][:, at] if before else rows
+        for group in range(2):
+            at = pl.ds(pl.multiple_of((group * CORE + side) * COLS, COLS), COLS)
+            part = rows[:, group * COLS : (group + 1) * COLS]
+            out[:, at] = part + refs[0][:, at] if before else part
 
 
 def put_call(table, put, gains, same, cross, *before):
     rows = put.shape[0]
-    part = pl.BlockSpec((CAP // len(cross), COLS), lambda i, s: (0, i))
-    block = pl.BlockSpec((rows, 2 * COLS), lambda i, s: (0, i))
+    part = pl.BlockSpec((CAP // len(cross), 2 * COLS), lambda i, s: (0, i))
+    block = pl.BlockSpec((rows, 4 * COLS), lambda i, s: (0, i))
     return pl.pallas_call(
         functools.partial(put_kernel, len(before)),
         grid_spec=pltpu.PrefetchScalarGridSpec(
             num_scalar_prefetch=1,
-            grid=(ZH,),
+            grid=(ZH // 2,),
             in_specs=[
                 pl.BlockSpec((rows, CAP), lambda i, s: (0, 0)),
                 pl.BlockSpec((1, rows), lambda i, s: (0, 0)),
-                pl.BlockSpec((CAP, COLS), lambda i, s: (0, i)),
+                pl.BlockSpec((CAP, 2 * COLS), lambda i, s: (0, i)),
             ]
             + [block] * len(before)
             + [part] * len(cross),
@@ -352,7 +354,7 @@
             scratch_shapes=[pltpu.VMEM((rows, 1), F32)],
         ),
         out_shape=jax.ShapeDtypeStruct((rows, D), BF16),
-        compiler_params=params(16),
+        compiler_params=params(20),
         cost_estimate=LARGE if before else SMALL,
         name="put",
     )(table, put, gains, same, *before, *cross)
@@ -389,6 +391,7 @@
     put_own, put_got = [(r[:, None] == slots[None, :]).astype(BF16) for r in rank_of]
     tokens_own = dot(pick_own, tokens).astype(BF16)
     tokens_sent = dot(pick_got, tokens).astype(BF16)
+    tokens_own, given = lax.optimization_barrier((tokens_own, given))
     other_own = lax.ppermute(tokens_own, "core", shift(CORE, 1))
 
     taken = lax.ppermute(given, "zl", shift(ZL, 1))

time: 145 us -> 144 us (level)
  transfers between devices with their start and end apart: 31 -> 31, of which waited for: 19 -> 18; matrix products, arithmetic and copies ran while one was open for 2% -> 3% of each run, Pallas kernels for 13% -> 11%
where the time goes in v3:
time: 144 us; the launch traced here: 143 us
  waiting for transfers between devices  56.7 us (39%)
  starting transfers between devices  47.4 us (33%)
  Pallas kernels  31.2 us (22%)
  other arithmetic  2.9 us (2%)
  local copies, waits for them, and re-layouts  2.23 us (2%)
  matrix products  1.69 us (1%)
    ppermute x10, waiting for transfers between devices, exchange(): lax.ppermute(a, ('core', axis), flip_pairs(turn))  36.2 us
    ppermute x10, starting transfers between devices, exchange(): lax.ppermute(a, ('core', axis), flip_pairs(turn))  17 us
    pallas_call x2, Pallas kernels, hidden_call(): pl.pallas_call(functools.partial(hidden_kernel, parts), in_specs=[pl.Bloc...  11.9 us
    ppermute x3, starting transfers between devices, body(): lax.ppermute(sent[s - 1], 'zh', shift(ZH, s))  10.5 us
    ppermute x3, starting transfers between devices, body(): lax.ppermute(both, 'zh', shift(ZH, s))  8.46 us
    pallas_call x2, Pallas kernels, outcome_call(): pl.pallas_call(outcome_kernel, in_specs=[pl.BlockSpec(memory_space=pltpu....  7.75 us
    pallas_call x2, Pallas kernels, put_call(): pl.pallas_call(functools.partial(put_kernel, len(before)), grid_spec=pltp...  6.09 us
    ppermute x1, waiting for transfers between devices, body(): back_same = lax.ppermute(far_mine, COLUMN, column_pairs(-1, 0))  5.98 us
  transfers between devices with their start and end apart: 31, of which 18 were waited for; matrix products, arithmetic and copies ran while one was open for 3% of the time, Pallas kernels for 11%

profile of v3, /device:TPU:32, one launch (start us, length us, event | category | flops | bytes accessed | tf_op | source)
XLA Modules:
  0.0 143.1 jit_solution(981114727848016115)
XLA Ops:
  0.7 0.7 pad_add_fusion.place
  1.3 3.8 %give.1 = (bf16[4,2,96,256]{3,2,1,0:T(8,128)(2,1)}, bf16[4,2,96,256]{3,2,1,0:T(8,128)(2,1)}, f32[2,64,256]{2,1,0:T(8,128)}, f32[2,32,256]{2,1,0:T(8,128)}, f32[2,64,256]{2,1,0:T(8,128)}, /*index=5*/f32[2,32,256]{2,1,0:T(8,128)}) custom-call(s32[4]{0:T(128)} %pad_add_fusion.place, f32[2,64,2048]{2,1,0:T(8,128)} %b_in.1, bf16[1,2,64,2048]{3,2,1,0:T(8,128)(2,1)} %l_in.1, ...), custom_call_target="tpu_custom_call" | custom-call | flops 1000000 | bytes 4194304 | tf_op jit(solution)/shard_map/give/pallas_call | solution.py:120
  5.3 1.9 %collective-permute-done.taken = bf16[4,2,96,256]{3,2,1,0:T(8,128)(2,1)S(1)} collective-permute-done((bf16[4,2,96,256]{3,2,1,0:T(8,128)(2,1)}, bf16[4,2,96,256]{3,2,1,0:T(8,128)(2,1)S(1)}, u32[]{:S(2)}, u32[]{:S(2)}) %collective-permute-start) | collective-permute-done | bytes 393248 | tf_op jit(solution)/shard_map/ppermute | solution.py:376
  7.2 1.0 copy-done.5
  9.4 3.3 %collective-permute-start.1 = (bf16[2,96,256]{2,1,0:T(8,128)(2,1)S(1)}, bf16[2,96,256]{2,1,0:T(8,128)(2,1)S(1)}, u32[]{:S(2)}, u32[]{:S(2)}) collective-permute-start(bf16[2,96,256]{2,1,0:T(8,128)(2,1)S(1)} %get-tuple-element.56), channel_id=1, source_target_pairs={{0,64},{64,128},{128,192},{192,0},{1,65},{65,129},{129,193},{193,1... | collective-permute-start | bytes 294920 | tf_op jit(solution)/shard_map/ppermute | solution.py:377
  12.7 4.5 %collective-permute-start.2 = (bf16[2,96,256]{2,1,0:T(8,128)(2,1)S(1)}, bf16[2,96,256]{2,1,0:T(8,128)(2,1)S(1)}, u32[]{:S(2)}, u32[]{:S(2)}) collective-permute-start(bf16[2,96,256]{2,1,0:T(8,128)(2,1)S(1)} %get-tuple-element.57), channel_id=1, source_target_pairs={{0,128},{64,192},{128,0},{192,64},{1,129},{65,193},{129,1},{193,65... | collective-permute-start | bytes 294920 | tf_op jit(solution)/shard_map/ppermute | solution.py:377
  17.2 2.7 %collective-permute-start.3 = (bf16[2,96,256]{2,1,0:T(8,128)(2,1)S(1)}, bf16[2,96,256]{2,1,0:T(8,128)(2,1)S(1)}, u32[]{:S(2)}, u32[]{:S(2)}) collective-permute-start(bf16[2,96,256]{2,1,0:T(8,128)(2,1)S(1)} %get-tuple-element.58), channel_id=1, source_target_pairs={{0,192},{64,0},{128,64},{192,128},{1,193},{65,1},{129,65},{193,129... | collective-permute-start | bytes 294920 | tf_op jit(solution)/shard_map/ppermute | solution.py:377
  20.0 0.8 convolution_convert_fusion.1.refs_1_
  20.9 0.5 collective-permute-done.2.r2
  21.4 3.6 %collective-permute-done.3.r3 = bf16[2,96,256]{2,1,0:T(8,128)(2,1)S(1)} collective-permute-done((bf16[2,96,256]{2,1,0:T(8,128)(2,1)S(1)}, bf16[2,96,256]{2,1,0:T(8,128)(2,1)S(1)}, u32[]{:S(2)}, u32[]{:S(2)}) %collective-permute-start.3) | collective-permute-done | bytes 98336 | tf_op jit(solution)/shard_map/ppermute | solution.py:377
  25.0 1.5 %step.1 = (f32[2,64,256]{2,1,0:T(8,128)}, f32[2,32,256]{2,1,0:T(8,128)}, f32[2,64,256]{2,1,0:T(8,128)}, f32[2,32,256]{2,1,0:T(8,128)}, bf16[96,256]{1,0:T(8,128)(2,1)S(1)}, /*index=5*/bf16[96,256]{1,0:T(8,128)(2,1)S(1)}) custom-call(s32[4]{0:T(128)S(1)} %copy-done.11, f32[2,96,256]{2,1,0:T(8,128)S(1)} %get-tuple-element.55.own, ...), custom_call_target="tpu_custom_call" | custom-call | flops 1000000 | bytes 2097152 | tf_op jit(solution)/shard_map/step/pallas_call | solution.py:177
  26.5 3.0 %collective-permute-start.4 = (bf16[96,256]{1,0:T(8,128)(2,1)S(1)}, bf16[96,256]{1,0:T(8,128)(2,1)S(1)}, u32[]{:S(2)}, u32[]{:S(2)}) collective-permute-start(bf16[96,256]{1,0:T(8,128)(2,1)S(1)} %get-tuple-element.70), channel_id=1, source_target_pairs={{0,16},{16,0},{1,17},{17,1},{2,18},{18,2},{3,19},{19,3},{4,20},{20... | collective-permute-start | bytes 147464 | tf_op jit(solution)/shard_map/ppermute | solution.py:397
  29.5 0.8 convolution_convert_fusion
  30.4 1.5 %collective-permute-done.4 = bf16[96,256]{1,0:T(8,128)(2,1)S(1)} collective-permute-done((bf16[96,256]{1,0:T(8,128)(2,1)S(1)}, bf16[96,256]{1,0:T(8,128)(2,1)S(1)}, u32[]{:S(2)}, u32[]{:S(2)}) %collective-permute-start.4) | collective-permute-done | bytes 49184 | tf_op jit(solution)/shard_map/ppermute | solution.py:397
  31.9 2.5 %collective-permute-start.6 = (bf16[2,96,256]{2,1,0:T(8,128)(2,1)S(1)}, bf16[2,96,256]{2,1,0:T(8,128)(2,1)S(1)}, u32[]{:S(2)}, u32[]{:S(2)}) collective-permute-start(bf16[2,96,256]{2,1,0:T(8,128)(2,1)S(1)} %pad_maximum_fusion.4), channel_id=1, source_target_pairs={{0,64},{64,128},{128,192},{192,0},{1,65},{65,129},{129,193},{193,1... | collective-permute-start | bytes 294920 | tf_op jit(solution)/shard_map/ppermute | solution.py:402
  34.5 3.5 %collective-permute-start.7 = (bf16[2,96,256]{2,1,0:T(8,128)(2,1)S(1)}, bf16[2,96,256]{2,1,0:T(8,128)(2,1)S(1)}, u32[]{:S(2)}, u32[]{:S(2)}) collective-permute-start(bf16[2,96,256]{2,1,0:T(8,128)(2,1)S(1)} %pad_maximum_fusion.4), channel_id=1, source_target_pairs={{0,128},{64,192},{128,0},{192,64},{1,129},{65,193},{129,1},{193,65... | collective-permute-start | bytes 294920 | tf_op jit(solution)/shard_map/ppermute | solution.py:402
  38.0 2.4 %collective-permute-start.8 = (bf16[2,96,256]{2,1,0:T(8,128)(2,1)S(1)}, bf16[2,96,256]{2,1,0:T(8,128)(2,1)S(1)}, u32[]{:S(2)}, u32[]{:S(2)}) collective-permute-start(bf16[2,96,256]{2,1,0:T(8,128)(2,1)S(1)} %pad_maximum_fusion.4), channel_id=1, source_target_pairs={{0,192},{64,0},{128,64},{192,128},{1,193},{65,1},{129,65},{193,129... | collective-permute-start | bytes 294920 | tf_op jit(solution)/shard_map/ppermute | solution.py:402
  40.7 5.1 %collective-permute-done.7 = bf16[2,96,256]{2,1,0:T(8,128)(2,1)S(1)} collective-permute-done((bf16[2,96,256]{2,1,0:T(8,128)(2,1)S(1)}, bf16[2,96,256]{2,1,0:T(8,128)(2,1)S(1)}, u32[]{:S(2)}, u32[]{:S(2)}) %collective-permute-start.7) | collective-permute-done | bytes 98336 | tf_op jit(solution)/shard_map/ppermute | solution.py:402
  45.8 4.1 %collective-permute-start.9 = (bf16[320,2048]{1,0:T(8,128)(2,1)S(1)}, bf16[320,2048]{1,0:T(8,128)(2,1)}, u32[]{:S(2)}, u32[]{:S(2)}) collective-permute-start(bf16[320,2048]{1,0:T(8,128)(2,1)S(1)} %convolution_convert_fusion), channel_id=1, source_target_pairs={{0,16},{16,64},{32,240},{48,32},{64,80},{80,128},{96,48},{112,96},... | collective-permute-start | bytes 3932168 | tf_op jit(solution)/shard_map/ppermute | solution.py:405
  49.9 1.7 %collective-permute-start.16 = (bf16[1,2,2,96,256]{4,3,2,1,0:T(8,128)(2,1)S(1)}, bf16[1,2,2,96,256]{4,3,2,1,0:T(8,128)(2,1)S(1)}, u32[]{:S(2)}, u32[]{:S(2)}) collective-permute-start(bf16[1,2,2,96,256]{4,3,2,1,0:T(8,128)(2,1)S(1)} %maximum_bitcast_fusion.1), channel_id=1, source_target_pairs={{0,4},{4,0},{8,12},{12,8},{32,44},{36,40},{40,36},{44,32},{1,5},{5... | collective-permute-start | bytes 589832 | tf_op jit(solution)/shard_map/ppermute | solution.py:410
  51.6 1.6 %collective-permute-start.11 = (bf16[1,2,2,96,256]{4,3,2,1,0:T(8,128)(2,1)S(1)}, bf16[1,2,2,96,256]{4,3,2,1,0:T(8,128)(2,1)S(1)}, u32[]{:S(2)}, u32[]{:S(2)}) collective-permute-start(bf16[1,2,2,96,256]{4,3,2,1,0:T(8,128)(2,1)S(1)} %maximum_bitcast_fusion), channel_id=1, source_target_pairs={{0,1},{1,0},{2,3},{3,2},{32,35},{33,34},{34,33},{35,32},{4,5},{5,4... | collective-permute-start | bytes 589832 | tf_op jit(solution)/shard_map/ppermute | solution.py:410
  53.2 2.5 %collective-permute-done.16 = bf16[1,2,2,96,256]{4,3,2,1,0:T(8,128)(2,1)S(1)} collective-permute-done((bf16[1,2,2,96,256]{4,3,2,1,0:T(8,128)(2,1)S(1)}, bf16[1,2,2,96,256]{4,3,2,1,0:T(8,128)(2,1)S(1)}, u32[]{:S(2)}, u32[]{:S(2)}) %collective-permute-start.16) | collective-permute-done | bytes 196640 | tf_op jit(solution)/shard_map/ppermute | solution.py:410
  55.7 3.1 %collective-permute-start.17 = (bf16[2,2,2,96,256]{4,3,2,1,0:T(8,128)(2,1)S(1)}, bf16[2,2,2,96,256]{4,3,2,1,0:T(8,128)(2,1)S(1)}, u32[]{:S(2)}, u32[]{:S(2)}) collective-permute-start(bf16[2,2,2,96,256]{4,3,2,1,0:T(8,128)(2,1)S(1)} %pad_maximum_fusion.3), channel_id=1, source_target_pairs={{0,12},{4,8},{8,4},{12,0},{32,36},{36,32},{40,44},{44,40},{1,13},{... | collective-permute-start | bytes 1179656 | tf_op jit(solution)/shard_map/ppermute | solution.py:410
  58.8 2.8 %collective-permute-start.12 = (bf16[2,2,2,96,256]{4,3,2,1,0:T(8,128)(2,1)S(1)}, bf16[2,2,2,96,256]{4,3,2,1,0:T(8,128)(2,1)S(1)}, u32[]{:S(2)}, u32[]{:S(2)}) collective-permute-start(bf16[2,2,2,96,256]{4,3,2,1,0:T(8,128)(2,1)S(1)} %pad_maximum_fusion.2), channel_id=1, source_target_pairs={{0,3},{1,2},{2,1},{3,0},{32,33},{33,32},{34,35},{35,34},{4,7},{5,6... | collective-permute-start | bytes 1179656 | tf_op jit(solution)/shard_map/ppermute | solution.py:410
  61.7 3.1 %collective-permute-done.17 = bf16[2,2,2,96,256]{4,3,2,1,0:T(8,128)(2,1)S(1)} collective-permute-done((bf16[2,2,2,96,256]{4,3,2,1,0:T(8,128)(2,1)S(1)}, bf16[2,2,2,96,256]{4,3,2,1,0:T(8,128)(2,1)S(1)}, u32[]{:S(2)}, u32[]{:S(2)}) %collective-permute-start.17) | collective-permute-done | bytes 393248 | tf_op jit(solution)/shard_map/ppermute | solution.py:410
  64.9 1.8 %collective-permute-start.18 = (bf16[4,2,2,96,256]{4,3,2,1,0:T(8,128)(2,1)S(1)}, bf16[4,2,2,96,256]{4,3,2,1,0:T(8,128)(2,1)}, u32[]{:S(2)}, u32[]{:S(2)}) collective-permute-start(bf16[4,2,2,96,256]{4,3,2,1,0:T(8,128)(2,1)S(1)} %pad_maximum_fusion.1.refs_6_.refs_4_), channel_id=1, source_target_pairs={{0,1},{1,0},{2,3},{3,2},{32,35},{33,34},{34,33},{35,32},{4,5},{5,4... | collective-permute-start | bytes 2359304 | tf_op jit(solution)/shard_map/ppermute | solution.py:410
  66.6 3.3 %collective-permute-done.12 = bf16[2,2,2,96,256]{4,3,2,1,0:T(8,128)(2,1)S(1)} collective-permute-done((bf16[2,2,2,96,256]{4,3,2,1,0:T(8,128)(2,1)S(1)}, bf16[2,2,2,96,256]{4,3,2,1,0:T(8,128)(2,1)S(1)}, u32[]{:S(2)}, u32[]{:S(2)}) %collective-permute-start.12) | collective-permute-done | bytes 393248 | tf_op jit(solution)/shard_map/ppermute | solution.py:410
  69.9 1.0 pad_maximum_fusion.refs_2_.refs_0_
  71.0 2.8 %collective-permute-start.19 = (bf16[4,2,2,96,256]{4,3,2,1,0:T(8,128)(2,1)S(1)}, bf16[4,2,2,96,256]{4,3,2,1,0:T(8,128)(2,1)}, u32[]{:S(2)}, u32[]{:S(2)}) collective-permute-start(bf16[4,2,2,96,256]{4,3,2,1,0:T(8,128)(2,1)S(1)} %pad_maximum_fusion.1.refs_6_.refs_4_), channel_id=1, source_target_pairs={{0,3},{1,2},{2,1},{3,0},{32,33},{33,32},{34,35},{35,34},{4,7},{5,6... | collective-permute-start | bytes 2359304 | tf_op jit(solution)/shard_map/ppermute | solution.py:410
  73.9 0.6 collective-permute-start.14
  74.5 5.8 %collective-permute-done.18.refs_7_.refs_5_ = bf16[4,2,2,96,256]{4,3,2,1,0:T(8,128)(2,1)} collective-permute-done((bf16[4,2,2,96,256]{4,3,2,1,0:T(8,128)(2,1)S(1)}, bf16[4,2,2,96,256]{4,3,2,1,0:T(8,128)(2,1)}, u32[]{:S(2)}, u32[]{:S(2)}) %collective-permute-start.18) | collective-permute-done | bytes 786464 | tf_op jit(solution)/shard_map/ppermute | solution.py:410
  80.3 2.6 %collective-permute-start.20 = (bf16[4,2,2,96,256]{4,3,2,1,0:T(8,128)(2,1)}, bf16[4,2,2,96,256]{4,3,2,1,0:T(8,128)(2,1)}, u32[]{:S(2)}, u32[]{:S(2)}) collective-permute-start(bf16[4,2,2,96,256]{4,3,2,1,0:T(8,128)(2,1)} %collective-permute-done.18.refs_7_.refs_5_), channel_id=1, source_target_pairs={{0,3},{1,2},{2,1},{3,0},{32,33},{33,32},{34,35},{35,34},{4,7},{5,6... | collective-permute-start | bytes 2359304 | tf_op jit(solution)/shard_map/ppermute | solution.py:410
  82.9 8.7 %collective-permute-done.13.refs_3_.refs_1_ = bf16[4,2,2,96,256]{4,3,2,1,0:T(8,128)(2,1)} collective-permute-done((bf16[4,2,2,96,256]{4,3,2,1,0:T(8,128)(2,1)}, bf16[4,2,2,96,256]{4,3,2,1,0:T(8,128)(2,1)}, u32[]{:S(2)}, u32[]{:S(2)}) %collective-permute-start.13) | collective-permute-done | bytes 786464 | tf_op jit(solution)/shard_map/ppermute | solution.py:410
  91.6 0.7 dynamic-slice_bitcast_fusion
  92.4 1.3 collective-permute-done.20.refs_9_.refs_7_
  93.8 11.4 %collective-permute-done.15.refs_5_.refs_3_ = bf16[4,2,2,96,256]{4,3,2,1,0:T(8,128)(2,1)} collective-permute-done((bf16[4,2,2,96,256]{4,3,2,1,0:T(8,128)(2,1)}, bf16[4,2,2,96,256]{4,3,2,1,0:T(8,128)(2,1)}, u32[]{:S(2)}, u32[]{:S(2)}) %collective-permute-start.15) | collective-permute-done | bytes 786464 | tf_op jit(solution)/shard_map/ppermute | solution.py:410
  105.2 6.1 %hidden.2 = (bf16[640,512]{1,0:T(8,128)(2,1)S(1)}, bf16[320,512]{1,0:T(8,128)(2,1)S(1)}, bf16[320,512]{1,0:T(8,128)(2,1)S(1)}) custom-call(s32[36]{0:T(128)S(1)} %concatenate.18.table, bf16[320,2048]{1,0:T(8,128)(2,1)} %collective-permute-done.10.refs_0_, bf16[320,2048]{1,0:T(8,128)(2,1)} %collective-permute-done.9.refs_1_, ...), custom_call_target="tpu_custom_call" | custom-call | flops 1000 | bytes 1000 | tf_op jit(solution)/shard_map/hidden/pallas_call | solution.py:251
  111.4 0.5 collective-permute-start.22
  111.9 5.8 %hidden.3 = (bf16[640,512]{1,0:T(8,128)(2,1)S(1)}, bf16[320,512]{1,0:T(8,128)(2,1)S(1)}, bf16[320,512]{1,0:T(8,128)(2,1)S(1)}) custom-call(s32[36]{0:T(128)S(1)} %concatenate.18.table, bf16[320,2048]{1,0:T(8,128)(2,1)S(1)} %copy-done.4, bf16[320,2048]{1,0:T(8,128)(2,1)S(1)} %copy-done.2, bf16[4,2,2,96,256]{4,3,2,1,0:T(8,128)(2,1)} %pad_maximum_fusion.refs_2_.refs_0_, ...), custom_call_target="tpu_custom_call" | custom-call | flops 1000 | bytes 1000 | tf_op jit(solution)/shard_map/hidden/pallas_call | solution.py:251
  118.3 3.9 %outcome.2 = (bf16[320,1024]{1,0:T(8,128)(2,1)S(1)}, bf16[320,1024]{1,0:T(8,128)(2,1)S(1)}) custom-call(s32[36]{0:T(128)S(1)} %concatenate.18.table, bf16[640,512]{1,0:T(8,128)(2,1)S(1)} %get-tuple-element.80.made, bf16[320,512]{1,0:T(8,128)(2,1)S(1)} %collective-permute-done.21.got0, bf16[320,512]{1,0:T(8,128)(2,1)S(1)} %collective-permute-done.22.got1, ...), custom_call_target="tpu_custom_call" | custom-call | flops 1000 | bytes 1000 | tf_op jit(solution)/shard_map/outcome/pallas_call | solution.py:302
  122.5 1.7 %collective-permute-start.30 = (bf16[320,1024]{1,0:T(8,128)(2,1)S(1)}, bf16[320,1024]{1,0:T(8,128)(2,1)S(1)}, u32[]{:S(2)}, u32[]{:S(2)}) collective-permute-start(bf16[320,1024]{1,0:T(8,128)(2,1)S(1)} %get-tuple-element.100), channel_id=1, source_target_pairs={{32,208},{48,0},{0,48},{16,96},{96,16},{112,64},{64,112},{80,160},... | collective-permute-start | bytes 1966088 | tf_op jit(solution)/shard_map/ppermute | solution.py:434
  124.3 3.9 %outcome.3 = (bf16[80,1024]{1,0:T(8,128)(2,1)S(1)}, bf16[80,1024]{1,0:T(8,128)(2,1)S(1)}, bf16[80,1024]{1,0:T(8,128)(2,1)S(1)}, bf16[80,1024]{1,0:T(8,128)(2,1)S(1)}, bf16[320,1024]{1,0:T(8,128)(2,1)S(1)}) custom-call(s32[36]{0:T(128)S(1)} %concatenate.18.table, bf16[640,512]{1,0:T(8,128)(2,1)S(1)} %get-tuple-element.92.made, ...), custom_call_target="tpu_custom_call" | custom-call | flops 1000 | bytes 1000 | tf_op jit(solution)/shard_map/outcome/pallas_call | solution.py:302
  128.4 0.6 collective-permute-start.27
  129.1 0.6 collective-permute-done.26.refs_0_
  130.4 0.7 collective-permute-done.29.refs_3_
  131.0 2.6 %put.2.refs_0_ = bf16[512,2048]{1,0:T(8,128)(2,1)S(1)} custom-call(s32[36]{0:T(128)S(1)} %concatenate.18.table, bf16[512,320]{1,0:T(8,128)(2,1)S(1)} %fusion.1.put, f32[1,512]{1,0:T(1,128)S(1)} %bitcast.29, bf16[320,1024]{1,0:T(8,128)(2,1)S(1)} %get-tuple-element.95.same, bf16[80,1024]{1,0:T(8,128)(2,1)S(1)} %collective-permute-done.26.refs_0_, ...), custom_call_target="tpu_custom_call" | custom-call | flops 1000 | bytes 1000 | tf_op jit(solution)/shard_map/put/pallas_call | solution.py:341
  133.6 6.0 %collective-permute-done.25.same = bf16[320,1024]{1,0:T(8,128)(2,1)S(1)} collective-permute-done((bf16[320,1024]{1,0:T(8,128)(2,1)S(1)}, bf16[320,1024]{1,0:T(8,128)(2,1)S(1)}, u32[]{:S(2)}, u32[]{:S(2)}) %collective-permute-start.25) | collective-permute-done | bytes 655392 | tf_op jit(solution)/shard_map/ppermute | solution.py:433
  139.6 3.5 %put.3 = bf16[512,2048]{1,0:T(8,128)(2,1)} custom-call(s32[36]{0:T(128)S(1)} %concatenate.18.table, bf16[512,320]{1,0:T(8,128)(2,1)S(1)} %fusion.put, f32[1,512]{1,0:T(1,128)S(1)} %bitcast.30, bf16[320,1024]{1,0:T(8,128)(2,1)S(1)} %collective-permute-done.25.same, bf16[512,2048]{1,0:T(8,128)(2,1)S(1)} %put.2.refs_0_, ...), custom_call_target="tpu_custom_call" | custom-call | flops 1000000000 | bytes 6291456 | tf_op jit(solution)/shard_map/put/pallas_call | solution.py:341
  (78 shorter events, 4.2 us)
Async XLA Ops:
  0.6 19.3 %copy-start = (bf16[512,2048]{1,0:T(8,128)(2,1)S(1)}, bf16[512,2048]{1,0:T(8,128)(2,1)}, u32[]{:S(2)}) copy-start(bf16[512,2048]{1,0:T(8,128)(2,1)} %param.20) | copy-start | bytes 6291460
  1.3 7.0 %copy-start.14 = (s32[512,1]{0,1:T(1,128)S(1)}, s32[512,1]{0,1:T(1,128)}, u32[]{:S(2)}) copy-start(s32[512,1]{0,1:T(1,128)} %param.21) | copy-start | bytes 6148
  5.2 2.0 %collective-permute-start = (bf16[4,2,96,256]{3,2,1,0:T(8,128)(2,1)}, bf16[4,2,96,256]{3,2,1,0:T(8,128)(2,1)S(1)}, u32[]{:S(2)}, u32[]{:S(2)}) collective-permute-start(bf16[4,2,96,256]{3,2,1,0:T(8,128)(2,1)} %get-tuple-element.54), channel_id=1, source_target_pairs={{0,32},{32,0},{1,33},{33,1},{2,34},{34,2},{3,35},{35,3},{4,36},{36... | collective-permute-start | bytes 1179656 | tf_op jit(solution)/shard_map/ppermute | solution.py:376
  7.2 1.0 copy-start.5
  9.4 11.5 %collective-permute-start.1 = (bf16[2,96,256]{2,1,0:T(8,128)(2,1)S(1)}, bf16[2,96,256]{2,1,0:T(8,128)(2,1)S(1)}, u32[]{:S(2)}, u32[]{:S(2)}) collective-permute-start(bf16[2,96,256]{2,1,0:T(8,128)(2,1)S(1)} %get-tuple-element.56), channel_id=1, source_target_pairs={{0,64},{64,128},{128,192},{192,0},{1,65},{65,129},{129,193},{193,1... | collective-permute-start | bytes 294920 | tf_op jit(solution)/shard_map/ppermute | solution.py:377
  12.7 8.7 %collective-permute-start.2 = (bf16[2,96,256]{2,1,0:T(8,128)(2,1)S(1)}, bf16[2,96,256]{2,1,0:T(8,128)(2,1)S(1)}, u32[]{:S(2)}, u32[]{:S(2)}) collective-permute-start(bf16[2,96,256]{2,1,0:T(8,128)(2,1)S(1)} %get-tuple-element.57), channel_id=1, source_target_pairs={{0,128},{64,192},{128,0},{192,64},{1,129},{65,193},{129,1},{193,65... | collective-permute-start | bytes 294920 | tf_op jit(solution)/shard_map/ppermute | solution.py:377
  17.2 7.7 %collective-permute-start.3 = (bf16[2,96,256]{2,1,0:T(8,128)(2,1)S(1)}, bf16[2,96,256]{2,1,0:T(8,128)(2,1)S(1)}, u32[]{:S(2)}, u32[]{:S(2)}) collective-permute-start(bf16[2,96,256]{2,1,0:T(8,128)(2,1)S(1)} %get-tuple-element.58), channel_id=1, source_target_pairs={{0,192},{64,0},{128,64},{192,128},{1,193},{65,1},{129,65},{193,129... | collective-permute-start | bytes 294920 | tf_op jit(solution)/shard_map/ppermute | solution.py:377
  20.0 5.0 %copy-start.6 = (f32[2,64,256]{2,1,0:T(8,128)S(1)}, f32[2,64,256]{2,1,0:T(8,128)}, u32[]{:S(2)}) copy-start(f32[2,64,256]{2,1,0:T(8,128)} %get-tuple-element.59.b_in) | copy-start | bytes 393220
  20.0 5.0 %copy-start.7 = (f32[2,64,256]{2,1,0:T(8,128)S(1)}, f32[2,64,256]{2,1,0:T(8,128)}, u32[]{:S(2)}) copy-start(f32[2,64,256]{2,1,0:T(8,128)} %get-tuple-element.60.m_in) | copy-start | bytes 393220
  20.0 5.0 %copy-start.8 = (f32[2,32,256]{2,1,0:T(8,128)S(1)}, f32[2,32,256]{2,1,0:T(8,128)}, u32[]{:S(2)}) copy-start(f32[2,32,256]{2,1,0:T(8,128)} %get-tuple-element.61.b_out) | copy-start | bytes 196612
  20.0 5.0 %copy-start.9 = (f32[2,32,256]{2,1,0:T(8,128)S(1)}, f32[2,32,256]{2,1,0:T(8,128)}, u32[]{:S(2)}) copy-start(f32[2,32,256]{2,1,0:T(8,128)} %get-tuple-element.62.m_out) | copy-start | bytes 196612
  20.0 5.0 %copy-start.11 = (s32[4]{0:T(128)S(1)}, s32[4]{0:T(128)}, u32[]{:S(2)}) copy-start(s32[4]{0:T(128)} %pad_add_fusion.place) | copy-start | bytes 52
  20.0 5.0 %copy-start.12 = (s32[2,64]{1,0:T(2,128)S(1)}, s32[2,64]{1,0:T(2,128)}, u32[]{:S(2)}) copy-start(s32[2,64]{1,0:T(2,128)} %e_in.3) | copy-start | bytes 1540
  20.0 5.0 %copy-start.13 = (s32[2,32]{1,0:T(2,128)S(1)}, s32[2,32]{1,0:T(2,128)}, u32[]{:S(2)}) copy-start(s32[2,32]{1,0:T(2,128)} %e_out.3) | copy-start | bytes 772
  20.9 9.5 %copy-start.1 = (bf16[320,2048]{1,0:T(8,128)(2,1)}, bf16[320,2048]{1,0:T(8,128)(2,1)S(1)}, u32[]{:S(2)}) copy-start(bf16[320,2048]{1,0:T(8,128)(2,1)S(1)} %convolution_convert_fusion.1.refs_1_) | copy-start | bytes 3932164
  26.5 5.4 %collective-permute-start.5 = (bf16[320,2048]{1,0:T(8,128)(2,1)S(1)}, bf16[320,2048]{1,0:T(8,128)(2,1)S(1)}, u32[]{:S(2)}, u32[]{:S(2)}) collective-permute-start(bf16[320,2048]{1,0:T(8,128)(2,1)S(1)} %convolution_convert_fusion.1.refs_1_), channel_id=1, source_target_pairs={{0,32},{32,0},{1,33},{33,1},{2,34},{34,2},{3,35},{35,3},{4,36},{36... | collective-permute-start | bytes 3932168 | tf_op jit(solution)/shard_map/ppermute | solution.py:395
  26.5 5.4 %collective-permute-start.4 = (bf16[96,256]{1,0:T(8,128)(2,1)S(1)}, bf16[96,256]{1,0:T(8,128)(2,1)S(1)}, u32[]{:S(2)}, u32[]{:S(2)}) collective-permute-start(bf16[96,256]{1,0:T(8,128)(2,1)S(1)} %get-tuple-element.70), channel_id=1, source_target_pairs={{0,16},{16,0},{1,17},{17,1},{2,18},{18,2},{3,19},{19,3},{4,20},{20... | collective-permute-start | bytes 147464 | tf_op jit(solution)/shard_map/ppermute | solution.py:397
  31.9 39.0 %copy-start.3 = (bf16[320,2048]{1,0:T(8,128)(2,1)}, bf16[320,2048]{1,0:T(8,128)(2,1)S(1)}, u32[]{:S(2)}) copy-start(bf16[320,2048]{1,0:T(8,128)(2,1)S(1)} %collective-permute-done.5.refs_0_) | copy-start | bytes 3932164
  31.9 8.8 %collective-permute-start.6 = (bf16[2,96,256]{2,1,0:T(8,128)(2,1)S(1)}, bf16[2,96,256]{2,1,0:T(8,128)(2,1)S(1)}, u32[]{:S(2)}, u32[]{:S(2)}) collective-permute-start(bf16[2,96,256]{2,1,0:T(8,128)(2,1)S(1)} %pad_maximum_fusion.4), channel_id=1, source_target_pairs={{0,64},{64,128},{128,192},{192,0},{1,65},{65,129},{129,193},{193,1... | collective-permute-start | bytes 294920 | tf_op jit(solution)/shard_map/ppermute | solution.py:402
  34.5 11.3 %collective-permute-start.7 = (bf16[2,96,256]{2,1,0:T(8,128)(2,1)S(1)}, bf16[2,96,256]{2,1,0:T(8,128)(2,1)S(1)}, u32[]{:S(2)}, u32[]{:S(2)}) collective-permute-start(bf16[2,96,256]{2,1,0:T(8,128)(2,1)S(1)} %pad_maximum_fusion.4), channel_id=1, source_target_pairs={{0,128},{64,192},{128,0},{192,64},{1,129},{65,193},{129,1},{193,65... | collective-permute-start | bytes 294920 | tf_op jit(solution)/shard_map/ppermute | solution.py:402
  38.0 7.8 %collective-permute-start.8 = (bf16[2,96,256]{2,1,0:T(8,128)(2,1)S(1)}, bf16[2,96,256]{2,1,0:T(8,128)(2,1)S(1)}, u32[]{:S(2)}, u32[]{:S(2)}) collective-permute-start(bf16[2,96,256]{2,1,0:T(8,128)(2,1)S(1)} %pad_maximum_fusion.4), channel_id=1, source_target_pairs={{0,192},{64,0},{128,64},{192,128},{1,193},{65,1},{129,65},{193,129... | collective-permute-start | bytes 294920 | tf_op jit(solution)/shard_map/ppermute | solution.py:402
  45.8 25.2 %collective-permute-start.9 = (bf16[320,2048]{1,0:T(8,128)(2,1)S(1)}, bf16[320,2048]{1,0:T(8,128)(2,1)}, u32[]{:S(2)}, u32[]{:S(2)}) collective-permute-start(bf16[320,2048]{1,0:T(8,128)(2,1)S(1)} %convolution_convert_fusion), channel_id=1, source_target_pairs={{0,16},{16,64},{32,240},{48,32},{64,80},{80,128},{96,48},{112,96},... | collective-permute-start | bytes 3932168 | tf_op jit(solution)/shard_map/ppermute | solution.py:405
  49.9 5.8 %collective-permute-start.16 = (bf16[1,2,2,96,256]{4,3,2,1,0:T(8,128)(2,1)S(1)}, bf16[1,2,2,96,256]{4,3,2,1,0:T(8,128)(2,1)S(1)}, u32[]{:S(2)}, u32[]{:S(2)}) collective-permute-start(bf16[1,2,2,96,256]{4,3,2,1,0:T(8,128)(2,1)S(1)} %maximum_bitcast_fusion.1), channel_id=1, source_target_pairs={{0,4},{4,0},{8,12},{12,8},{32,44},{36,40},{40,36},{44,32},{1,5},{5... | collective-permute-start | bytes 589832 | tf_op jit(solution)/shard_map/ppermute | solution.py:410
  51.6 7.2 %collective-permute-start.11 = (bf16[1,2,2,96,256]{4,3,2,1,0:T(8,128)(2,1)S(1)}, bf16[1,2,2,96,256]{4,3,2,1,0:T(8,128)(2,1)S(1)}, u32[]{:S(2)}, u32[]{:S(2)}) collective-permute-start(bf16[1,2,2,96,256]{4,3,2,1,0:T(8,128)(2,1)S(1)} %maximum_bitcast_fusion), channel_id=1, source_target_pairs={{0,1},{1,0},{2,3},{3,2},{32,35},{33,34},{34,33},{35,32},{4,5},{5,4... | collective-permute-start | bytes 589832 | tf_op jit(solution)/shard_map/ppermute | solution.py:410
  55.7 9.1 %collective-permute-start.17 = (bf16[2,2,2,96,256]{4,3,2,1,0:T(8,128)(2,1)S(1)}, bf16[2,2,2,96,256]{4,3,2,1,0:T(8,128)(2,1)S(1)}, u32[]{:S(2)}, u32[]{:S(2)}) collective-permute-start(bf16[2,2,2,96,256]{4,3,2,1,0:T(8,128)(2,1)S(1)} %pad_maximum_fusion.3), channel_id=1, source_target_pairs={{0,12},{4,8},{8,4},{12,0},{32,36},{36,32},{40,44},{44,40},{1,13},{... | collective-permute-start | bytes 1179656 | tf_op jit(solution)/shard_map/ppermute | solution.py:410
  58.8 11.1 %collective-permute-start.12 = (bf16[2,2,2,96,256]{4,3,2,1,0:T(8,128)(2,1)S(1)}, bf16[2,2,2,96,256]{4,3,2,1,0:T(8,128)(2,1)S(1)}, u32[]{:S(2)}, u32[]{:S(2)}) collective-permute-start(bf16[2,2,2,96,256]{4,3,2,1,0:T(8,128)(2,1)S(1)} %pad_maximum_fusion.2), channel_id=1, source_target_pairs={{0,3},{1,2},{2,1},{3,0},{32,33},{33,32},{34,35},{35,34},{4,7},{5,6... | collective-permute-start | bytes 1179656 | tf_op jit(solution)/shard_map/ppermute | solution.py:410
  64.9 15.4 %collective-permute-start.18 = (bf16[4,2,2,96,256]{4,3,2,1,0:T(8,128)(2,1)S(1)}, bf16[4,2,2,96,256]{4,3,2,1,0:T(8,128)(2,1)}, u32[]{:S(2)}, u32[]{:S(2)}) collective-permute-start(bf16[4,2,2,96,256]{4,3,2,1,0:T(8,128)(2,1)S(1)} %pad_maximum_fusion.1.refs_6_.refs_4_), channel_id=1, source_target_pairs={{0,1},{1,0},{2,3},{3,2},{32,35},{33,34},{34,33},{35,32},{4,5},{5,4... | collective-permute-start | bytes 2359304 | tf_op jit(solution)/shard_map/ppermute | solution.py:410
  70.9 20.7 %collective-permute-start.13 = (bf16[4,2,2,96,256]{4,3,2,1,0:T(8,128)(2,1)}, bf16[4,2,2,96,256]{4,3,2,1,0:T(8,128)(2,1)}, u32[]{:S(2)}, u32[]{:S(2)}) collective-permute-start(bf16[4,2,2,96,256]{4,3,2,1,0:T(8,128)(2,1)} %pad_maximum_fusion.refs_2_.refs_0_), channel_id=1, source_target_pairs={{0,4},{4,0},{8,12},{12,8},{32,44},{36,40},{40,36},{44,32},{1,5},{5... | collective-permute-start | bytes 2359304 | tf_op jit(solution)/shard_map/ppermute | solution.py:410
  70.9 34.2 %collective-permute-start.10 = (bf16[320,2048]{1,0:T(8,128)(2,1)}, bf16[320,2048]{1,0:T(8,128)(2,1)}, u32[]{:S(2)}, u32[]{:S(2)}) collective-permute-start(bf16[320,2048]{1,0:T(8,128)(2,1)} %collective-permute-done.9.refs_1_), channel_id=1, source_target_pairs={{0,32},{32,0},{1,33},{33,1},{2,34},{34,2},{3,35},{35,3},{4,36},{36... | collective-permute-start | bytes 3932168 | tf_op jit(solution)/shard_map/ppermute | solution.py:419
  71.0 21.4 %collective-permute-start.19 = (bf16[4,2,2,96,256]{4,3,2,1,0:T(8,128)(2,1)S(1)}, bf16[4,2,2,96,256]{4,3,2,1,0:T(8,128)(2,1)}, u32[]{:S(2)}, u32[]{:S(2)}) collective-permute-start(bf16[4,2,2,96,256]{4,3,2,1,0:T(8,128)(2,1)S(1)} %pad_maximum_fusion.1.refs_6_.refs_4_), channel_id=1, source_target_pairs={{0,3},{1,2},{2,1},{3,0},{32,33},{33,32},{34,35},{35,34},{4,7},{5,6... | collective-permute-start | bytes 2359304 | tf_op jit(solution)/shard_map/ppermute | solution.py:410
  73.9 18.6 %collective-permute-start.14 = (bf16[4,2,2,96,256]{4,3,2,1,0:T(8,128)(2,1)}, bf16[4,2,2,96,256]{4,3,2,1,0:T(8,128)(2,1)}, u32[]{:S(2)}, u32[]{:S(2)}) collective-permute-start(bf16[4,2,2,96,256]{4,3,2,1,0:T(8,128)(2,1)} %pad_maximum_fusion.refs_2_.refs_0_), channel_id=1, source_target_pairs={{0,12},{4,8},{8,4},{12,0},{32,36},{36,32},{40,44},{44,40},{1,13},{... | collective-permute-start | bytes 2359304 | tf_op jit(solution)/shard_map/ppermute | solution.py:410
  80.3 13.5 %collective-permute-start.20 = (bf16[4,2,2,96,256]{4,3,2,1,0:T(8,128)(2,1)}, bf16[4,2,2,96,256]{4,3,2,1,0:T(8,128)(2,1)}, u32[]{:S(2)}, u32[]{:S(2)}) collective-permute-start(bf16[4,2,2,96,256]{4,3,2,1,0:T(8,128)(2,1)} %collective-permute-done.18.refs_7_.refs_5_), channel_id=1, source_target_pairs={{0,3},{1,2},{2,1},{3,0},{32,33},{33,32},{34,35},{35,34},{4,7},{5,6... | collective-permute-start | bytes 2359304 | tf_op jit(solution)/shard_map/ppermute | solution.py:410
  91.6 13.5 %collective-permute-start.15 = (bf16[4,2,2,96,256]{4,3,2,1,0:T(8,128)(2,1)}, bf16[4,2,2,96,256]{4,3,2,1,0:T(8,128)(2,1)}, u32[]{:S(2)}, u32[]{:S(2)}) collective-permute-start(bf16[4,2,2,96,256]{4,3,2,1,0:T(8,128)(2,1)} %collective-permute-done.13.refs_3_.refs_1_), channel_id=1, source_target_pairs={{0,12},{4,8},{8,4},{12,0},{32,36},{36,32},{40,44},{44,40},{1,13},{... | collective-permute-start | bytes 2359304 | tf_op jit(solution)/shard_map/ppermute | solution.py:410
  92.4 19.5 %copy-start.2 = (bf16[320,2048]{1,0:T(8,128)(2,1)S(1)}, bf16[320,2048]{1,0:T(8,128)(2,1)}, u32[]{:S(2)}) copy-start(bf16[320,2048]{1,0:T(8,128)(2,1)} %copy-done.1) | copy-start | bytes 3932164
  92.4 19.5 %copy-start.4 = (bf16[320,2048]{1,0:T(8,128)(2,1)S(1)}, bf16[320,2048]{1,0:T(8,128)(2,1)}, u32[]{:S(2)}) copy-start(bf16[320,2048]{1,0:T(8,128)(2,1)} %copy-done.3) | copy-start | bytes 3932164
  111.3 7.0 %collective-permute-start.21 = (bf16[320,512]{1,0:T(8,128)(2,1)S(1)}, bf16[320,512]{1,0:T(8,128)(2,1)S(1)}, u32[]{:S(2)}, u32[]{:S(2)}) collective-permute-start(bf16[320,512]{1,0:T(8,128)(2,1)S(1)} %get-tuple-element.81), channel_id=1, source_target_pairs={{0,32},{32,0},{1,33},{33,1},{2,34},{34,2},{3,35},{35,3},{4,36},{36... | collective-permute-start | bytes 983048 | tf_op jit(solution)/shard_map/ppermute | solution.py:422
  111.4 6.9 %collective-permute-start.22 = (bf16[320,512]{1,0:T(8,128)(2,1)S(1)}, bf16[320,512]{1,0:T(8,128)(2,1)S(1)}, u32[]{:S(2)}, u32[]{:S(2)}) collective-permute-start(bf16[320,512]{1,0:T(8,128)(2,1)S(1)} %get-tuple-element.82), channel_id=1, source_target_pairs={{0,32},{32,0},{1,33},{33,1},{2,34},{34,2},{3,35},{35,3},{4,36},{36... | collective-permute-start | bytes 983048 | tf_op jit(solution)/shard_map/ppermute | solution.py:422
  117.7 4.5 %collective-permute-start.23 = (bf16[320,512]{1,0:T(8,128)(2,1)S(1)}, bf16[320,512]{1,0:T(8,128)(2,1)S(1)}, u32[]{:S(2)}, u32[]{:S(2)}) collective-permute-start(bf16[320,512]{1,0:T(8,128)(2,1)S(1)} %get-tuple-element.89), channel_id=1, source_target_pairs={{0,32},{32,0},{1,33},{33,1},{2,34},{34,2},{3,35},{35,3},{4,36},{36... | collective-permute-start | bytes 983048 | tf_op jit(solution)/shard_map/ppermute | solution.py:422
  117.9 4.3 %collective-permute-start.24 = (bf16[320,512]{1,0:T(8,128)(2,1)S(1)}, bf16[320,512]{1,0:T(8,128)(2,1)S(1)}, u32[]{:S(2)}, u32[]{:S(2)}) collective-permute-start(bf16[320,512]{1,0:T(8,128)(2,1)S(1)} %get-tuple-element.90), channel_id=1, source_target_pairs={{0,32},{32,0},{1,33},{33,1},{2,34},{34,2},{3,35},{35,3},{4,36},{36... | collective-permute-start | bytes 983048 | tf_op jit(solution)/shard_map/ppermute | solution.py:422
  122.2 17.4 %collective-permute-start.25 = (bf16[320,1024]{1,0:T(8,128)(2,1)S(1)}, bf16[320,1024]{1,0:T(8,128)(2,1)S(1)}, u32[]{:S(2)}, u32[]{:S(2)}) collective-permute-start(bf16[320,1024]{1,0:T(8,128)(2,1)S(1)} %get-tuple-element.91), channel_id=1, source_target_pairs={{0,208},{16,0},{32,48},{48,96},{64,16},{80,64},{96,112},{112,160},... | collective-permute-start | bytes 1966088 | tf_op jit(solution)/shard_map/ppermute | solution.py:433
  122.5 17.1 %collective-permute-start.30 = (bf16[320,1024]{1,0:T(8,128)(2,1)S(1)}, bf16[320,1024]{1,0:T(8,128)(2,1)S(1)}, u32[]{:S(2)}, u32[]{:S(2)}) collective-permute-start(bf16[320,1024]{1,0:T(8,128)(2,1)S(1)} %get-tuple-element.100), channel_id=1, source_target_pairs={{32,208},{48,0},{0,48},{16,96},{96,16},{112,64},{64,112},{80,160},... | collective-permute-start | bytes 1966088 | tf_op jit(solution)/shard_map/ppermute | solution.py:434
  124.3 6.8 %copy-start.10 = (f32[512]{0:T(512)S(1)}, f32[512]{0:T(512)}, u32[]{:S(2)}) copy-start(f32[512]{0:T(512)} %param.22) | copy-start | bytes 6148
  128.2 1.5 %collective-permute-start.26 = (bf16[80,1024]{1,0:T(8,128)(2,1)S(1)}, bf16[80,1024]{1,0:T(8,128)(2,1)S(1)}, u32[]{:S(2)}, u32[]{:S(2)}) collective-permute-start(bf16[80,1024]{1,0:T(8,128)(2,1)S(1)} %get-tuple-element.96), channel_id=1, source_target_pairs={{0,32},{32,0},{1,33},{33,1},{2,34},{34,2},{3,35},{35,3},{4,36},{36... | collective-permute-start | bytes 491528 | tf_op jit(solution)/shard_map/ppermute | solution.py:422
  128.4 1.6 %collective-permute-start.27 = (bf16[80,1024]{1,0:T(8,128)(2,1)S(1)}, bf16[80,1024]{1,0:T(8,128)(2,1)S(1)}, u32[]{:S(2)}, u32[]{:S(2)}) collective-permute-start(bf16[80,1024]{1,0:T(8,128)(2,1)S(1)} %get-tuple-element.97), channel_id=1, source_target_pairs={{0,32},{32,0},{1,33},{33,1},{2,34},{34,2},{3,35},{35,3},{4,36},{36... | collective-permute-start | bytes 491528 | tf_op jit(solution)/shard_map/ppermute | solution.py:422
  129.0 1.4 collective-permute-start.28
  129.6 1.4 collective-permute-start.29

commit v4 on v3

--- a/solution.py
+++ b/solution.py
@@ -18,6 +18,7 @@
 FSDP = ("zl", "y", "x")
 COLUMN = ("zh", "core", "zl")
 GROUPS = ZH * CORE
+FAR_FIRST = (2, 1, 3)
 COLS = 256
 ROWS_IN, ROWS_OUT = 64, 32
 ROWS = ROWS_IN + ROWS_OUT
@@ -374,7 +375,7 @@
         place, (base_in, local_in, exp_in, base_out, local_out, exp_out), (mom_in, mom_out)
     )
     own, *sent = pair_call(kept, lax.ppermute(given, "core", shift(CORE, 1)))
-    received = [lax.ppermute(sent[s - 1], "zh", shift(ZH, s)) for s in range(1, ZH)]
+    received = [lax.ppermute(sent[s - 1], "zh", shift(ZH, s)) for s in FAR_FIRST]
     new_base_in, new_base_out, new_mom_in, new_mom_out, kept, given = step_call(
         place, own, received, b_in, m_in, exp_in, b_out, m_out, exp_out
     )
@@ -399,7 +400,8 @@
         (kept, taken, tokens_sent, other_own)
     )
     both = jnp.stack([kept, taken])
-    column = [both] + [lax.ppermute(both, "zh", shift(ZH, s)) for s in range(1, ZH)]
+    by_step = {s: lax.ppermute(both, "zh", shift(ZH, s)) for s in FAR_FIRST}
+    column = [both] + [by_step[s] for s in range(1, ZH)]
     *column, tokens_sent = lax.optimization_barrier((*column, tokens_sent))
 
     tokens_got = lax.ppermute(tokens_sent, COLUMN, column_pairs(1, 0))

time: 144 us -> 143 us (level)
  no operation moved by 1% of the time
where the time goes in v4:
time: 143 us; the launch traced here: 142 us
  waiting for transfers between devices  56 us (39%)
  starting transfers between devices  47.3 us (33%)
  Pallas kernels  31.2 us (22%)
  other arithmetic  2.9 us (2%)
  local copies, waits for them, and re-layouts  2.23 us (2%)
  matrix products  1.69 us (1%)
    ppermute x10, waiting for transfers between devices, exchange(): lax.ppermute(a, ('core', axis), flip_pairs(turn))  36.1 us
    ppermute x10, starting transfers between devices, exchange(): lax.ppermute(a, ('core', axis), flip_pairs(turn))  17 us
    pallas_call x2, Pallas kernels, hidden_call(): pl.pallas_call(functools.partial(hidden_kernel, parts), in_specs=[pl.Bloc...  11.9 us
    ppermute x3, starting transfers between devices, body(): lax.ppermute(sent[s - 1], 'zh', shift(ZH, s))  10.5 us
    ppermute x3, starting transfers between devices, body(): by_step = {s: lax.ppermute(both, 'zh', shift(ZH, s)) for s in FAR_FIRST}  9.05 us
    pallas_call x2, Pallas kernels, outcome_call(): pl.pallas_call(outcome_kernel, in_specs=[pl.BlockSpec(memory_space=pltpu....  7.75 us
    pallas_call x2, Pallas kernels, put_call(): pl.pallas_call(functools.partial(put_kernel, len(before)), grid_spec=pltp...  6.1 us
    ppermute x1, waiting for transfers between devices, body(): back_same = lax.ppermute(far_mine, COLUMN, column_pairs(-1, 0))  5.53 us
  transfers between devices with their start and end apart: 31, of which 18 were waited for; matrix products, arithmetic and copies ran while one was open for 3% of the time, Pallas kernels for 11%

profile of v4, /device:TPU:32, one launch (start us, length us, event | category | flops | bytes accessed | tf_op | source)
XLA Modules:
  0.0 142.3 jit_solution(3137562423722872712)
XLA Ops:
  0.7 0.7 pad_add_fusion.place
  1.3 3.8 %give.1 = (bf16[4,2,96,256]{3,2,1,0:T(8,128)(2,1)}, bf16[4,2,96,256]{3,2,1,0:T(8,128)(2,1)}, f32[2,64,256]{2,1,0:T(8,128)}, f32[2,32,256]{2,1,0:T(8,128)}, f32[2,64,256]{2,1,0:T(8,128)}, /*index=5*/f32[2,32,256]{2,1,0:T(8,128)}) custom-call(s32[4]{0:T(128)} %pad_add_fusion.place, f32[2,64,2048]{2,1,0:T(8,128)} %b_in.1, bf16[1,2,64,2048]{3,2,1,0:T(8,128)(2,1)} %l_in.1, ...), custom_call_target="tpu_custom_call" | custom-call | flops 1000000 | bytes 4194304 | tf_op jit(solution)/shard_map/give/pallas_call | solution.py:121
  5.3 1.9 %collective-permute-done.taken = bf16[4,2,96,256]{3,2,1,0:T(8,128)(2,1)S(1)} collective-permute-done((bf16[4,2,96,256]{3,2,1,0:T(8,128)(2,1)}, bf16[4,2,96,256]{3,2,1,0:T(8,128)(2,1)S(1)}, u32[]{:S(2)}, u32[]{:S(2)}) %collective-permute-start) | collective-permute-done | bytes 393248 | tf_op jit(solution)/shard_map/ppermute | solution.py:377
  7.2 1.0 copy-done.5
  9.4 6.4 %collective-permute-start.1 = (bf16[2,96,256]{2,1,0:T(8,128)(2,1)S(1)}, bf16[2,96,256]{2,1,0:T(8,128)(2,1)S(1)}, u32[]{:S(2)}, u32[]{:S(2)}) collective-permute-start(bf16[2,96,256]{2,1,0:T(8,128)(2,1)S(1)} %get-tuple-element.56), channel_id=1, source_target_pairs={{0,128},{64,192},{128,0},{192,64},{1,129},{65,193},{129,1},{193,65... | collective-permute-start | bytes 294920 | tf_op jit(solution)/shard_map/ppermute | solution.py:378
  15.8 1.5 %collective-permute-start.2 = (bf16[2,96,256]{2,1,0:T(8,128)(2,1)S(1)}, bf16[2,96,256]{2,1,0:T(8,128)(2,1)S(1)}, u32[]{:S(2)}, u32[]{:S(2)}) collective-permute-start(bf16[2,96,256]{2,1,0:T(8,128)(2,1)S(1)} %get-tuple-element.57), channel_id=1, source_target_pairs={{0,64},{64,128},{128,192},{192,0},{1,65},{65,129},{129,193},{193,1... | collective-permute-start | bytes 294920 | tf_op jit(solution)/shard_map/ppermute | solution.py:378
  17.2 2.7 %collective-permute-start.3 = (bf16[2,96,256]{2,1,0:T(8,128)(2,1)S(1)}, bf16[2,96,256]{2,1,0:T(8,128)(2,1)S(1)}, u32[]{:S(2)}, u32[]{:S(2)}) collective-permute-start(bf16[2,96,256]{2,1,0:T(8,128)(2,1)S(1)} %get-tuple-element.58), channel_id=1, source_target_pairs={{0,192},{64,0},{128,64},{192,128},{1,193},{65,1},{129,65},{193,129... | collective-permute-start | bytes 294920 | tf_op jit(solution)/shard_map/ppermute | solution.py:378
  20.0 0.8 convolution_convert_fusion.1.refs_1_
  20.9 4.2 %collective-permute-done.2.r2 = bf16[2,96,256]{2,1,0:T(8,128)(2,1)S(1)} collective-permute-done((bf16[2,96,256]{2,1,0:T(8,128)(2,1)S(1)}, bf16[2,96,256]{2,1,0:T(8,128)(2,1)S(1)}, u32[]{:S(2)}, u32[]{:S(2)}) %collective-permute-start.2) | collective-permute-done | bytes 98336 | tf_op jit(solution)/shard_map/ppermute | solution.py:378
  25.1 1.5 %step.1 = (f32[2,64,256]{2,1,0:T(8,128)}, f32[2,32,256]{2,1,0:T(8,128)}, f32[2,64,256]{2,1,0:T(8,128)}, f32[2,32,256]{2,1,0:T(8,128)}, bf16[96,256]{1,0:T(8,128)(2,1)S(1)}, /*index=5*/bf16[96,256]{1,0:T(8,128)(2,1)S(1)}) custom-call(s32[4]{0:T(128)S(1)} %copy-done.11, f32[2,96,256]{2,1,0:T(8,128)S(1)} %get-tuple-element.55.own, ...), custom_call_target="tpu_custom_call" | custom-call | flops 1000000 | bytes 2097152 | tf_op jit(solution)/shard_map/step/pallas_call | solution.py:178
  26.7 1.7 %collective-permute-start.4 = (bf16[96,256]{1,0:T(8,128)(2,1)S(1)}, bf16[96,256]{1,0:T(8,128)(2,1)S(1)}, u32[]{:S(2)}, u32[]{:S(2)}) collective-permute-start(bf16[96,256]{1,0:T(8,128)(2,1)S(1)} %get-tuple-element.70), channel_id=1, source_target_pairs={{0,16},{16,0},{1,17},{17,1},{2,18},{18,2},{3,19},{19,3},{4,20},{20... | collective-permute-start | bytes 147464 | tf_op jit(solution)/shard_map/ppermute | solution.py:398
  28.4 0.8 convolution_convert_fusion
  29.2 1.6 %collective-permute-done.4 = bf16[96,256]{1,0:T(8,128)(2,1)S(1)} collective-permute-done((bf16[96,256]{1,0:T(8,128)(2,1)S(1)}, bf16[96,256]{1,0:T(8,128)(2,1)S(1)}, u32[]{:S(2)}, u32[]{:S(2)}) %collective-permute-start.4) | collective-permute-done | bytes 49184 | tf_op jit(solution)/shard_map/ppermute | solution.py:398
  30.8 2.4 %collective-permute-start.6 = (bf16[2,96,256]{2,1,0:T(8,128)(2,1)S(1)}, bf16[2,96,256]{2,1,0:T(8,128)(2,1)S(1)}, u32[]{:S(2)}, u32[]{:S(2)}) collective-permute-start(bf16[2,96,256]{2,1,0:T(8,128)(2,1)S(1)} %pad_maximum_fusion.4), channel_id=1, source_target_pairs={{0,64},{64,128},{128,192},{192,0},{1,65},{65,129},{129,193},{193,1... | collective-permute-start | bytes 294920 | tf_op jit(solution)/shard_map/ppermute | solution.py:403
  33.2 4.0 %collective-permute-start.7 = (bf16[2,96,256]{2,1,0:T(8,128)(2,1)S(1)}, bf16[2,96,256]{2,1,0:T(8,128)(2,1)S(1)}, u32[]{:S(2)}, u32[]{:S(2)}) collective-permute-start(bf16[2,96,256]{2,1,0:T(8,128)(2,1)S(1)} %pad_maximum_fusion.4), channel_id=1, source_target_pairs={{0,128},{64,192},{128,0},{192,64},{1,129},{65,193},{129,1},{193,65... | collective-permute-start | bytes 294920 | tf_op jit(solution)/shard_map/ppermute | solution.py:403
  37.2 2.7 %collective-permute-start.8 = (bf16[2,96,256]{2,1,0:T(8,128)(2,1)S(1)}, bf16[2,96,256]{2,1,0:T(8,128)(2,1)S(1)}, u32[]{:S(2)}, u32[]{:S(2)}) collective-permute-start(bf16[2,96,256]{2,1,0:T(8,128)(2,1)S(1)} %pad_maximum_fusion.4), channel_id=1, source_target_pairs={{0,192},{64,0},{128,64},{192,128},{1,193},{65,1},{129,65},{193,129... | collective-permute-start | bytes 294920 | tf_op jit(solution)/shard_map/ppermute | solution.py:403
  39.9 4.5 %collective-permute-done.7 = bf16[2,96,256]{2,1,0:T(8,128)(2,1)S(1)} collective-permute-done((bf16[2,96,256]{2,1,0:T(8,128)(2,1)S(1)}, bf16[2,96,256]{2,1,0:T(8,128)(2,1)S(1)}, u32[]{:S(2)}, u32[]{:S(2)}) %collective-permute-start.7) | collective-permute-done | bytes 98336 | tf_op jit(solution)/shard_map/ppermute | solution.py:403
  44.7 3.9 %collective-permute-start.9 = (bf16[320,2048]{1,0:T(8,128)(2,1)S(1)}, bf16[320,2048]{1,0:T(8,128)(2,1)}, u32[]{:S(2)}, u32[]{:S(2)}) collective-permute-start(bf16[320,2048]{1,0:T(8,128)(2,1)S(1)} %convolution_convert_fusion), channel_id=1, source_target_pairs={{0,16},{16,64},{32,240},{48,32},{64,80},{80,128},{96,48},{112,96},... | collective-permute-start | bytes 3932168 | tf_op jit(solution)/shard_map/ppermute | solution.py:407
  48.7 1.7 %collective-permute-start.16 = (bf16[1,2,2,96,256]{4,3,2,1,0:T(8,128)(2,1)S(1)}, bf16[1,2,2,96,256]{4,3,2,1,0:T(8,128)(2,1)S(1)}, u32[]{:S(2)}, u32[]{:S(2)}) collective-permute-start(bf16[1,2,2,96,256]{4,3,2,1,0:T(8,128)(2,1)S(1)} %maximum_bitcast_fusion.1), channel_id=1, source_target_pairs={{0,4},{4,0},{8,12},{12,8},{32,44},{36,40},{40,36},{44,32},{1,5},{5... | collective-permute-start | bytes 589832 | tf_op jit(solution)/shard_map/ppermute | solution.py:412
  50.4 1.6 %collective-permute-start.11 = (bf16[1,2,2,96,256]{4,3,2,1,0:T(8,128)(2,1)S(1)}, bf16[1,2,2,96,256]{4,3,2,1,0:T(8,128)(2,1)S(1)}, u32[]{:S(2)}, u32[]{:S(2)}) collective-permute-start(bf16[1,2,2,96,256]{4,3,2,1,0:T(8,128)(2,1)S(1)} %maximum_bitcast_fusion), channel_id=1, source_target_pairs={{0,1},{1,0},{2,3},{3,2},{32,35},{33,34},{34,33},{35,32},{4,5},{5,4... | collective-permute-start | bytes 589832 | tf_op jit(solution)/shard_map/ppermute | solution.py:412
  51.9 2.5 %collective-permute-done.16 = bf16[1,2,2,96,256]{4,3,2,1,0:T(8,128)(2,1)S(1)} collective-permute-done((bf16[1,2,2,96,256]{4,3,2,1,0:T(8,128)(2,1)S(1)}, bf16[1,2,2,96,256]{4,3,2,1,0:T(8,128)(2,1)S(1)}, u32[]{:S(2)}, u32[]{:S(2)}) %collective-permute-start.16) | collective-permute-done | bytes 196640 | tf_op jit(solution)/shard_map/ppermute | solution.py:412
  54.5 3.1 %collective-permute-start.17 = (bf16[2,2,2,96,256]{4,3,2,1,0:T(8,128)(2,1)S(1)}, bf16[2,2,2,96,256]{4,3,2,1,0:T(8,128)(2,1)S(1)}, u32[]{:S(2)}, u32[]{:S(2)}) collective-permute-start(bf16[2,2,2,96,256]{4,3,2,1,0:T(8,128)(2,1)S(1)} %pad_maximum_fusion.3), channel_id=1, source_target_pairs={{0,12},{4,8},{8,4},{12,0},{32,36},{36,32},{40,44},{44,40},{1,13},{... | collective-permute-start | bytes 1179656 | tf_op jit(solution)/shard_map/ppermute | solution.py:412
  57.6 2.8 %collective-permute-start.12 = (bf16[2,2,2,96,256]{4,3,2,1,0:T(8,128)(2,1)S(1)}, bf16[2,2,2,96,256]{4,3,2,1,0:T(8,128)(2,1)S(1)}, u32[]{:S(2)}, u32[]{:S(2)}) collective-permute-start(bf16[2,2,2,96,256]{4,3,2,1,0:T(8,128)(2,1)S(1)} %pad_maximum_fusion.2), channel_id=1, source_target_pairs={{0,3},{1,2},{2,1},{3,0},{32,33},{33,32},{34,35},{35,34},{4,7},{5,6... | collective-permute-start | bytes 1179656 | tf_op jit(solution)/shard_map/ppermute | solution.py:412
  60.5 3.1 %collective-permute-done.17 = bf16[2,2,2,96,256]{4,3,2,1,0:T(8,128)(2,1)S(1)} collective-permute-done((bf16[2,2,2,96,256]{4,3,2,1,0:T(8,128)(2,1)S(1)}, bf16[2,2,2,96,256]{4,3,2,1,0:T(8,128)(2,1)S(1)}, u32[]{:S(2)}, u32[]{:S(2)}) %collective-permute-start.17) | collective-permute-done | bytes 393248 | tf_op jit(solution)/shard_map/ppermute | solution.py:412
  63.6 1.8 %collective-permute-start.18 = (bf16[4,2,2,96,256]{4,3,2,1,0:T(8,128)(2,1)S(1)}, bf16[4,2,2,96,256]{4,3,2,1,0:T(8,128)(2,1)}, u32[]{:S(2)}, u32[]{:S(2)}) collective-permute-start(bf16[4,2,2,96,256]{4,3,2,1,0:T(8,128)(2,1)S(1)} %pad_maximum_fusion.1.refs_6_.refs_4_), channel_id=1, source_target_pairs={{0,1},{1,0},{2,3},{3,2},{32,35},{33,34},{34,33},{35,32},{4,5},{5,4... | collective-permute-start | bytes 2359304 | tf_op jit(solution)/shard_map/ppermute | solution.py:412
  65.4 3.3 %collective-permute-done.12 = bf16[2,2,2,96,256]{4,3,2,1,0:T(8,128)(2,1)S(1)} collective-permute-done((bf16[2,2,2,96,256]{4,3,2,1,0:T(8,128)(2,1)S(1)}, bf16[2,2,2,96,256]{4,3,2,1,0:T(8,128)(2,1)S(1)}, u32[]{:S(2)}, u32[]{:S(2)}) %collective-permute-start.12) | collective-permute-done | bytes 393248 | tf_op jit(solution)/shard_map/ppermute | solution.py:412
  68.6 1.0 pad_maximum_fusion.refs_2_.refs_0_
  69.7 2.8 %collective-permute-start.19 = (bf16[4,2,2,96,256]{4,3,2,1,0:T(8,128)(2,1)S(1)}, bf16[4,2,2,96,256]{4,3,2,1,0:T(8,128)(2,1)}, u32[]{:S(2)}, u32[]{:S(2)}) collective-permute-start(bf16[4,2,2,96,256]{4,3,2,1,0:T(8,128)(2,1)S(1)} %pad_maximum_fusion.1.refs_6_.refs_4_), channel_id=1, source_target_pairs={{0,3},{1,2},{2,1},{3,0},{32,33},{33,32},{34,35},{35,34},{4,7},{5,6... | collective-permute-start | bytes 2359304 | tf_op jit(solution)/shard_map/ppermute | solution.py:412
  72.6 0.6 collective-permute-start.14
  73.2 6.0 %collective-permute-done.18.refs_7_.refs_5_ = bf16[4,2,2,96,256]{4,3,2,1,0:T(8,128)(2,1)} collective-permute-done((bf16[4,2,2,96,256]{4,3,2,1,0:T(8,128)(2,1)S(1)}, bf16[4,2,2,96,256]{4,3,2,1,0:T(8,128)(2,1)}, u32[]{:S(2)}, u32[]{:S(2)}) %collective-permute-start.18) | collective-permute-done | bytes 786464 | tf_op jit(solution)/shard_map/ppermute | solution.py:412
  79.1 2.6 %collective-permute-start.20 = (bf16[4,2,2,96,256]{4,3,2,1,0:T(8,128)(2,1)}, bf16[4,2,2,96,256]{4,3,2,1,0:T(8,128)(2,1)}, u32[]{:S(2)}, u32[]{:S(2)}) collective-permute-start(bf16[4,2,2,96,256]{4,3,2,1,0:T(8,128)(2,1)} %collective-permute-done.18.refs_7_.refs_5_), channel_id=1, source_target_pairs={{0,3},{1,2},{2,1},{3,0},{32,33},{33,32},{34,35},{35,34},{4,7},{5,6... | collective-permute-start | bytes 2359304 | tf_op jit(solution)/shard_map/ppermute | solution.py:412
  81.8 8.6 %collective-permute-done.13.refs_3_.refs_1_ = bf16[4,2,2,96,256]{4,3,2,1,0:T(8,128)(2,1)} collective-permute-done((bf16[4,2,2,96,256]{4,3,2,1,0:T(8,128)(2,1)}, bf16[4,2,2,96,256]{4,3,2,1,0:T(8,128)(2,1)}, u32[]{:S(2)}, u32[]{:S(2)}) %collective-permute-start.13) | collective-permute-done | bytes 786464 | tf_op jit(solution)/shard_map/ppermute | solution.py:412
  90.3 0.7 dynamic-slice_bitcast_fusion
  91.1 1.5 %collective-permute-done.20.refs_9_.refs_7_ = bf16[4,2,2,96,256]{4,3,2,1,0:T(8,128)(2,1)} collective-permute-done((bf16[4,2,2,96,256]{4,3,2,1,0:T(8,128)(2,1)}, bf16[4,2,2,96,256]{4,3,2,1,0:T(8,128)(2,1)}, u32[]{:S(2)}, u32[]{:S(2)}) %collective-permute-start.20) | collective-permute-done | bytes 786464 | tf_op jit(solution)/shard_map/ppermute | solution.py:412
  92.6 11.2 %collective-permute-done.15.refs_5_.refs_3_ = bf16[4,2,2,96,256]{4,3,2,1,0:T(8,128)(2,1)} collective-permute-done((bf16[4,2,2,96,256]{4,3,2,1,0:T(8,128)(2,1)}, bf16[4,2,2,96,256]{4,3,2,1,0:T(8,128)(2,1)}, u32[]{:S(2)}, u32[]{:S(2)}) %collective-permute-start.15) | collective-permute-done | bytes 786464 | tf_op jit(solution)/shard_map/ppermute | solution.py:412
  103.9 6.1 %hidden.2 = (bf16[640,512]{1,0:T(8,128)(2,1)S(1)}, bf16[320,512]{1,0:T(8,128)(2,1)S(1)}, bf16[320,512]{1,0:T(8,128)(2,1)S(1)}) custom-call(s32[36]{0:T(128)S(1)} %concatenate.18.table, bf16[320,2048]{1,0:T(8,128)(2,1)} %collective-permute-done.10.refs_0_, bf16[320,2048]{1,0:T(8,128)(2,1)} %collective-permute-done.9.refs_1_, ...), custom_call_target="tpu_custom_call" | custom-call | flops 1000 | bytes 1000 | tf_op jit(solution)/shard_map/hidden/pallas_call | solution.py:252
  110.1 0.5 collective-permute-start.22
  110.6 5.8 %hidden.3 = (bf16[640,512]{1,0:T(8,128)(2,1)S(1)}, bf16[320,512]{1,0:T(8,128)(2,1)S(1)}, bf16[320,512]{1,0:T(8,128)(2,1)S(1)}) custom-call(s32[36]{0:T(128)S(1)} %concatenate.18.table, bf16[320,2048]{1,0:T(8,128)(2,1)S(1)} %copy-done.4, bf16[320,2048]{1,0:T(8,128)(2,1)S(1)} %copy-done.2, bf16[4,2,2,96,256]{4,3,2,1,0:T(8,128)(2,1)} %pad_maximum_fusion.refs_2_.refs_0_, ...), custom_call_target="tpu_custom_call" | custom-call | flops 1000 | bytes 1000 | tf_op jit(solution)/shard_map/hidden/pallas_call | solution.py:252
  116.6 0.4 collective-permute-start.24
  117.0 3.9 %outcome.2 = (bf16[320,1024]{1,0:T(8,128)(2,1)S(1)}, bf16[320,1024]{1,0:T(8,128)(2,1)S(1)}) custom-call(s32[36]{0:T(128)S(1)} %concatenate.18.table, bf16[640,512]{1,0:T(8,128)(2,1)S(1)} %get-tuple-element.80.made, bf16[320,512]{1,0:T(8,128)(2,1)S(1)} %collective-permute-done.21.got0, bf16[320,512]{1,0:T(8,128)(2,1)S(1)} %collective-permute-done.22.got1, ...), custom_call_target="tpu_custom_call" | custom-call | flops 1000 | bytes 1000 | tf_op jit(solution)/shard_map/outcome/pallas_call | solution.py:303
  121.2 2.5 %collective-permute-start.30 = (bf16[320,1024]{1,0:T(8,128)(2,1)S(1)}, bf16[320,1024]{1,0:T(8,128)(2,1)S(1)}, u32[]{:S(2)}, u32[]{:S(2)}) collective-permute-start(bf16[320,1024]{1,0:T(8,128)(2,1)S(1)} %get-tuple-element.100), channel_id=1, source_target_pairs={{32,208},{48,0},{0,48},{16,96},{96,16},{112,64},{64,112},{80,160},... | collective-permute-start | bytes 1966088 | tf_op jit(solution)/shard_map/ppermute | solution.py:436
  123.7 3.9 %outcome.3 = (bf16[80,1024]{1,0:T(8,128)(2,1)S(1)}, bf16[80,1024]{1,0:T(8,128)(2,1)S(1)}, bf16[80,1024]{1,0:T(8,128)(2,1)S(1)}, bf16[80,1024]{1,0:T(8,128)(2,1)S(1)}, bf16[320,1024]{1,0:T(8,128)(2,1)S(1)}) custom-call(s32[36]{0:T(128)S(1)} %concatenate.18.table, bf16[640,512]{1,0:T(8,128)(2,1)S(1)} %get-tuple-element.92.made, ...), custom_call_target="tpu_custom_call" | custom-call | flops 1000 | bytes 1000 | tf_op jit(solution)/shard_map/outcome/pallas_call | solution.py:303
  127.8 0.6 collective-permute-start.27
  128.5 0.6 collective-permute-done.26.refs_0_
  129.8 0.7 collective-permute-done.29.refs_3_
  130.5 2.6 %put.2.refs_0_ = bf16[512,2048]{1,0:T(8,128)(2,1)S(1)} custom-call(s32[36]{0:T(128)S(1)} %concatenate.18.table, bf16[512,320]{1,0:T(8,128)(2,1)S(1)} %fusion.1.put, f32[1,512]{1,0:T(1,128)S(1)} %bitcast.29, bf16[320,1024]{1,0:T(8,128)(2,1)S(1)} %get-tuple-element.95.same, bf16[80,1024]{1,0:T(8,128)(2,1)S(1)} %collective-permute-done.26.refs_0_, ...), custom_call_target="tpu_custom_call" | custom-call | flops 1000 | bytes 1000 | tf_op jit(solution)/shard_map/put/pallas_call | solution.py:342
  133.1 5.5 %collective-permute-done.25.same = bf16[320,1024]{1,0:T(8,128)(2,1)S(1)} collective-permute-done((bf16[320,1024]{1,0:T(8,128)(2,1)S(1)}, bf16[320,1024]{1,0:T(8,128)(2,1)S(1)}, u32[]{:S(2)}, u32[]{:S(2)}) %collective-permute-start.25) | collective-permute-done | bytes 655392 | tf_op jit(solution)/shard_map/ppermute | solution.py:435
  138.8 3.5 %put.3 = bf16[512,2048]{1,0:T(8,128)(2,1)} custom-call(s32[36]{0:T(128)S(1)} %concatenate.18.table, bf16[512,320]{1,0:T(8,128)(2,1)S(1)} %fusion.put, f32[1,512]{1,0:T(1,128)S(1)} %bitcast.30, bf16[320,1024]{1,0:T(8,128)(2,1)S(1)} %collective-permute-done.25.same, bf16[512,2048]{1,0:T(8,128)(2,1)S(1)} %put.2.refs_0_, ...), custom_call_target="tpu_custom_call" | custom-call | flops 1000000000 | bytes 6291456 | tf_op jit(solution)/shard_map/put/pallas_call | solution.py:342
  (78 shorter events, 4.0 us)
Async XLA Ops:
  0.6 19.3 %copy-start = (bf16[512,2048]{1,0:T(8,128)(2,1)S(1)}, bf16[512,2048]{1,0:T(8,128)(2,1)}, u32[]{:S(2)}) copy-start(bf16[512,2048]{1,0:T(8,128)(2,1)} %param.20) | copy-start | bytes 6291460
  1.3 7.0 %copy-start.14 = (s32[512,1]{0,1:T(1,128)S(1)}, s32[512,1]{0,1:T(1,128)}, u32[]{:S(2)}) copy-start(s32[512,1]{0,1:T(1,128)} %param.21) | copy-start | bytes 6148
  5.2 2.0 %collective-permute-start = (bf16[4,2,96,256]{3,2,1,0:T(8,128)(2,1)}, bf16[4,2,96,256]{3,2,1,0:T(8,128)(2,1)S(1)}, u32[]{:S(2)}, u32[]{:S(2)}) collective-permute-start(bf16[4,2,96,256]{3,2,1,0:T(8,128)(2,1)} %get-tuple-element.54), channel_id=1, source_target_pairs={{0,32},{32,0},{1,33},{33,1},{2,34},{34,2},{3,35},{35,3},{4,36},{36... | collective-permute-start | bytes 1179656 | tf_op jit(solution)/shard_map/ppermute | solution.py:377
  7.2 1.0 copy-start.5
  9.4 11.5 %collective-permute-start.1 = (bf16[2,96,256]{2,1,0:T(8,128)(2,1)S(1)}, bf16[2,96,256]{2,1,0:T(8,128)(2,1)S(1)}, u32[]{:S(2)}, u32[]{:S(2)}) collective-permute-start(bf16[2,96,256]{2,1,0:T(8,128)(2,1)S(1)} %get-tuple-element.56), channel_id=1, source_target_pairs={{0,128},{64,192},{128,0},{192,64},{1,129},{65,193},{129,1},{193,65... | collective-permute-start | bytes 294920 | tf_op jit(solution)/shard_map/ppermute | solution.py:378
  15.8 9.3 %collective-permute-start.2 = (bf16[2,96,256]{2,1,0:T(8,128)(2,1)S(1)}, bf16[2,96,256]{2,1,0:T(8,128)(2,1)S(1)}, u32[]{:S(2)}, u32[]{:S(2)}) collective-permute-start(bf16[2,96,256]{2,1,0:T(8,128)(2,1)S(1)} %get-tuple-element.57), channel_id=1, source_target_pairs={{0,64},{64,128},{128,192},{192,0},{1,65},{65,129},{129,193},{193,1... | collective-permute-start | bytes 294920 | tf_op jit(solution)/shard_map/ppermute | solution.py:378
  17.2 7.9 %collective-permute-start.3 = (bf16[2,96,256]{2,1,0:T(8,128)(2,1)S(1)}, bf16[2,96,256]{2,1,0:T(8,128)(2,1)S(1)}, u32[]{:S(2)}, u32[]{:S(2)}) collective-permute-start(bf16[2,96,256]{2,1,0:T(8,128)(2,1)S(1)} %get-tuple-element.58), channel_id=1, source_target_pairs={{0,192},{64,0},{128,64},{192,128},{1,193},{65,1},{129,65},{193,129... | collective-permute-start | bytes 294920 | tf_op jit(solution)/shard_map/ppermute | solution.py:378
  20.0 5.1 %copy-start.6 = (f32[2,64,256]{2,1,0:T(8,128)S(1)}, f32[2,64,256]{2,1,0:T(8,128)}, u32[]{:S(2)}) copy-start(f32[2,64,256]{2,1,0:T(8,128)} %get-tuple-element.59.b_in) | copy-start | bytes 393220
  20.0 5.1 %copy-start.7 = (f32[2,64,256]{2,1,0:T(8,128)S(1)}, f32[2,64,256]{2,1,0:T(8,128)}, u32[]{:S(2)}) copy-start(f32[2,64,256]{2,1,0:T(8,128)} %get-tuple-element.60.m_in) | copy-start | bytes 393220
  20.0 5.1 %copy-start.8 = (f32[2,32,256]{2,1,0:T(8,128)S(1)}, f32[2,32,256]{2,1,0:T(8,128)}, u32[]{:S(2)}) copy-start(f32[2,32,256]{2,1,0:T(8,128)} %get-tuple-element.61.b_out) | copy-start | bytes 196612
  20.0 5.1 %copy-start.9 = (f32[2,32,256]{2,1,0:T(8,128)S(1)}, f32[2,32,256]{2,1,0:T(8,128)}, u32[]{:S(2)}) copy-start(f32[2,32,256]{2,1,0:T(8,128)} %get-tuple-element.62.m_out) | copy-start | bytes 196612
  20.0 5.1 %copy-start.11 = (s32[4]{0:T(128)S(1)}, s32[4]{0:T(128)}, u32[]{:S(2)}) copy-start(s32[4]{0:T(128)} %pad_add_fusion.place) | copy-start | bytes 52
  20.0 5.1 %copy-start.12 = (s32[2,64]{1,0:T(2,128)S(1)}, s32[2,64]{1,0:T(2,128)}, u32[]{:S(2)}) copy-start(s32[2,64]{1,0:T(2,128)} %e_in.3) | copy-start | bytes 1540
  20.0 5.1 %copy-start.13 = (s32[2,32]{1,0:T(2,128)S(1)}, s32[2,32]{1,0:T(2,128)}, u32[]{:S(2)}) copy-start(s32[2,32]{1,0:T(2,128)} %e_out.3) | copy-start | bytes 772
  20.9 8.3 %copy-start.1 = (bf16[320,2048]{1,0:T(8,128)(2,1)}, bf16[320,2048]{1,0:T(8,128)(2,1)S(1)}, u32[]{:S(2)}) copy-start(bf16[320,2048]{1,0:T(8,128)(2,1)S(1)} %convolution_convert_fusion.1.refs_1_) | copy-start | bytes 3932164
  26.7 4.2 %collective-permute-start.5 = (bf16[320,2048]{1,0:T(8,128)(2,1)S(1)}, bf16[320,2048]{1,0:T(8,128)(2,1)S(1)}, u32[]{:S(2)}, u32[]{:S(2)}) collective-permute-start(bf16[320,2048]{1,0:T(8,128)(2,1)S(1)} %convolution_convert_fusion.1.refs_1_), channel_id=1, source_target_pairs={{0,32},{32,0},{1,33},{33,1},{2,34},{34,2},{3,35},{35,3},{4,36},{36... | collective-permute-start | bytes 3932168 | tf_op jit(solution)/shard_map/ppermute | solution.py:396
  26.7 4.2 %collective-permute-start.4 = (bf16[96,256]{1,0:T(8,128)(2,1)S(1)}, bf16[96,256]{1,0:T(8,128)(2,1)S(1)}, u32[]{:S(2)}, u32[]{:S(2)}) collective-permute-start(bf16[96,256]{1,0:T(8,128)(2,1)S(1)} %get-tuple-element.70), channel_id=1, source_target_pairs={{0,16},{16,0},{1,17},{17,1},{2,18},{18,2},{3,19},{19,3},{4,20},{20... | collective-permute-start | bytes 147464 | tf_op jit(solution)/shard_map/ppermute | solution.py:398
  30.8 38.8 %copy-start.3 = (bf16[320,2048]{1,0:T(8,128)(2,1)}, bf16[320,2048]{1,0:T(8,128)(2,1)S(1)}, u32[]{:S(2)}) copy-start(bf16[320,2048]{1,0:T(8,128)(2,1)S(1)} %collective-permute-done.5.refs_0_) | copy-start | bytes 3932164
  30.8 9.1 %collective-permute-start.6 = (bf16[2,96,256]{2,1,0:T(8,128)(2,1)S(1)}, bf16[2,96,256]{2,1,0:T(8,128)(2,1)S(1)}, u32[]{:S(2)}, u32[]{:S(2)}) collective-permute-start(bf16[2,96,256]{2,1,0:T(8,128)(2,1)S(1)} %pad_maximum_fusion.4), channel_id=1, source_target_pairs={{0,64},{64,128},{128,192},{192,0},{1,65},{65,129},{129,193},{193,1... | collective-permute-start | bytes 294920 | tf_op jit(solution)/shard_map/ppermute | solution.py:403
  33.2 11.2 %collective-permute-start.7 = (bf16[2,96,256]{2,1,0:T(8,128)(2,1)S(1)}, bf16[2,96,256]{2,1,0:T(8,128)(2,1)S(1)}, u32[]{:S(2)}, u32[]{:S(2)}) collective-permute-start(bf16[2,96,256]{2,1,0:T(8,128)(2,1)S(1)} %pad_maximum_fusion.4), channel_id=1, source_target_pairs={{0,128},{64,192},{128,0},{192,64},{1,129},{65,193},{129,1},{193,65... | collective-permute-start | bytes 294920 | tf_op jit(solution)/shard_map/ppermute | solution.py:403
  37.2 7.5 %collective-permute-start.8 = (bf16[2,96,256]{2,1,0:T(8,128)(2,1)S(1)}, bf16[2,96,256]{2,1,0:T(8,128)(2,1)S(1)}, u32[]{:S(2)}, u32[]{:S(2)}) collective-permute-start(bf16[2,96,256]{2,1,0:T(8,128)(2,1)S(1)} %pad_maximum_fusion.4), channel_id=1, source_target_pairs={{0,192},{64,0},{128,64},{192,128},{1,193},{65,1},{129,65},{193,129... | collective-permute-start | bytes 294920 | tf_op jit(solution)/shard_map/ppermute | solution.py:403
  44.7 24.9 %collective-permute-start.9 = (bf16[320,2048]{1,0:T(8,128)(2,1)S(1)}, bf16[320,2048]{1,0:T(8,128)(2,1)}, u32[]{:S(2)}, u32[]{:S(2)}) collective-permute-start(bf16[320,2048]{1,0:T(8,128)(2,1)S(1)} %convolution_convert_fusion), channel_id=1, source_target_pairs={{0,16},{16,64},{32,240},{48,32},{64,80},{80,128},{96,48},{112,96},... | collective-permute-start | bytes 3932168 | tf_op jit(solution)/shard_map/ppermute | solution.py:407
  48.7 5.8 %collective-permute-start.16 = (bf16[1,2,2,96,256]{4,3,2,1,0:T(8,128)(2,1)S(1)}, bf16[1,2,2,96,256]{4,3,2,1,0:T(8,128)(2,1)S(1)}, u32[]{:S(2)}, u32[]{:S(2)}) collective-permute-start(bf16[1,2,2,96,256]{4,3,2,1,0:T(8,128)(2,1)S(1)} %maximum_bitcast_fusion.1), channel_id=1, source_target_pairs={{0,4},{4,0},{8,12},{12,8},{32,44},{36,40},{40,36},{44,32},{1,5},{5... | collective-permute-start | bytes 589832 | tf_op jit(solution)/shard_map/ppermute | solution.py:412
  50.4 7.2 %collective-permute-start.11 = (bf16[1,2,2,96,256]{4,3,2,1,0:T(8,128)(2,1)S(1)}, bf16[1,2,2,96,256]{4,3,2,1,0:T(8,128)(2,1)S(1)}, u32[]{:S(2)}, u32[]{:S(2)}) collective-permute-start(bf16[1,2,2,96,256]{4,3,2,1,0:T(8,128)(2,1)S(1)} %maximum_bitcast_fusion), channel_id=1, source_target_pairs={{0,1},{1,0},{2,3},{3,2},{32,35},{33,34},{34,33},{35,32},{4,5},{5,4... | collective-permute-start | bytes 589832 | tf_op jit(solution)/shard_map/ppermute | solution.py:412
  54.5 9.1 %collective-permute-start.17 = (bf16[2,2,2,96,256]{4,3,2,1,0:T(8,128)(2,1)S(1)}, bf16[2,2,2,96,256]{4,3,2,1,0:T(8,128)(2,1)S(1)}, u32[]{:S(2)}, u32[]{:S(2)}) collective-permute-start(bf16[2,2,2,96,256]{4,3,2,1,0:T(8,128)(2,1)S(1)} %pad_maximum_fusion.3), channel_id=1, source_target_pairs={{0,12},{4,8},{8,4},{12,0},{32,36},{36,32},{40,44},{44,40},{1,13},{... | collective-permute-start | bytes 1179656 | tf_op jit(solution)/shard_map/ppermute | solution.py:412
  57.6 11.0 %collective-permute-start.12 = (bf16[2,2,2,96,256]{4,3,2,1,0:T(8,128)(2,1)S(1)}, bf16[2,2,2,96,256]{4,3,2,1,0:T(8,128)(2,1)S(1)}, u32[]{:S(2)}, u32[]{:S(2)}) collective-permute-start(bf16[2,2,2,96,256]{4,3,2,1,0:T(8,128)(2,1)S(1)} %pad_maximum_fusion.2), channel_id=1, source_target_pairs={{0,3},{1,2},{2,1},{3,0},{32,33},{33,32},{34,35},{35,34},{4,7},{5,6... | collective-permute-start | bytes 1179656 | tf_op jit(solution)/shard_map/ppermute | solution.py:412
  63.6 15.5 %collective-permute-start.18 = (bf16[4,2,2,96,256]{4,3,2,1,0:T(8,128)(2,1)S(1)}, bf16[4,2,2,96,256]{4,3,2,1,0:T(8,128)(2,1)}, u32[]{:S(2)}, u32[]{:S(2)}) collective-permute-start(bf16[4,2,2,96,256]{4,3,2,1,0:T(8,128)(2,1)S(1)} %pad_maximum_fusion.1.refs_6_.refs_4_), channel_id=1, source_target_pairs={{0,1},{1,0},{2,3},{3,2},{32,35},{33,34},{34,33},{35,32},{4,5},{5,4... | collective-permute-start | bytes 2359304 | tf_op jit(solution)/shard_map/ppermute | solution.py:412
  69.6 20.7 %collective-permute-start.13 = (bf16[4,2,2,96,256]{4,3,2,1,0:T(8,128)(2,1)}, bf16[4,2,2,96,256]{4,3,2,1,0:T(8,128)(2,1)}, u32[]{:S(2)}, u32[]{:S(2)}) collective-permute-start(bf16[4,2,2,96,256]{4,3,2,1,0:T(8,128)(2,1)} %pad_maximum_fusion.refs_2_.refs_0_), channel_id=1, source_target_pairs={{0,4},{4,0},{8,12},{12,8},{32,44},{36,40},{40,36},{44,32},{1,5},{5... | collective-permute-start | bytes 2359304 | tf_op jit(solution)/shard_map/ppermute | solution.py:412
  69.6 34.2 %collective-permute-start.10 = (bf16[320,2048]{1,0:T(8,128)(2,1)}, bf16[320,2048]{1,0:T(8,128)(2,1)}, u32[]{:S(2)}, u32[]{:S(2)}) collective-permute-start(bf16[320,2048]{1,0:T(8,128)(2,1)} %collective-permute-done.9.refs_1_), channel_id=1, source_target_pairs={{0,32},{32,0},{1,33},{33,1},{2,34},{34,2},{3,35},{35,3},{4,36},{36... | collective-permute-start | bytes 3932168 | tf_op jit(solution)/shard_map/ppermute | solution.py:421
  69.7 21.4 %collective-permute-start.19 = (bf16[4,2,2,96,256]{4,3,2,1,0:T(8,128)(2,1)S(1)}, bf16[4,2,2,96,256]{4,3,2,1,0:T(8,128)(2,1)}, u32[]{:S(2)}, u32[]{:S(2)}) collective-permute-start(bf16[4,2,2,96,256]{4,3,2,1,0:T(8,128)(2,1)S(1)} %pad_maximum_fusion.1.refs_6_.refs_4_), channel_id=1, source_target_pairs={{0,3},{1,2},{2,1},{3,0},{32,33},{33,32},{34,35},{35,34},{4,7},{5,6... | collective-permute-start | bytes 2359304 | tf_op jit(solution)/shard_map/ppermute | solution.py:412
  72.6 18.6 %collective-permute-start.14 = (bf16[4,2,2,96,256]{4,3,2,1,0:T(8,128)(2,1)}, bf16[4,2,2,96,256]{4,3,2,1,0:T(8,128)(2,1)}, u32[]{:S(2)}, u32[]{:S(2)}) collective-permute-start(bf16[4,2,2,96,256]{4,3,2,1,0:T(8,128)(2,1)} %pad_maximum_fusion.refs_2_.refs_0_), channel_id=1, source_target_pairs={{0,12},{4,8},{8,4},{12,0},{32,36},{36,32},{40,44},{44,40},{1,13},{... | collective-permute-start | bytes 2359304 | tf_op jit(solution)/shard_map/ppermute | solution.py:412
  79.1 13.5 %collective-permute-start.20 = (bf16[4,2,2,96,256]{4,3,2,1,0:T(8,128)(2,1)}, bf16[4,2,2,96,256]{4,3,2,1,0:T(8,128)(2,1)}, u32[]{:S(2)}, u32[]{:S(2)}) collective-permute-start(bf16[4,2,2,96,256]{4,3,2,1,0:T(8,128)(2,1)} %collective-permute-done.18.refs_7_.refs_5_), channel_id=1, source_target_pairs={{0,3},{1,2},{2,1},{3,0},{32,33},{33,32},{34,35},{35,34},{4,7},{5,6... | collective-permute-start | bytes 2359304 | tf_op jit(solution)/shard_map/ppermute | solution.py:412
  90.3 13.5 %collective-permute-start.15 = (bf16[4,2,2,96,256]{4,3,2,1,0:T(8,128)(2,1)}, bf16[4,2,2,96,256]{4,3,2,1,0:T(8,128)(2,1)}, u32[]{:S(2)}, u32[]{:S(2)}) collective-permute-start(bf16[4,2,2,96,256]{4,3,2,1,0:T(8,128)(2,1)} %collective-permute-done.13.refs_3_.refs_1_), channel_id=1, source_target_pairs={{0,12},{4,8},{8,4},{12,0},{32,36},{36,32},{40,44},{44,40},{1,13},{... | collective-permute-start | bytes 2359304 | tf_op jit(solution)/shard_map/ppermute | solution.py:412
  91.1 19.5 %copy-start.2 = (bf16[320,2048]{1,0:T(8,128)(2,1)S(1)}, bf16[320,2048]{1,0:T(8,128)(2,1)}, u32[]{:S(2)}) copy-start(bf16[320,2048]{1,0:T(8,128)(2,1)} %copy-done.1) | copy-start | bytes 3932164
  91.1 19.5 %copy-start.4 = (bf16[320,2048]{1,0:T(8,128)(2,1)S(1)}, bf16[320,2048]{1,0:T(8,128)(2,1)}, u32[]{:S(2)}) copy-start(bf16[320,2048]{1,0:T(8,128)(2,1)} %copy-done.3) | copy-start | bytes 3932164
  110.0 7.0 %collective-permute-start.21 = (bf16[320,512]{1,0:T(8,128)(2,1)S(1)}, bf16[320,512]{1,0:T(8,128)(2,1)S(1)}, u32[]{:S(2)}, u32[]{:S(2)}) collective-permute-start(bf16[320,512]{1,0:T(8,128)(2,1)S(1)} %get-tuple-element.81), channel_id=1, source_target_pairs={{0,32},{32,0},{1,33},{33,1},{2,34},{34,2},{3,35},{35,3},{4,36},{36... | collective-permute-start | bytes 983048 | tf_op jit(solution)/shard_map/ppermute | solution.py:424
  110.1 6.9 %collective-permute-start.22 = (bf16[320,512]{1,0:T(8,128)(2,1)S(1)}, bf16[320,512]{1,0:T(8,128)(2,1)S(1)}, u32[]{:S(2)}, u32[]{:S(2)}) collective-permute-start(bf16[320,512]{1,0:T(8,128)(2,1)S(1)} %get-tuple-element.82), channel_id=1, source_target_pairs={{0,32},{32,0},{1,33},{33,1},{2,34},{34,2},{3,35},{35,3},{4,36},{36... | collective-permute-start | bytes 983048 | tf_op jit(solution)/shard_map/ppermute | solution.py:424
  116.4 4.5 %collective-permute-start.23 = (bf16[320,512]{1,0:T(8,128)(2,1)S(1)}, bf16[320,512]{1,0:T(8,128)(2,1)S(1)}, u32[]{:S(2)}, u32[]{:S(2)}) collective-permute-start(bf16[320,512]{1,0:T(8,128)(2,1)S(1)} %get-tuple-element.89), channel_id=1, source_target_pairs={{0,32},{32,0},{1,33},{33,1},{2,34},{34,2},{3,35},{35,3},{4,36},{36... | collective-permute-start | bytes 983048 | tf_op jit(solution)/shard_map/ppermute | solution.py:424
  116.6 4.3 %collective-permute-start.24 = (bf16[320,512]{1,0:T(8,128)(2,1)S(1)}, bf16[320,512]{1,0:T(8,128)(2,1)S(1)}, u32[]{:S(2)}, u32[]{:S(2)}) collective-permute-start(bf16[320,512]{1,0:T(8,128)(2,1)S(1)} %get-tuple-element.90), channel_id=1, source_target_pairs={{0,32},{32,0},{1,33},{33,1},{2,34},{34,2},{3,35},{35,3},{4,36},{36... | collective-permute-start | bytes 983048 | tf_op jit(solution)/shard_map/ppermute | solution.py:424
  120.9 17.7 %collective-permute-start.25 = (bf16[320,1024]{1,0:T(8,128)(2,1)S(1)}, bf16[320,1024]{1,0:T(8,128)(2,1)S(1)}, u32[]{:S(2)}, u32[]{:S(2)}) collective-permute-start(bf16[320,1024]{1,0:T(8,128)(2,1)S(1)} %get-tuple-element.91), channel_id=1, source_target_pairs={{0,208},{16,0},{32,48},{48,96},{64,16},{80,64},{96,112},{112,160},... | collective-permute-start | bytes 1966088 | tf_op jit(solution)/shard_map/ppermute | solution.py:435
  121.2 17.6 %collective-permute-start.30 = (bf16[320,1024]{1,0:T(8,128)(2,1)S(1)}, bf16[320,1024]{1,0:T(8,128)(2,1)S(1)}, u32[]{:S(2)}, u32[]{:S(2)}) collective-permute-start(bf16[320,1024]{1,0:T(8,128)(2,1)S(1)} %get-tuple-element.100), channel_id=1, source_target_pairs={{32,208},{48,0},{0,48},{16,96},{96,16},{112,64},{64,112},{80,160},... | collective-permute-start | bytes 1966088 | tf_op jit(solution)/shard_map/ppermute | solution.py:436
  123.7 6.8 %copy-start.10 = (f32[512]{0:T(512)S(1)}, f32[512]{0:T(512)}, u32[]{:S(2)}) copy-start(f32[512]{0:T(512)} %param.22) | copy-start | bytes 6148
  127.6 1.5 %collective-permute-start.26 = (bf16[80,1024]{1,0:T(8,128)(2,1)S(1)}, bf16[80,1024]{1,0:T(8,128)(2,1)S(1)}, u32[]{:S(2)}, u32[]{:S(2)}) collective-permute-start(bf16[80,1024]{1,0:T(8,128)(2,1)S(1)} %get-tuple-element.96), channel_id=1, source_target_pairs={{0,32},{32,0},{1,33},{33,1},{2,34},{34,2},{3,35},{35,3},{4,36},{36... | collective-permute-start | bytes 491528 | tf_op jit(solution)/shard_map/ppermute | solution.py:424
  127.8 1.6 %collective-permute-start.27 = (bf16[80,1024]{1,0:T(8,128)(2,1)S(1)}, bf16[80,1024]{1,0:T(8,128)(2,1)S(1)}, u32[]{:S(2)}, u32[]{:S(2)}) collective-permute-start(bf16[80,1024]{1,0:T(8,128)(2,1)S(1)} %get-tuple-element.97), channel_id=1, source_target_pairs={{0,32},{32,0},{1,33},{33,1},{2,34},{34,2},{3,35},{35,3},{4,36},{36... | collective-permute-start | bytes 491528 | tf_op jit(solution)/shard_map/ppermute | solution.py:424
  128.4 1.4 collective-permute-start.28
  129.1 1.4 collective-permute-start.29
